TPU v7x, 512 devices: a whole 4x4x16 slice. The times are simulated.
512 devices in a mesh: row: 16 (over z), col: 8 (over y, core), rep: 4 (over x).
Axes of the slice: x: 4, y: 4, z: 16, core: 2. Of those that a mesh axis runs over, the one named last changes fastest.
Arguments:
- p_vals: bfloat16 [384, 16, 128, 128], P('row', 'col'), may hold values from -0.8984375 to 0.8984375
- p_cols: int32 [384, 16], P('row', 'col'), may hold values from 0 to 23
- square_cols: int32 [128, 16, 2], P('row', 'col'), may hold values from 0 to 23, as said below
- cube_cols: int32 [128, 16, 1], P('row', 'col'), may hold values from 0 to 23
Outputs:
- new_density: bfloat16 [128, 16, 1, 128, 128], P(('row', 'rep'), 'col')
Inputs may be any that keep to these rules, and one draw needn't show every extreme that they name: `square_cols`: the 2 columns of one block row and group are distinct.
All inputs are finite; a program needn't handle non-finite values.
Results may differ from a plain program's by a relative error of at most 0.014.
Values may be sent and summed in bfloat16 or wider, within the bound.
No kernel may reach another device: no remote copies, remote signals or barrier semaphores. Data moves between devices by JAX's collectives and lax.ppermute only.
A program may use at most 64 MiB of HBM per device.

v0:
```python
import jax
import jax.numpy as jnp
from jax import lax
from jax.sharding import PartitionSpec as P


def passed_along(value, axis, steps):
    count = lax.axis_size(axis)
    pairs = [(source, (source + steps) % count) for source in range(count)]
    return lax.ppermute(value, axis, pairs)


def as_sent(value):

    def short(part):
        return part.astype(jnp.bfloat16) if part.dtype == jnp.float32 else part

    return jax.tree.map(short, value)


def from_root(value, axis, root):
    mine = lax.axis_index(axis) == root
    return lax.psum(jnp.where(mine, value, jnp.zeros_like(value)), axis)


def pick_tuple(flag, moved, staying):
    return (jnp.where(flag, moved[0], staying[0]), jnp.where(flag, moved[1], staying[1]))


def first_panels(p_vals, p_cols, lift, rounds, n_rep):
    start = (p_vals, p_cols)
    one = passed_along((start[0], start[1]), "row", -1)
    start = pick_tuple(lift % 2 == 1, one, start)
    two = passed_along((start[0], as_sent(start[1])), "row", -2)
    start = pick_tuple(lift // 2 == 1, two, start)
    panels = [start]
    for q in range(1, rounds):
        prev = panels[-1]
        panels.append(passed_along((prev[0], as_sent(prev[1])), "row", -n_rep))
    return panels


def on_device(p_vals, p_cols, square_cols, cube_cols):
    n_rep = lax.axis_size("rep")
    n_row = lax.axis_size("row")
    n_col = lax.axis_size("col")
    replica = lax.axis_index("rep")
    row_index = lax.axis_index("row")
    groups = n_row // n_col
    rounds = n_row // n_rep
    window = square_cols.shape[0]
    quarter_rows = window // n_rep
    k_two = square_cols.shape[2]
    k_three = cube_cols.shape[2]
    block = p_vals.shape[2]
    lift = (replica - row_index) % n_rep
    base_step = row_index + lift
    kept_panels = first_panels(p_vals, p_cols, lift, rounds, n_rep)
    square_part = jnp.zeros((window, groups, k_two, block, block), jnp.float32)
    for q in range(rounds):
        step = (base_step + q * n_rep) % n_row
        owner = step // groups
        inside = step % groups
        own_vals = lax.dynamic_index_in_dim(p_vals[:window], inside, 1, keepdims=False)
        own_cols = lax.dynamic_index_in_dim(p_cols[:window], inside, 1, keepdims=False)
        left_vals, left_cols = (
            from_root(own_vals, "col", owner),
            from_root(own_cols, "col", owner),
        )
        panel_vals, panel_cols = kept_panels[q]
        picked = panel_vals[left_cols]
        picked_cols = panel_cols[left_cols]
        product = jnp.einsum(
            "iab,igbc->igac", left_vals, picked, preferred_element_type=jnp.float32
        )
        match = (square_cols == picked_cols[:, :, None]).astype(jnp.float32)
        square_part = square_part + match[:, :, :, None, None] * product[:, :, None]
    square_own = lax.psum_scatter(
        square_part.astype(jnp.bfloat16), "rep", scatter_dimension=0, tiled=True
    )
    square_all = lax.all_gather(square_own, "rep", axis=0, tiled=True)
    cube_part = jnp.zeros((window, groups, k_three, block, block), jnp.float32)
    for q in range(rounds):
        step = (base_step + q * n_rep) % n_row
        owner = step // groups
        inside = step % groups
        own_vals = lax.dynamic_index_in_dim(square_all, inside, 1, keepdims=False)
        own_cols = lax.dynamic_index_in_dim(square_cols, inside, 1, keepdims=False)
        left_vals, left_cols = (
            from_root(own_vals, "col", owner),
            from_root(own_cols, "col", owner),
        )
        panel_vals, panel_cols = kept_panels[q]
        picked = panel_vals[left_cols]
        picked_cols = panel_cols[left_cols]
        product = jnp.einsum(
            "itab,itgbc->itgac", left_vals, picked, preferred_element_type=jnp.float32
        )
        match = (picked_cols[:, :, :, None] == cube_cols[:, None]).astype(jnp.float32)
        cube_part = cube_part + jnp.einsum("itgm,itgac->igmac", match, product)
    cube = lax.psum_scatter(
        cube_part.astype(jnp.bfloat16), "rep", scatter_dimension=0, tiled=True
    ).astype(jnp.float32)
    own_square_cols = lax.dynamic_slice_in_dim(square_cols, replica * quarter_rows, quarter_rows, 0)
    own_cube_cols = lax.dynamic_slice_in_dim(cube_cols, replica * quarter_rows, quarter_rows, 0)
    found = (own_square_cols[:, :, :, None] == own_cube_cols[:, :, None, :]).astype(jnp.float32)
    at_cube = jnp.einsum("igtm,igtac->igmac", found, square_own.astype(jnp.float32))
    return (3.0 * at_cube - 2.0 * cube).astype(jnp.bfloat16)


def solution(mesh):
    in_specs = (
        P("row", "col", None, None),
        P("row", "col"),
        P("row", "col", None),
        P("row", "col", None),
    )
    out_specs = P(("row", "rep"), "col", None, None, None)
    return jax.shard_map(
        on_device, mesh=mesh, in_specs=in_specs, out_specs=out_specs, check_vma=False
    )
```

profile of v0, /device:TPU:1, one launch (start us, length us, event | category | flops | bytes accessed | tf_op | source)
XLA Modules:
  0.0 809.1 jit_solution(12156330980871107587)
XLA Ops:
  6.5 11.9 %collective-permute-start.2 = (bf16[24,2,128,128]{3,2,1,0:T(8,128)(2,1)}, bf16[24,2,128,128]{3,2,1,0:T(8,128)(2,1)S(1)}, u32[]{:S(2)}, u32[]{:S(2)}) collective-permute-start(bf16[24,2,128,128]{3,2,1,0:T(8,128)(2,1)} %param.4), channel_id=1, source_target_pairs={{0,480},{32,0},{64,32},{96,64},{128,96},{160,128},{192,160},{224,1... | collective-permute-start | bytes 4718600 | tf_op jit(solution)/shard_map/ppermute | solution.py:10
  18.5 33.3 %collective-permute-done.2 = bf16[24,2,128,128]{3,2,1,0:T(8,128)(2,1)S(1)} collective-permute-done((bf16[24,2,128,128]{3,2,1,0:T(8,128)(2,1)}, bf16[24,2,128,128]{3,2,1,0:T(8,128)(2,1)S(1)}, u32[]{:S(2)}, u32[]{:S(2)}) %collective-permute-start.2) | collective-permute-done | bytes 1572896 | tf_op jit(solution)/shard_map/ppermute | solution.py:10
  51.8 1.6 broadcast_select_fusion
  53.4 4.4 collective-permute-start.3
  57.9 63.1 %collective-permute-done.3 = bf16[24,2,128,128]{3,2,1,0:T(8,128)(2,1)} collective-permute-done((bf16[24,2,128,128]{3,2,1,0:T(8,128)(2,1)S(1)}, bf16[24,2,128,128]{3,2,1,0:T(8,128)(2,1)}, u32[]{:S(2)}, u32[]{:S(2)}) %collective-permute-start.3) | collective-permute-done | bytes 1572896 | tf_op jit(solution)/shard_map/ppermute | solution.py:10
  121.1 7.9 collective-permute-start.5
  129.0 68.2 %collective-permute-done.5 = bf16[24,2,128,128]{3,2,1,0:T(8,128)(2,1)} collective-permute-done((bf16[24,2,128,128]{3,2,1,0:T(8,128)(2,1)S(1)}, bf16[24,2,128,128]{3,2,1,0:T(8,128)(2,1)}, u32[]{:S(2)}, u32[]{:S(2)}) %collective-permute-start.5) | collective-permute-done | bytes 1572896 | tf_op jit(solution)/shard_map/ppermute | solution.py:10
  197.2 75.2 %collective-permute-start.7 = (bf16[24,2,128,128]{3,2,1,0:T(8,128)(2,1)}, bf16[24,2,128,128]{3,2,1,0:T(8,128)(2,1)}, u32[]{:S(2)}, u32[]{:S(2)}) collective-permute-start(bf16[24,2,128,128]{3,2,1,0:T(8,128)(2,1)} %collective-permute-done.5), channel_id=1, source_target_pairs={{0,384},{32,416},{64,448},{96,480},{128,0},{160,32},{192,64},{224,... | collective-permute-start | bytes 4718600 | tf_op jit(solution)/shard_map/ppermute | solution.py:10
  272.6 1.9 collective-permute-start
  277.1 9.3 %all-reduce = (s32[8,2]{0,1:T(2,128)S(1)}, s32[8]{0:T(128)S(1)}, s32[8]{0:T(128)S(1)}, s32[8]{0:T(128)S(1)}, s32[8]{0:T(128)S(1)}, /*index=5*/s32[8,2]{0,1:T(2,128)S(1)}, s32[8,2]{0,1:T(2,128)S(1)}, s32[8,2]{0,1:T(2,128)S(1)}) all-reduce(s32[8,2]{0,1:T(2,128)S(1)} %get-tuple-element.35, ...), channel_id=1, replica_groups=mesh['row'=16,'col'=8,'rep'=4] {'col'}, use_global_device_ids=true, to_apply=%region_15.16 | all-reduce | flops 96 | bytes 768 | tf_op jit(solution)/shard_map/psum | solution.py:23
  286.5 219.6 %collective-permute-done.7 = bf16[24,2,128,128]{3,2,1,0:T(8,128)(2,1)} collective-permute-done((bf16[24,2,128,128]{3,2,1,0:T(8,128)(2,1)}, bf16[24,2,128,128]{3,2,1,0:T(8,128)(2,1)}, u32[]{:S(2)}, u32[]{:S(2)}) %collective-permute-start.7) | collective-permute-done | bytes 1572896 | tf_op jit(solution)/shard_map/ppermute | solution.py:10
  506.1 8.0 collective-permute-start.9
  514.1 1.9 collective-permute-start.1
  516.0 32.3 %collective-permute-done.1 = s32[24,2]{1,0:T(8,128)S(1)} collective-permute-done((s32[24,2]{1,0:T(8,128)S(1)}, s32[24,2]{1,0:T(8,128)S(1)}, u32[]{:S(2)}, u32[]{:S(2)}) %collective-permute-start.1) | collective-permute-done | bytes 224 | tf_op jit(solution)/shard_map/ppermute | solution.py:10
  548.3 2.1 collective-permute-start.4
  550.4 6.3 collective-permute-done.4
  556.7 2.0 collective-permute-start.6
  559.9 5.1 collective-permute-done.6
  565.0 2.0 collective-permute-start.8
  567.8 5.6 collective-permute-done.8
  575.1 2.3 convolution_bitcast_fusion.7
  577.4 1.6 copy.71
  579.0 2.1 gather_fusion.3
  581.1 1.4 convolution_bitcast_fusion.6
  582.4 2.6 copy.75
  585.0 2.1 gather_fusion.5
  587.1 1.4 convolution_bitcast_fusion.5
  588.5 2.6 copy.79
  591.1 2.1 gather_fusion.7
  593.1 1.4 convolution_bitcast_fusion.4
  594.5 2.6 copy.83
  597.1 3.7 add_convert_fusion
  600.9 26.5 %reduce-scatter.3.cloned.1.call-done = bf16[2,2,2,128,128]{4,3,2,1,0:T(8,128)(2,1)} async-done(((bf16[8,2,2,128,128]{4,3,2,1,0:T(8,128)(2,1)}), bf16[2,2,2,128,128]{4,3,2,1,0:T(8,128)(2,1)}) %reduce-scatter.3.cloned.1.call-update) | async-done | bytes 262160 | tf_op jit(solution)/shard_map/reduce_scatter | solution.py:78
  627.4 34.6 %all-gather.2.cloned.1.call-done = bf16[8,2,2,128,128]{4,3,2,1,0:T(8,128)(2,1)} async-done(((bf16[2,2,2,128,128]{4,3,2,1,0:T(8,128)(2,1)}), bf16[8,2,2,128,128]{4,3,2,1,0:T(8,128)(2,1)}) %all-gather.2.cloned.1.call-update) | async-done | bytes 1048592 | tf_op jit(solution)/shard_map/all_gather | solution.py:81
  662.0 3.2 fusion.3
  669.7 3.1 gather_fusion.11
  672.8 2.2 gather_fusion.13
  675.0 3.1 gather_fusion.15
  678.0 68.2 %all-reduce.6.cloned.1.call-done = (bf16[8,2,128,128]{3,2,1,0:T(8,128)(2,1)}, bf16[8,2,128,128]{3,2,1,0:T(8,128)(2,1)}, bf16[8,2,128,128]{3,2,1,0:T(8,128)(2,1)}, bf16[8,2,128,128]{3,2,1,0:T(8,128)(2,1)}) async-done(((bf16[8,2,128,128]{3,2,1,0:T(8,128)(2,1)}, bf16[8,2,128,128]{3,2,1,0:T(8,128)(2,1)}, bf16[8,2,128,128]{3,2,1,0:T(8,128)(2,1)}, bf16[8,2,128,128]{3,2,1,0:T(8,128)(2,1)}), ...) | async-done | bytes 2097168 | tf_op jit(solution)/shard_map/psum | solution.py:23
  746.3 2.8 convolution_bitcast_fusion.2
  749.1 3.7 copy.119
  752.8 1.5 convolution_bitcast_fusion.3
  754.3 3.8 copy.114
  758.1 1.5 convolution_bitcast_fusion
  759.5 3.7 copy.129
  763.7 2.0 copy.124
  772.6 28.3 %reduce-scatter.5.cloned.1.call-done = bf16[2,2,1,128,128]{4,3,2,1,0:T(8,128)(2,1)} async-done(((bf16[8,2,1,128,128]{4,3,2,1,0:T(8,128)(2,1)}), bf16[2,2,1,128,128]{4,3,2,1,0:T(8,128)(2,1)}) %reduce-scatter.5.cloned.1.call-update) | async-done | bytes 131088 | tf_op jit(solution)/shard_map/reduce_scatter | solution.py:101
  800.9 1.6 fusion.17
  (107 shorter events, 18.1 us)
Async XLA Ops:
  6.5 568.5 %all-reduce.8.cloned.1.call-start = ((), (), s32[]{:S(2)}) async-start(), calls=%async_computation.6 | async-start | bytes 2097152 | tf_op jit(solution)/shard_map/psum | solution.py:23
  6.5 45.3 %collective-permute-start.2 = (bf16[24,2,128,128]{3,2,1,0:T(8,128)(2,1)}, bf16[24,2,128,128]{3,2,1,0:T(8,128)(2,1)S(1)}, u32[]{:S(2)}, u32[]{:S(2)}) collective-permute-start(bf16[24,2,128,128]{3,2,1,0:T(8,128)(2,1)} %param.4), channel_id=1, source_target_pairs={{0,480},{32,0},{64,32},{96,64},{128,96},{160,128},{192,160},{224,1... | collective-permute-start | bytes 4718600 | tf_op jit(solution)/shard_map/ppermute | solution.py:10
  53.4 67.6 %collective-permute-start.3 = (bf16[24,2,128,128]{3,2,1,0:T(8,128)(2,1)S(1)}, bf16[24,2,128,128]{3,2,1,0:T(8,128)(2,1)}, u32[]{:S(2)}, u32[]{:S(2)}) collective-permute-start(bf16[24,2,128,128]{3,2,1,0:T(8,128)(2,1)S(1)} %broadcast_select_fusion), channel_id=1, source_target_pairs={{0,448},{32,480},{64,0},{96,32},{128,64},{160,96},{192,128},{224,1... | collective-permute-start | bytes 4718600 | tf_op jit(solution)/shard_map/ppermute | solution.py:10
  57.9 214.6 %copy-start.13 = (s32[24,2]{0,1:T(2,128)S(1)}, s32[24,2]{0,1:T(2,128)}, u32[]{:S(2)}) copy-start(s32[24,2]{0,1:T(2,128)} %param.5) | copy-start | bytes 580
  121.1 76.1 %collective-permute-start.5 = (bf16[24,2,128,128]{3,2,1,0:T(8,128)(2,1)S(1)}, bf16[24,2,128,128]{3,2,1,0:T(8,128)(2,1)}, u32[]{:S(2)}, u32[]{:S(2)}) collective-permute-start(bf16[24,2,128,128]{3,2,1,0:T(8,128)(2,1)S(1)} %broadcast_select_fusion.1), channel_id=1, source_target_pairs={{0,384},{32,416},{64,448},{96,480},{128,0},{160,32},{192,64},{224,... | collective-permute-start | bytes 4718600 | tf_op jit(solution)/shard_map/ppermute | solution.py:10
  197.2 308.8 %collective-permute-start.7 = (bf16[24,2,128,128]{3,2,1,0:T(8,128)(2,1)}, bf16[24,2,128,128]{3,2,1,0:T(8,128)(2,1)}, u32[]{:S(2)}, u32[]{:S(2)}) collective-permute-start(bf16[24,2,128,128]{3,2,1,0:T(8,128)(2,1)} %collective-permute-done.5), channel_id=1, source_target_pairs={{0,384},{32,416},{64,448},{96,480},{128,0},{160,32},{192,64},{224,... | collective-permute-start | bytes 4718600 | tf_op jit(solution)/shard_map/ppermute | solution.py:10
  272.6 241.5 %collective-permute-start = (s32[24,2]{1,0:T(8,128)S(1)}, s32[24,2]{1,0:T(8,128)S(1)}, u32[]{:S(2)}, u32[]{:S(2)}) collective-permute-start(s32[24,2]{1,0:T(8,128)S(1)} %copy.65), channel_id=1, source_target_pairs={{0,480},{32,0},{64,32},{96,64},{128,96},{160,128},{192,160},{224,1... | collective-permute-start | bytes 584 | tf_op jit(solution)/shard_map/ppermute | solution.py:10
  275.8 1.2 copy-start.12
  277.0 350.4 %reduce-scatter.3.cloned.1.call-start = ((), (), s32[]{:S(2)}) async-start(), calls=%async_computation.2 | async-start | bytes 1310720 | tf_op jit(solution)/shard_map/reduce_scatter | solution.py:78
  506.1 85.0 %collective-permute-start.9 = (bf16[24,2,128,128]{3,2,1,0:T(8,128)(2,1)}, bf16[24,2,128,128]{3,2,1,0:T(8,128)(2,1)}, u32[]{:S(2)}, u32[]{:S(2)}) collective-permute-start(bf16[24,2,128,128]{3,2,1,0:T(8,128)(2,1)} %collective-permute-done.7), channel_id=1, source_target_pairs={{0,384},{32,416},{64,448},{96,480},{128,0},{160,32},{192,64},{224,... | collective-permute-start | bytes 4718600 | tf_op jit(solution)/shard_map/ppermute | solution.py:10
  514.1 34.2 %collective-permute-start.1 = (s32[24,2]{1,0:T(8,128)S(1)}, s32[24,2]{1,0:T(8,128)S(1)}, u32[]{:S(2)}, u32[]{:S(2)}) collective-permute-start(s32[24,2]{1,0:T(8,128)S(1)} %broadcast_select_fusion.2), channel_id=1, source_target_pairs={{0,448},{32,480},{64,0},{96,32},{128,64},{160,96},{192,128},{224,1... | collective-permute-start | bytes 584 | tf_op jit(solution)/shard_map/ppermute | solution.py:10
  548.3 8.4 %collective-permute-start.4 = (s32[24,2]{1,0:T(8,128)S(1)}, s32[24,2]{1,0:T(8,128)S(1)}, u32[]{:S(2)}, u32[]{:S(2)}) collective-permute-start(s32[24,2]{1,0:T(8,128)S(1)} %broadcast_select_fusion.3), channel_id=1, source_target_pairs={{0,384},{32,416},{64,448},{96,480},{128,0},{160,32},{192,64},{224,... | collective-permute-start | bytes 584 | tf_op jit(solution)/shard_map/ppermute | solution.py:10
  556.7 8.3 %collective-permute-start.6 = (s32[24,2]{1,0:T(8,128)S(1)}, s32[24,2]{1,0:T(8,128)S(1)}, u32[]{:S(2)}, u32[]{:S(2)}) collective-permute-start(s32[24,2]{1,0:T(8,128)S(1)} %collective-permute-done.4), channel_id=1, source_target_pairs={{0,384},{32,416},{64,448},{96,480},{128,0},{160,32},{192,64},{224,... | collective-permute-start | bytes 584 | tf_op jit(solution)/shard_map/ppermute | solution.py:10
  565.0 8.3 %collective-permute-start.8 = (s32[24,2]{1,0:T(8,128)S(1)}, s32[24,2]{1,0:T(8,128)S(1)}, u32[]{:S(2)}, u32[]{:S(2)}) collective-permute-start(s32[24,2]{1,0:T(8,128)S(1)} %collective-permute-done.6), channel_id=1, source_target_pairs={{0,384},{32,416},{64,448},{96,480},{128,0},{160,32},{192,64},{224,... | collective-permute-start | bytes 584 | tf_op jit(solution)/shard_map/ppermute | solution.py:10
  577.4 3.7 copy-start.10
  582.4 4.7 copy-start.9
  588.4 4.7 copy-start.8
  600.8 61.1 %all-gather.2.cloned.1.call-start = ((), (), s32[]{:S(2)}) async-start(), calls=%async_computation.3 | async-start | bytes 1310720 | tf_op jit(solution)/shard_map/all_gather | solution.py:81
  627.4 118.9 %all-reduce.6.cloned.1.call-start = ((), (), s32[]{:S(2)}) async-start(), calls=%async_computation.5 | async-start | bytes 4194304 | tf_op jit(solution)/shard_map/psum | solution.py:23
  665.1 3.8 copy-start.14
  665.1 135.8 %reduce-scatter.5.cloned.1.call-start = ((), (), s32[]{:S(2)}) async-start(), calls=%async_computation.4 | async-start | bytes 655360 | tf_op jit(solution)/shard_map/reduce_scatter | solution.py:101
  749.1 3.7 copy-start.7
  754.3 3.8 copy-start
  754.3 3.8 copy-start.6
  759.5 3.7 copy-start.5
  763.7 2.0 copy-start.1
  765.8 1.2 copy-start.2
  767.0 1.2 copy-start.3
  768.3 1.2 copy-start.4
  770.7 1.4 copy-start.11
Sparse Core Ops, SparseCore 0:
  277.1 140.2 all-reduce.7
  600.9 26.3 reduce-scatter.2
  629.6 32.2 all-gather.1
  665.3 80.9 all-reduce.5
  772.0 28.8 reduce-scatter.4
where the time goes:
time: 811 us; the launch traced here: 809 us
  waiting for transfers between devices  591 us (73%)
  starting transfers between devices  118 us (15%)
  local copies, waits for them, and re-layouts  46.2 us (6%)
  matrix products  18 us (2%)
  between operations  14 us (2%)
  other arithmetic  12.7 us (2%)
  blocking collectives  9.31 us (1%)
    ppermute x10, waiting for transfers between devices, passed_along(): return lax.ppermute(value, axis, pairs)  433 us
    ppermute x10, starting transfers between devices, passed_along(): return lax.ppermute(value, axis, pairs)  118 us
    psum x2, waiting for transfers between devices, from_root(): return lax.psum(jnp.where(mine, value, jnp.zeros_like(value)), axis)  68.3 us
    all_gather x1, waiting for transfers between devices, on_device(): square_all = lax.all_gather(square_own, 'rep', axis=0, tiled=True)  34.6 us
    reduce_scatter x1, waiting for transfers between devices, on_device(): lax.psum_scatter(cube_part.astype(jnp.bfloat16), 'rep', scatter_dimension...  28.3 us
    reduce_scatter x1, waiting for transfers between devices, on_device(): lax.psum_scatter(square_part.astype(jnp.bfloat16), 'rep', scatter_dimensi...  26.5 us
  transfers between devices with their start and end apart: 15, of which 12 were waited for; matrix products, arithmetic and copies ran while one was open for 4% of the time, Pallas kernels for 0%

commit v1 on v0

v1 whole, which is shorter than its diff:
```python
import jax
import jax.numpy as jnp
from jax import lax
from jax.experimental import pallas as pl
from jax.experimental.pallas import tpu as pltpu
from jax.sharding import PartitionSpec as P

ROWS = 16
COLS = 8
REPS = 4
GROUPS = 2
WIN = 8
BR = 24
BS = 128
Q = BS // REPS
HALF = BR + 1
KEPT = 2


def along_row(value, steps):
    pairs = [(i, (i + steps) % ROWS) for i in range(ROWS)]
    return lax.ppermute(value, "row", pairs)


def square_kernel(where, left_cols, cols, keep, lefts, *refs):
    panels, low, high, out, right = refs[:15], refs[15], refs[16], refs[17], refs[18]
    row = where[0]
    lane = lax.broadcasted_iota(jnp.int32, (BS, BS), 1) // Q

    def one(w, _):
        for d in range(ROWS):
            s = lax.rem(row + d, ROWS)
            k = left_cols[w * ROWS + s]
            for g in range(GROUPS):
                if d < 8:
                    block = panels[d][g * HALF + k]
                elif d == 8:
                    block = (low[k], high[1 + k])[g]
                else:
                    block = panels[d - 1][g * HALF + k]
                col = cols[d * GROUPS * BR + g * BR + k]
                for m in range(KEPT):
                    hit = col == keep[w * GROUPS * KEPT + g * KEPT + m]
                    at = (g * KEPT + m) * BS
                    right[pl.ds(pl.multiple_of(s * Q, Q), Q), at : at + BS] = jnp.where(
                        hit, block, jnp.zeros_like(block)
                    )
        full = jnp.dot(lefts[w], right[...], preferred_element_type=jnp.float32)
        parts = [full[:, i * BS : (i + 1) * BS] for i in range(GROUPS * KEPT)]
        for x in range(REPS):
            mixed = parts[x]
            for i in range(GROUPS * KEPT):
                if i != x:
                    moved = pltpu.roll(parts[i], (Q * (i - x)) % BS, 1)
                    mixed = jnp.where(lane == i, moved, mixed)
            out[x, w] = mixed.astype(jnp.bfloat16)
        return 0

    lax.fori_loop(0, WIN, one, 0)


def cube_kernel(where, mid_cols, cols, keep, own_keep, lefts, own, *refs):
    panels, low, high, out, right = refs[:15], refs[15], refs[16], refs[17], refs[18]
    row, rep = where[0], where[1]
    inner = ROWS * KEPT * Q
    wide = lax.broadcasted_iota(jnp.int32, (BS, BS), 1)
    tall = lax.broadcasted_iota(jnp.int32, (BS, BS), 0)
    place = wide == (rep * Q + tall % Q)
    slot = tall // Q

    def one(w, _):
        for d in range(ROWS):
            s = lax.rem(row + d, ROWS)
            for t in range(KEPT):
                k = mid_cols[w * ROWS * KEPT + s * KEPT + t]
                for g in range(GROUPS):
                    if d < 8:
                        block = panels[d][g * HALF + k]
                    elif d == 8:
                        block = (low[k], high[1 + k])[g]
                    else:
                        block = panels[d - 1][g * HALF + k]
                    hit = cols[d * GROUPS * BR + g * BR + k] == keep[w * GROUPS + g]
                    at = pl.multiple_of((s * KEPT + t) * Q, Q)
                    right[pl.ds(at, Q), g * BS : (g + 1) * BS] = jnp.where(
                        hit, block, jnp.zeros_like(block)
                    )
        for g in range(GROUPS):
            found = jnp.zeros((BS, BS), jnp.float32)
            for m in range(KEPT):
                hit = own_keep[w * GROUPS * KEPT + g * KEPT + m] == keep[w * GROUPS + g]
                scale = jnp.where(hit, -1.5, 0.0)
                found = jnp.where(slot == g * KEPT + m, scale, found)
            found = jnp.where(place, found, 0.0)
            right[inner : inner + BS, g * BS : (g + 1) * BS] = found.astype(jnp.bfloat16)
        total = jnp.dot(own[w], right[inner : inner + BS, :], preferred_element_type=jnp.float32)
        for c in range(COLS):
            total += jnp.dot(
                lefts[c, w], right[c * BS : (c + 1) * BS, :], preferred_element_type=jnp.float32
            )
        total = -2.0 * total
        for g in range(GROUPS):
            out[w, g] = total[:, g * BS : (g + 1) * BS].astype(jnp.bfloat16)
        return 0

    lax.fori_loop(0, WIN, one, 0)


def on_device(p_vals, p_cols, square_cols, cube_cols):
    row = lax.axis_index("row")
    rep = lax.axis_index("rep")
    smem = pl.BlockSpec(memory_space=pltpu.SMEM)
    vmem = pl.BlockSpec(memory_space=pltpu.VMEM)

    mine = lax.dynamic_slice_in_dim(p_vals, rep * Q, Q, 2)
    marks = p_cols.T.reshape(1, 1, GROUPS * BR).astype(jnp.bfloat16)
    marks = jnp.pad(marks, ((0, 0), (0, Q - 1), (0, BS - GROUPS * BR)))
    panel = jnp.concatenate([mine[:, 0], marks, mine[:, 1]], axis=0)

    left = lax.dynamic_slice_in_dim(p_vals[:WIN], rep * Q, Q, 3)
    left = left.transpose(0, 2, 1, 3).reshape(WIN // 2, 2, BS, GROUPS * Q)
    left = left.transpose(0, 2, 1, 3).reshape(WIN // 2 * BS, BS)
    notes = jnp.concatenate([p_cols[:WIN].reshape(-1), square_cols.reshape(-1)])
    notes = jnp.pad(notes.astype(jnp.bfloat16)[None], ((0, 15), (0, BS - notes.shape[0])))
    lefts = lax.all_gather(jnp.concatenate([left, notes], axis=0), "col")
    notes = lefts[:, WIN // 2 * BS, :].astype(jnp.int32)
    left_cols = notes[:, : WIN * GROUPS].reshape(COLS, WIN, GROUPS).transpose(1, 0, 2).reshape(-1)
    mid_cols = notes[:, WIN * GROUPS : WIN * GROUPS * (1 + KEPT)]
    mid_cols = mid_cols.reshape(COLS, WIN, GROUPS, KEPT).transpose(1, 0, 2, 3).reshape(-1)
    lefts = lefts[:, : WIN // 2 * BS].reshape(COLS, WIN // 2, BS, 2, GROUPS * Q)
    lefts = lefts.transpose(1, 3, 2, 0, 4).reshape(WIN, BS, ROWS * Q)

    ups, downs = [panel], [panel]
    for _ in range(ROWS // 2 - 1):
        ups.append(along_row(ups[-1], 1))
        downs.append(along_row(downs[-1], -1))
    low = along_row(ups[-1][:HALF], 1)
    high = along_row(downs[-1][HALF - 1 :], -1)
    panels = downs + ups[:0:-1]
    marks = [p[BR, 0, : GROUPS * BR] for p in panels]
    marks.insert(8, low[BR, 0, : GROUPS * BR])
    cols = jnp.concatenate(marks).astype(jnp.int32)

    where = jnp.stack([row, rep]).astype(jnp.int32)
    keep = square_cols.reshape(-1)
    partial = pl.pallas_call(
        square_kernel,
        out_shape=jax.ShapeDtypeStruct((REPS, WIN, BS, BS), jnp.bfloat16),
        in_specs=[smem] * 4 + [vmem] * 18,
        out_specs=vmem,
        scratch_shapes=[pltpu.VMEM((ROWS * Q, GROUPS * KEPT * BS), jnp.bfloat16)],
        compiler_params=pltpu.CompilerParams(vmem_limit_bytes=40 * 2**20),
    )(where, left_cols, cols, keep, lefts, *panels, low, high)
    parts = lax.all_to_all(partial, "rep", 0, 0, tiled=True)
    own = jnp.sum(parts.astype(jnp.float32), axis=0).astype(jnp.bfloat16)
    squares = lax.all_to_all(jnp.broadcast_to(own[None], (COLS,) + own.shape), "col", 0, 0)
    partial = pl.pallas_call(
        cube_kernel,
        out_shape=jax.ShapeDtypeStruct((WIN, GROUPS, BS, BS), jnp.bfloat16),
        in_specs=[smem] * 5 + [vmem] * 19,
        out_specs=vmem,
        scratch_shapes=[pltpu.VMEM((ROWS * KEPT * Q + BS, GROUPS * BS), jnp.bfloat16)],
        compiler_params=pltpu.CompilerParams(vmem_limit_bytes=40 * 2**20),
    )(where, mid_cols, cols, cube_cols.reshape(-1), keep, squares, own, *panels, low, high)
    parts = lax.all_to_all(partial, "rep", 0, 0, tiled=True)
    parts = parts.reshape((REPS, WIN // REPS) + parts.shape[1:]).astype(jnp.float32)
    return jnp.sum(parts, axis=0).astype(jnp.bfloat16)[:, :, None]


def solution(mesh):
    in_specs = (
        P("row", "col", None, None),
        P("row", "col"),
        P("row", "col", None),
        P("row", "col", None),
    )
    out_specs = P(("row", "rep"), "col", None, None, None)
    return jax.shard_map(
        on_device, mesh=mesh, in_specs=in_specs, out_specs=out_specs, check_vma=False
    )
```

time: 811 us -> 219 us (0.27)
  waiting for transfers between devices: 591 us -> 49.9 us
  starting transfers between devices: 118 us -> 73.8 us
  matrix products: 18 us -> 0 us
  blocking collectives: 9.31 us -> 24.6 us
  Pallas kernels: 0 us -> 11.4 us
  other arithmetic: 12.7 us -> 2.64 us
    ppermute x10 -> x16, waiting for transfers between devices: 433 us -> 25.6 us  [along_row(): return lax.ppermute(value, 'row', pairs)]
    psum x2 -> x0, waiting for transfers between devices: 68.3 us -> none  [from_root(): return lax.psum(jnp.where(mine, value, jnp.zeros_like(value)), axis)]
    ppermute x10 -> x16, starting transfers between devices: 118 us -> 59.3 us  [along_row(): return lax.ppermute(value, 'row', pairs)]
    reduce_scatter x2 -> x0, waiting for transfers between devices: 54.8 us -> none  [the longest x1 28.3 us: on_device(): lax.psum_scatter(cube_part.astype(jnp.bfloat16), 'rep', scatter_dimension...]
    all_gather x1, waiting for transfers between devices: 34.6 us -> 0.02 us  [on_device(): lefts = lax.all_gather(jnp.concatenate([left, notes], axis=0), 'col')]
    all_to_all x0 -> x2, blocking collectives: none -> 24.6 us  [on_device(): parts = lax.all_to_all(partial, 'rep', 0, 0, tiled=True)]
    all_to_all x0 -> x1, waiting for transfers between devices: none -> 24.2 us  [on_device(): lax.all_to_all(jnp.broadcast_to(own[None], (COLS,) + own.shape), 'col', 0...]
    unnamed x31 -> x74, local copies, waits for them, and re-layouts: 0.15 us -> 23.3 us
  transfers between devices with their start and end apart: 15 -> 18, of which waited for: 12 -> 9; matrix products, arithmetic and copies ran while one was open for 4% -> 8% of each run, Pallas kernels for 0% -> 0%
where the time goes in v1:
time: 219 us; the launch traced here: 218 us
  starting transfers between devices  73.8 us (34%)
  waiting for transfers between devices  49.9 us (23%)
  local copies, waits for them, and re-layouts  41.4 us (19%)
  blocking collectives  24.6 us (11%)
  between operations  13.9 us (6%)
  Pallas kernels  11.4 us (5%)
  other arithmetic  2.64 us (1%)
    ppermute x16, starting transfers between devices, along_row(): return lax.ppermute(value, 'row', pairs)  59.3 us
    ppermute x16, waiting for transfers between devices, along_row(): return lax.ppermute(value, 'row', pairs)  25.6 us
    all_to_all x2, blocking collectives, on_device(): parts = lax.all_to_all(partial, 'rep', 0, 0, tiled=True)  24.6 us
    all_to_all x1, waiting for transfers between devices, on_device(): lax.all_to_all(jnp.broadcast_to(own[None], (COLS,) + own.shape), 'col', 0...  24.2 us
    unnamed x74, local copies, waits for them, and re-layouts  23.3 us
    all_to_all x1, starting transfers between devices, on_device(): lax.all_to_all(jnp.broadcast_to(own[None], (COLS,) + own.shape), 'col', 0...  14.5 us
    pallas_call x1, Pallas kernels, on_device(): pl.pallas_call(square_kernel, out_shape=jax.ShapeDtypeStruct((REPS, WIN,...  5.77 us
    pallas_call x1, Pallas kernels, on_device(): pl.pallas_call(cube_kernel, out_shape=jax.ShapeDtypeStruct((WIN, GROUPS,...  5.59 us
  transfers between devices with their start and end apart: 18, of which 9 were waited for; matrix products, arithmetic and copies ran while one was open for 8% of the time, Pallas kernels for 0%

profile of v1, /device:TPU:1, one launch (start us, length us, event | category | flops | bytes accessed | tf_op | source)
XLA Modules:
  0.0 217.6 jit_solution(7428787324747901754)
XLA Ops:
  7.4 1.1 dynamic-slice_bitcast_fusion.1
  8.5 4.4 %collective-permute-start.7 = (bf16[49,32,128]{2,1,0:T(8,128)(2,1)S(1)}, bf16[49,32,128]{2,1,0:T(8,128)(2,1)S(1)}, u32[]{:S(2)}, u32[]{:S(2)}) collective-permute-start(bf16[49,32,128]{2,1,0:T(8,128)(2,1)S(1)} %fusion.3.refs_0_), channel_id=1, source_target_pairs={{0,32},{32,64},{64,96},{96,128},{128,160},{160,192},{192,224},{224... | collective-permute-start | bytes 1204232 | tf_op jit(solution)/shard_map/ppermute | solution.py:22
  12.9 9.5 %collective-permute-start = (bf16[49,32,128]{2,1,0:T(8,128)(2,1)S(1)}, bf16[49,32,128]{2,1,0:T(8,128)(2,1)S(1)}, u32[]{:S(2)}, u32[]{:S(2)}) collective-permute-start(bf16[49,32,128]{2,1,0:T(8,128)(2,1)S(1)} %fusion.3.refs_0_), channel_id=1, source_target_pairs={{0,480},{32,0},{64,32},{96,64},{128,96},{160,128},{192,160},{224,1... | collective-permute-start | bytes 1204232 | tf_op jit(solution)/shard_map/ppermute | solution.py:22
  24.7 4.7 %collective-permute-done.7.refs_14_ = bf16[49,32,128]{2,1,0:T(8,128)(2,1)S(1)} collective-permute-done((bf16[49,32,128]{2,1,0:T(8,128)(2,1)S(1)}, bf16[49,32,128]{2,1,0:T(8,128)(2,1)S(1)}, u32[]{:S(2)}, u32[]{:S(2)}) %collective-permute-start.7) | collective-permute-done | bytes 401440 | tf_op jit(solution)/shard_map/ppermute | solution.py:22
  29.4 1.9 collective-permute-start.8
  31.4 4.6 %collective-permute-start.1 = (bf16[49,32,128]{2,1,0:T(8,128)(2,1)S(1)}, bf16[49,32,128]{2,1,0:T(8,128)(2,1)S(1)}, u32[]{:S(2)}, u32[]{:S(2)}) collective-permute-start(bf16[49,32,128]{2,1,0:T(8,128)(2,1)S(1)} %collective-permute-done.refs_1_), channel_id=1, source_target_pairs={{0,480},{32,0},{64,32},{96,64},{128,96},{160,128},{192,160},{224,1... | collective-permute-start | bytes 1204232 | tf_op jit(solution)/shard_map/ppermute | solution.py:22
  36.0 6.1 %collective-permute-done.8.refs_13_ = bf16[49,32,128]{2,1,0:T(8,128)(2,1)S(1)} collective-permute-done((bf16[49,32,128]{2,1,0:T(8,128)(2,1)S(1)}, bf16[49,32,128]{2,1,0:T(8,128)(2,1)S(1)}, u32[]{:S(2)}, u32[]{:S(2)}) %collective-permute-start.8) | collective-permute-done | bytes 401440 | tf_op jit(solution)/shard_map/ppermute | solution.py:22
  42.1 1.9 collective-permute-start.9
  44.0 4.6 %collective-permute-start.2 = (bf16[49,32,128]{2,1,0:T(8,128)(2,1)S(1)}, bf16[49,32,128]{2,1,0:T(8,128)(2,1)S(1)}, u32[]{:S(2)}, u32[]{:S(2)}) collective-permute-start(bf16[49,32,128]{2,1,0:T(8,128)(2,1)S(1)} %collective-permute-done.1.refs_2_), channel_id=1, source_target_pairs={{0,480},{32,0},{64,32},{96,64},{128,96},{160,128},{192,160},{224,1... | collective-permute-start | bytes 1204232 | tf_op jit(solution)/shard_map/ppermute | solution.py:22
  50.1 3.7 %collective-permute-done.9.refs_12_ = bf16[49,32,128]{2,1,0:T(8,128)(2,1)S(1)} collective-permute-done((bf16[49,32,128]{2,1,0:T(8,128)(2,1)S(1)}, bf16[49,32,128]{2,1,0:T(8,128)(2,1)S(1)}, u32[]{:S(2)}, u32[]{:S(2)}) %collective-permute-start.9) | collective-permute-done | bytes 401440 | tf_op jit(solution)/shard_map/ppermute | solution.py:22
  53.8 1.9 collective-permute-start.10
  55.7 4.6 %collective-permute-start.3 = (bf16[49,32,128]{2,1,0:T(8,128)(2,1)S(1)}, bf16[49,32,128]{2,1,0:T(8,128)(2,1)S(1)}, u32[]{:S(2)}, u32[]{:S(2)}) collective-permute-start(bf16[49,32,128]{2,1,0:T(8,128)(2,1)S(1)} %collective-permute-done.2.refs_3_), channel_id=1, source_target_pairs={{0,480},{32,0},{64,32},{96,64},{128,96},{160,128},{192,160},{224,1... | collective-permute-start | bytes 1204232 | tf_op jit(solution)/shard_map/ppermute | solution.py:22
  61.9 2.8 %collective-permute-done.10.refs_11_ = bf16[49,32,128]{2,1,0:T(8,128)(2,1)S(1)} collective-permute-done((bf16[49,32,128]{2,1,0:T(8,128)(2,1)S(1)}, bf16[49,32,128]{2,1,0:T(8,128)(2,1)S(1)}, u32[]{:S(2)}, u32[]{:S(2)}) %collective-permute-start.10) | collective-permute-done | bytes 401440 | tf_op jit(solution)/shard_map/ppermute | solution.py:22
  64.6 1.9 collective-permute-start.11
  66.6 4.6 %collective-permute-start.4 = (bf16[49,32,128]{2,1,0:T(8,128)(2,1)S(1)}, bf16[49,32,128]{2,1,0:T(8,128)(2,1)}, u32[]{:S(2)}, u32[]{:S(2)}) collective-permute-start(bf16[49,32,128]{2,1,0:T(8,128)(2,1)S(1)} %collective-permute-done.3.refs_4_), channel_id=1, source_target_pairs={{0,480},{32,0},{64,32},{96,64},{128,96},{160,128},{192,160},{224,1... | collective-permute-start | bytes 1204232 | tf_op jit(solution)/shard_map/ppermute | solution.py:22
  71.2 2.3 %slice.119 = bf16[8,512,128]{2,1,0:T(8,128)(2,1)} slice(bf16[8,528,128]{2,1,0:T(8,128)(2,1)} %bitcast.75), slice={[0:8], [0:512], [0:128]} | slice | bytes 2097152 | tf_op jit(solution)/shard_map/slice | solution.py:130
  73.5 1.5 copy.57
  75.0 1.1 reshape.95
  76.1 2.5 %copy.58 = bf16[4,2,128,8,64]{2,4,3,1,0:T(8,128)(2,1)} copy(bf16[4,2,128,8,64]{2,0,4,1,3:T(4,128)(2,1)} %bitcast.72) | data formatting | bytes 2097152 | tf_op jit(solution)/shard_map/transpose | solution.py:131
  78.6 1.5 copy.59.lefts
  81.1 1.9 collective-permute-start.12
  83.1 4.6 %collective-permute-start.5 = (bf16[49,32,128]{2,1,0:T(8,128)(2,1)}, bf16[49,32,128]{2,1,0:T(8,128)(2,1)S(1)}, u32[]{:S(2)}, u32[]{:S(2)}) collective-permute-start(bf16[49,32,128]{2,1,0:T(8,128)(2,1)} %collective-permute-done.4.refs_5_), channel_id=1, source_target_pairs={{0,480},{32,0},{64,32},{96,64},{128,96},{160,128},{192,160},{224,1... | collective-permute-start | bytes 1204232 | tf_op jit(solution)/shard_map/ppermute | solution.py:22
  89.0 2.2 collective-permute-done.12.refs_9_
  91.1 1.9 collective-permute-start.13
  93.1 4.6 %collective-permute-start.6 = (bf16[49,32,128]{2,1,0:T(8,128)(2,1)S(1)}, bf16[49,32,128]{2,1,0:T(8,128)(2,1)S(1)}, u32[]{:S(2)}, u32[]{:S(2)}) collective-permute-start(bf16[49,32,128]{2,1,0:T(8,128)(2,1)S(1)} %collective-permute-done.5.refs_6_), channel_id=1, source_target_pairs={{0,480},{32,0},{64,32},{96,64},{128,96},{160,128},{192,160},{224,1... | collective-permute-start | bytes 1204232 | tf_op jit(solution)/shard_map/ppermute | solution.py:22
  97.7 3.3 %collective-permute-done.13.refs_8_ = bf16[49,32,128]{2,1,0:T(8,128)(2,1)S(1)} collective-permute-done((bf16[49,32,128]{2,1,0:T(8,128)(2,1)S(1)}, bf16[49,32,128]{2,1,0:T(8,128)(2,1)S(1)}, u32[]{:S(2)}, u32[]{:S(2)}) %collective-permute-start.13) | collective-permute-done | bytes 401440 | tf_op jit(solution)/shard_map/ppermute | solution.py:22
  101.0 1.9 collective-permute-start.14
  103.6 4.6 %collective-permute-start.15 = (bf16[25,32,128]{2,1,0:T(8,128)(2,1)}, bf16[25,32,128]{2,1,0:T(8,128)(2,1)S(1)}, u32[]{:S(2)}, u32[]{:S(2)}) collective-permute-start(bf16[25,32,128]{2,1,0:T(8,128)(2,1)} %slice.120), channel_id=1, source_target_pairs={{0,480},{32,0},{64,32},{96,64},{128,96},{160,128},{192,160},{224,1... | collective-permute-start | bytes 614408 | tf_op jit(solution)/shard_map/ppermute | solution.py:22
  108.2 1.1 collective-permute-done.14.refs_15_
  109.4 1.8 collective-permute-done.15.refs_16_
  111.2 1.0 copy-done.7
  113.2 1.0 copy-done.13
  114.2 1.0 copy-done.16
  115.2 1.0 copy-done.19
  116.2 1.0 copy-done.22
  117.2 1.0 copy-done.25
  118.2 1.0 copy-done.28
  119.2 5.8 %shard_map.46 = bf16[4,8,128,128]{3,2,1,0:T(8,128)(2,1)S(1)} custom-call(s32[2]{0:T(128)S(1)} %pad_add_fusion.where, s32[128]{0:T(128)S(1)} %reshape.94.left_cols, s32[768]{0:T(1024)S(1)} %convert_element_type.50.cols, s32[32]{0:T(128)S(1)} %reshape.92.keep.own_keep, bf16[8,128,512]{2,1,0:T(8,128)(2,1)S(1)} %copy.59.lefts, ...), custom_call_target="tpu_custom_call" | custom-call | tf_op jit(solution)/shard_map/pallas_call | solution.py:146
  125.0 13.6 %all_to_all.15 = bf16[4,8,128,128]{3,2,1,0:T(8,128)(2,1)S(1)} all-to-all(bf16[4,8,128,128]{3,2,1,0:T(8,128)(2,1)S(1)} %shard_map.46), channel_id=1, replica_groups=mesh['row'=16,'col'=8,'rep'=4] {'rep'}, dimensions={0} | all-to-all | bytes 2097152 | tf_op jit(solution)/shard_map/all_to_all | solution.py:154
  138.8 1.9 broadcast_in_dim.4
  140.6 14.5 %all-to-all-start.1 = ((bf16[8,8,128,128]{3,2,1,0:T(8,128)(2,1)}), bf16[8,8,128,128]{3,2,1,0:T(8,128)(2,1)S(1)}, u32[]{:S(2)}, u32[]{:S(2)}) async-start(bf16[8,8,128,128]{3,2,1,0:T(8,128)(2,1)} %broadcast_in_dim.4), calls=%async_computation.1 | async-start | bytes 4194304 | tf_op jit(solution)/shard_map/all_to_all | solution.py:156
  157.3 24.2 %all-to-all-done.1.lefts = bf16[8,8,128,128]{3,2,1,0:T(8,128)(2,1)S(1)} async-done(((bf16[8,8,128,128]{3,2,1,0:T(8,128)(2,1)}), bf16[8,8,128,128]{3,2,1,0:T(8,128)(2,1)S(1)}, u32[]{:S(2)}, u32[]{:S(2)}) %all-to-all-start.1) | async-done | bytes 2097184 | tf_op jit(solution)/shard_map/all_to_all | solution.py:156
  182.5 1.0 copy-done.3
  184.5 1.0 copy-done.8
  185.5 1.0 copy-done.11
  187.4 1.0 copy-done.17
  193.4 5.6 %shard_map.47 = bf16[8,2,128,128]{3,2,1,0:T(8,128)(2,1)S(1)} custom-call(s32[2]{0:T(128)S(1)} %pad_add_fusion.where, s32[256]{0:T(256)S(1)} %reshape.90.mid_cols, s32[768]{0:T(1024)S(1)} %convert_element_type.50.cols, s32[16]{0:T(128)S(1)} %reshape.91.keep, s32[32]{0:T(128)S(1)} %reshape.92.keep.own_keep, bf16[8,8,128,128]{3,2,1,0:T(8,128)(2,1)S(1)} %all-to-all-done.1.lefts, ...), custom_call_target="tpu_custom_call" | custom-call | tf_op jit(solution)/shard_map/pallas_call | solution.py:157
  199.0 11.0 %all_to_all.16 = bf16[8,2,128,128]{3,2,1,0:T(8,128)(2,1)S(1)} all-to-all(bf16[8,2,128,128]{3,2,1,0:T(8,128)(2,1)S(1)} %shard_map.47), channel_id=1, replica_groups=mesh['row'=16,'col'=8,'rep'=4] {'rep'}, dimensions={0} | all-to-all | bytes 1048576 | tf_op jit(solution)/shard_map/all_to_all | solution.py:165
  (124 shorter events, 21.4 us)
Async XLA Ops:
  6.5 15.8 %copy-start.34 = (s32[24,2]{0,1:T(2,128)S(1)}, s32[24,2]{0,1:T(2,128)}, u32[]{:S(2)}) copy-start(s32[24,2]{0,1:T(2,128)} %param.5) | copy-start | bytes 580
  6.5 16.4 %slice-start = ((bf16[24,2,128,128]{3,2,1,0:T(8,128)(2,1)}), bf16[8,2,128,128]{3,2,1,0:T(8,128)(2,1)S(1)}, s32[]{:S(2)}) async-start(bf16[24,2,128,128]{3,2,1,0:T(8,128)(2,1)} %param.4), calls=%async_computation.4 | async-start | bytes 1048576 | tf_op jit(solution)/shard_map/slice | solution.py:120
  6.5 15.8 %copy-start.32 = (s32[8,2,2]{0,2,1:T(2,128)S(1)}, s32[8,2,2]{0,2,1:T(2,128)}, u32[]{:S(2)}) copy-start(s32[8,2,2]{0,2,1:T(2,128)} %param.6) | copy-start | bytes 388
  6.5 64.6 %all-gather.3.cloned.1.call-start = ((), (), s32[]{:S(2)}) async-start(), calls=%async_computation.3 | async-start | bytes 1216512 | tf_op jit(solution)/shard_map/all_gather | solution.py:125
  8.5 21.0 %collective-permute-start.7 = (bf16[49,32,128]{2,1,0:T(8,128)(2,1)S(1)}, bf16[49,32,128]{2,1,0:T(8,128)(2,1)S(1)}, u32[]{:S(2)}, u32[]{:S(2)}) collective-permute-start(bf16[49,32,128]{2,1,0:T(8,128)(2,1)S(1)} %fusion.3.refs_0_), channel_id=1, source_target_pairs={{0,32},{32,64},{64,96},{96,128},{128,160},{160,192},{192,224},{224... | collective-permute-start | bytes 1204232 | tf_op jit(solution)/shard_map/ppermute | solution.py:22
  12.9 18.5 %collective-permute-start = (bf16[49,32,128]{2,1,0:T(8,128)(2,1)S(1)}, bf16[49,32,128]{2,1,0:T(8,128)(2,1)S(1)}, u32[]{:S(2)}, u32[]{:S(2)}) collective-permute-start(bf16[49,32,128]{2,1,0:T(8,128)(2,1)S(1)} %fusion.3.refs_0_), channel_id=1, source_target_pairs={{0,480},{32,0},{64,32},{96,64},{128,96},{160,128},{192,160},{224,1... | collective-permute-start | bytes 1204232 | tf_op jit(solution)/shard_map/ppermute | solution.py:22
  29.4 81.8 %copy-start.2 = (bf16[49,32,128]{2,1,0:T(8,128)(2,1)}, bf16[49,32,128]{2,1,0:T(8,128)(2,1)S(1)}, u32[]{:S(2)}) copy-start(bf16[49,32,128]{2,1,0:T(8,128)(2,1)S(1)} %collective-permute-done.7.refs_14_) | copy-start | bytes 1204228
  29.4 12.6 %collective-permute-start.8 = (bf16[49,32,128]{2,1,0:T(8,128)(2,1)S(1)}, bf16[49,32,128]{2,1,0:T(8,128)(2,1)S(1)}, u32[]{:S(2)}, u32[]{:S(2)}) collective-permute-start(bf16[49,32,128]{2,1,0:T(8,128)(2,1)S(1)} %collective-permute-done.7.refs_14_), channel_id=1, source_target_pairs={{0,32},{32,64},{64,96},{96,128},{128,160},{160,192},{192,224},{224... | collective-permute-start | bytes 1204232 | tf_op jit(solution)/shard_map/ppermute | solution.py:22
  31.4 79.8 %copy-start.4 = (bf16[49,32,128]{2,1,0:T(8,128)(2,1)}, bf16[49,32,128]{2,1,0:T(8,128)(2,1)S(1)}, u32[]{:S(2)}) copy-start(bf16[49,32,128]{2,1,0:T(8,128)(2,1)S(1)} %collective-permute-done.refs_1_) | copy-start | bytes 1204228
  31.4 12.6 %collective-permute-start.1 = (bf16[49,32,128]{2,1,0:T(8,128)(2,1)S(1)}, bf16[49,32,128]{2,1,0:T(8,128)(2,1)S(1)}, u32[]{:S(2)}, u32[]{:S(2)}) collective-permute-start(bf16[49,32,128]{2,1,0:T(8,128)(2,1)S(1)} %collective-permute-done.refs_1_), channel_id=1, source_target_pairs={{0,480},{32,0},{64,32},{96,64},{128,96},{160,128},{192,160},{224,1... | collective-permute-start | bytes 1204232 | tf_op jit(solution)/shard_map/ppermute | solution.py:22
  42.1 11.7 %collective-permute-start.9 = (bf16[49,32,128]{2,1,0:T(8,128)(2,1)S(1)}, bf16[49,32,128]{2,1,0:T(8,128)(2,1)S(1)}, u32[]{:S(2)}, u32[]{:S(2)}) collective-permute-start(bf16[49,32,128]{2,1,0:T(8,128)(2,1)S(1)} %collective-permute-done.8.refs_13_), channel_id=1, source_target_pairs={{0,32},{32,64},{64,96},{96,128},{128,160},{160,192},{192,224},{224... | collective-permute-start | bytes 1204232 | tf_op jit(solution)/shard_map/ppermute | solution.py:22
  44.0 11.7 %collective-permute-start.2 = (bf16[49,32,128]{2,1,0:T(8,128)(2,1)S(1)}, bf16[49,32,128]{2,1,0:T(8,128)(2,1)S(1)}, u32[]{:S(2)}, u32[]{:S(2)}) collective-permute-start(bf16[49,32,128]{2,1,0:T(8,128)(2,1)S(1)} %collective-permute-done.1.refs_2_), channel_id=1, source_target_pairs={{0,480},{32,0},{64,32},{96,64},{128,96},{160,128},{192,160},{224,1... | collective-permute-start | bytes 1204232 | tf_op jit(solution)/shard_map/ppermute | solution.py:22
  53.8 10.8 %collective-permute-start.10 = (bf16[49,32,128]{2,1,0:T(8,128)(2,1)S(1)}, bf16[49,32,128]{2,1,0:T(8,128)(2,1)S(1)}, u32[]{:S(2)}, u32[]{:S(2)}) collective-permute-start(bf16[49,32,128]{2,1,0:T(8,128)(2,1)S(1)} %collective-permute-done.9.refs_12_), channel_id=1, source_target_pairs={{0,32},{32,64},{64,96},{96,128},{128,160},{160,192},{192,224},{224... | collective-permute-start | bytes 1204232 | tf_op jit(solution)/shard_map/ppermute | solution.py:22
  55.7 10.8 %collective-permute-start.3 = (bf16[49,32,128]{2,1,0:T(8,128)(2,1)S(1)}, bf16[49,32,128]{2,1,0:T(8,128)(2,1)S(1)}, u32[]{:S(2)}, u32[]{:S(2)}) collective-permute-start(bf16[49,32,128]{2,1,0:T(8,128)(2,1)S(1)} %collective-permute-done.2.refs_3_), channel_id=1, source_target_pairs={{0,480},{32,0},{64,32},{96,64},{128,96},{160,128},{192,160},{224,1... | collective-permute-start | bytes 1204232 | tf_op jit(solution)/shard_map/ppermute | solution.py:22
  64.6 10.3 %copy-start.18 = (bf16[49,32,128]{2,1,0:T(8,128)(2,1)}, bf16[49,32,128]{2,1,0:T(8,128)(2,1)S(1)}, u32[]{:S(2)}) copy-start(bf16[49,32,128]{2,1,0:T(8,128)(2,1)S(1)} %collective-permute-done.10.refs_11_) | copy-start | bytes 1204228
  64.6 16.5 %collective-permute-start.11 = (bf16[49,32,128]{2,1,0:T(8,128)(2,1)S(1)}, bf16[49,32,128]{2,1,0:T(8,128)(2,1)}, u32[]{:S(2)}, u32[]{:S(2)}) collective-permute-start(bf16[49,32,128]{2,1,0:T(8,128)(2,1)S(1)} %collective-permute-done.10.refs_11_), channel_id=1, source_target_pairs={{0,32},{32,64},{64,96},{96,128},{128,160},{160,192},{192,224},{224... | collective-permute-start | bytes 1204232 | tf_op jit(solution)/shard_map/ppermute | solution.py:22
  66.5 8.4 %copy-start.21 = (bf16[49,32,128]{2,1,0:T(8,128)(2,1)}, bf16[49,32,128]{2,1,0:T(8,128)(2,1)S(1)}, u32[]{:S(2)}) copy-start(bf16[49,32,128]{2,1,0:T(8,128)(2,1)S(1)} %collective-permute-done.3.refs_4_) | copy-start | bytes 1204228
  66.6 16.5 %collective-permute-start.4 = (bf16[49,32,128]{2,1,0:T(8,128)(2,1)S(1)}, bf16[49,32,128]{2,1,0:T(8,128)(2,1)}, u32[]{:S(2)}, u32[]{:S(2)}) collective-permute-start(bf16[49,32,128]{2,1,0:T(8,128)(2,1)S(1)} %collective-permute-done.3.refs_4_), channel_id=1, source_target_pairs={{0,480},{32,0},{64,32},{96,64},{128,96},{160,128},{192,160},{224,1... | collective-permute-start | bytes 1204232 | tf_op jit(solution)/shard_map/ppermute | solution.py:22
  81.1 10.0 %collective-permute-start.12 = (bf16[49,32,128]{2,1,0:T(8,128)(2,1)}, bf16[49,32,128]{2,1,0:T(8,128)(2,1)S(1)}, u32[]{:S(2)}, u32[]{:S(2)}) collective-permute-start(bf16[49,32,128]{2,1,0:T(8,128)(2,1)} %collective-permute-done.11.refs_10_), channel_id=1, source_target_pairs={{0,32},{32,64},{64,96},{96,128},{128,160},{160,192},{192,224},{224... | collective-permute-start | bytes 1204232 | tf_op jit(solution)/shard_map/ppermute | solution.py:22
  83.1 10.0 %collective-permute-start.5 = (bf16[49,32,128]{2,1,0:T(8,128)(2,1)}, bf16[49,32,128]{2,1,0:T(8,128)(2,1)S(1)}, u32[]{:S(2)}, u32[]{:S(2)}) collective-permute-start(bf16[49,32,128]{2,1,0:T(8,128)(2,1)} %collective-permute-done.4.refs_5_), channel_id=1, source_target_pairs={{0,480},{32,0},{64,32},{96,64},{128,96},{160,128},{192,160},{224,1... | collective-permute-start | bytes 1204232 | tf_op jit(solution)/shard_map/ppermute | solution.py:22
  91.1 11.8 %copy-start.24 = (bf16[49,32,128]{2,1,0:T(8,128)(2,1)}, bf16[49,32,128]{2,1,0:T(8,128)(2,1)S(1)}, u32[]{:S(2)}) copy-start(bf16[49,32,128]{2,1,0:T(8,128)(2,1)S(1)} %collective-permute-done.12.refs_9_) | copy-start | bytes 1204228
  91.1 9.8 %collective-permute-start.13 = (bf16[49,32,128]{2,1,0:T(8,128)(2,1)S(1)}, bf16[49,32,128]{2,1,0:T(8,128)(2,1)S(1)}, u32[]{:S(2)}, u32[]{:S(2)}) collective-permute-start(bf16[49,32,128]{2,1,0:T(8,128)(2,1)S(1)} %collective-permute-done.12.refs_9_), channel_id=1, source_target_pairs={{0,32},{32,64},{64,96},{96,128},{128,160},{160,192},{192,224},{224... | collective-permute-start | bytes 1204232 | tf_op jit(solution)/shard_map/ppermute | solution.py:22
  93.1 10.5 %copy-start.27 = (bf16[49,32,128]{2,1,0:T(8,128)(2,1)}, bf16[49,32,128]{2,1,0:T(8,128)(2,1)S(1)}, u32[]{:S(2)}) copy-start(bf16[49,32,128]{2,1,0:T(8,128)(2,1)S(1)} %collective-permute-done.5.refs_6_) | copy-start | bytes 1204228
  93.1 9.8 %collective-permute-start.6 = (bf16[49,32,128]{2,1,0:T(8,128)(2,1)S(1)}, bf16[49,32,128]{2,1,0:T(8,128)(2,1)S(1)}, u32[]{:S(2)}, u32[]{:S(2)}) collective-permute-start(bf16[49,32,128]{2,1,0:T(8,128)(2,1)S(1)} %collective-permute-done.5.refs_6_), channel_id=1, source_target_pairs={{0,480},{32,0},{64,32},{96,64},{128,96},{160,128},{192,160},{224,1... | collective-permute-start | bytes 1204232 | tf_op jit(solution)/shard_map/ppermute | solution.py:22
  101.0 8.3 %collective-permute-start.14 = (bf16[25,32,128]{2,1,0:T(8,128)(2,1)S(1)}, bf16[25,32,128]{2,1,0:T(8,128)(2,1)S(1)}, u32[]{:S(2)}, u32[]{:S(2)}) collective-permute-start(bf16[25,32,128]{2,1,0:T(8,128)(2,1)S(1)} %slice.110), channel_id=1, source_target_pairs={{0,32},{32,64},{64,96},{96,128},{128,160},{160,192},{192,224},{224... | collective-permute-start | bytes 614408 | tf_op jit(solution)/shard_map/ppermute | solution.py:22
  103.6 7.6 %collective-permute-start.15 = (bf16[25,32,128]{2,1,0:T(8,128)(2,1)}, bf16[25,32,128]{2,1,0:T(8,128)(2,1)S(1)}, u32[]{:S(2)}, u32[]{:S(2)}) collective-permute-start(bf16[25,32,128]{2,1,0:T(8,128)(2,1)} %slice.120), channel_id=1, source_target_pairs={{0,480},{32,0},{64,32},{96,64},{128,96},{160,128},{192,160},{224,1... | collective-permute-start | bytes 614408 | tf_op jit(solution)/shard_map/ppermute | solution.py:22
  111.2 1.0 copy-start.7
  112.2 1.0 copy-start.10
  113.2 1.0 copy-start.13
  114.2 1.0 copy-start.16
  115.2 1.0 copy-start.19
  116.2 1.0 copy-start.22
  117.2 1.0 copy-start.25
  118.2 1.0 copy-start.28
  119.2 5.8 %copy-start.30 = (bf16[25,32,128]{2,1,0:T(8,128)(2,1)}, bf16[25,32,128]{2,1,0:T(8,128)(2,1)S(1)}, u32[]{:S(2)}) copy-start(bf16[25,32,128]{2,1,0:T(8,128)(2,1)S(1)} %collective-permute-done.15.refs_16_) | copy-start | bytes 614404
  138.7 1.9 copy-start
  140.6 14.6 %copy-start.33 = (s32[8,2,1]{0,2,1:T(1,128)S(1)}, s32[8,2,1]{0,2,1:T(1,128)}, u32[]{:S(2)}) copy-start(s32[8,2,1]{0,2,1:T(1,128)} %param.7) | copy-start | bytes 196
  140.6 40.9 %all-to-all-start.1 = ((bf16[8,8,128,128]{3,2,1,0:T(8,128)(2,1)}), bf16[8,8,128,128]{3,2,1,0:T(8,128)(2,1)S(1)}, u32[]{:S(2)}, u32[]{:S(2)}) async-start(bf16[8,8,128,128]{3,2,1,0:T(8,128)(2,1)} %broadcast_in_dim.4), calls=%async_computation.1 | async-start | bytes 4194304 | tf_op jit(solution)/shard_map/all_to_all | solution.py:156
  182.5 1.0 copy-start.3
  183.5 1.0 copy-start.5
  184.4 1.0 copy-start.8
  185.4 1.0 copy-start.11
  186.4 1.0 copy-start.14
  187.4 1.0 copy-start.17
  188.4 1.0 copy-start.20
  189.4 1.0 copy-start.23
  190.4 1.0 copy-start.26
  191.4 1.0 copy-start.29
  (6 other events, 4.9 us)
Sparse Core Ops, SparseCore 0:
  24.5 30.0 all-gather.2

commit v2 on v1

v2 whole, which is shorter than its diff:
```python
import jax
import jax.numpy as jnp
from jax import lax
from jax.experimental import pallas as pl
from jax.experimental.pallas import tpu as pltpu
from jax.sharding import PartitionSpec as P

ROWS = 16
COLS = 8
CHIPS = 4
REPS = 4
GROUPS = 2
WIN = 8
BR = 24
BS = 128
Q = BS // REPS
HALF = BR + 1
KEPT = 2
SLOTS = GROUPS * KEPT
MARKS = GROUPS * BR
INNER = ROWS * KEPT * Q

EVEN = [(i, i ^ 1) for i in range(ROWS)]
ODD = [(i, (i + 1) % ROWS if i % 2 else (i - 1) % ROWS) for i in range(ROWS)]
CORES = [(i, i ^ 1) for i in range(COLS)]
SAME_CORE = [[c + i for i in range(0, COLS, 2)] for c in range(2)]

SMEM = pl.BlockSpec(memory_space=pltpu.SMEM)
VMEM = pl.BlockSpec(memory_space=pltpu.VMEM)


def over_even(value):
    return lax.ppermute(value, "row", EVEN)


def over_odd(value):
    return lax.ppermute(value, "row", ODD)


def step_of(where, offset):
    return lax.rem(where[0] + where[2] * offset + ROWS, ROWS)


def put_square(right, w, s, blocks, cols, base, k, keep):
    for g in range(GROUPS):
        block = blocks[g]
        col = cols[base + g * BR + k]
        for m in range(KEPT):
            slot = g * KEPT + m
            hit = col == keep[w * SLOTS + slot]
            right[w, pl.ds(pl.multiple_of(s * Q, Q), Q), slot * BS : (slot + 1) * BS] = jnp.where(
                hit, block, jnp.zeros_like(block)
            )


def put_cube(right, w, s, t, blocks, cols, base, k, keep):
    at = pl.multiple_of((s * KEPT + t) * Q, Q)
    for g in range(GROUPS):
        block = blocks[g]
        hit = cols[base + g * BR + k] == keep[w * GROUPS + g]
        right[w, pl.ds(at, Q), g * BS : (g + 1) * BS] = jnp.where(hit, block, jnp.zeros_like(block))


def late_blocks(i, k, near, far, low, high):
    if i < 2:
        panel = (near, far)[i]
        return panel[k], panel[HALF + k]
    return low[k], high[1 + k]


LATE = (ROWS // 2 - 1, 1 - ROWS // 2, ROWS // 2)


def early_kernel(where, left_cols, mid_cols, cols, keep, cube_keep, *refs):
    panels, squares, cubes = refs[:-2], refs[-2], refs[-1]
    wide = lax.broadcasted_iota(jnp.int32, (BS, BS), 1)
    tall = lax.broadcasted_iota(jnp.int32, (BS, BS), 0)
    place = wide == (where[1] * Q + tall % Q)
    near = (len(panels) + 1) // 2

    def one(w, _):
        for i, panel in enumerate(panels):
            s = step_of(where, i if i < near else near - 1 - i)
            k = left_cols[w * ROWS + s]
            put_square(squares, w, s, (panel[k], panel[HALF + k]), cols, i * MARKS, k, keep)
            for t in range(KEPT):
                k = mid_cols[(w * ROWS + s) * KEPT + t]
                blocks = (panel[k], panel[HALF + k])
                put_cube(cubes, w, s, t, blocks, cols, i * MARKS, k, cube_keep)
        for g in range(GROUPS):
            found = jnp.zeros((BS, BS), jnp.float32)
            for m in range(KEPT):
                hit = keep[w * SLOTS + g * KEPT + m] == cube_keep[w * GROUPS + g]
                scale = jnp.where(hit, -1.5, 0.0)
                found = jnp.where(tall // Q == g * KEPT + m, scale, found)
            found = jnp.where(place, found, 0.0)
            cubes[w, INNER : INNER + BS, g * BS : (g + 1) * BS] = found.astype(jnp.bfloat16)
        return 0

    lax.fori_loop(0, WIN, one, 0)


def square_kernel(where, left_cols, cols, keep, lefts, near, far, low, high, given, out, right):
    lane = lax.broadcasted_iota(jnp.int32, (BS, BS), 1) // Q

    def one(w, _):
        for i, offset in enumerate(LATE):
            s = step_of(where, offset)
            k = left_cols[w * ROWS + s]
            blocks = late_blocks(i, k, near, far, low, high)
            put_square(right, w, s, blocks, cols, i * MARKS, k, keep)
        rows = pl.ds(pl.multiple_of(w * BS, BS), BS)
        left = jnp.concatenate([lefts[y, rows, :] for y in range(CHIPS)], axis=1)
        full = jnp.dot(left, right[w], preferred_element_type=jnp.float32)
        parts = [full[:, i * BS : (i + 1) * BS] for i in range(SLOTS)]
        for x in range(REPS):
            mixed = parts[x]
            for i in range(SLOTS):
                if i != x:
                    moved = pltpu.roll(parts[i], (Q * (i - x)) % BS, 1)
                    mixed = jnp.where(lane == i, moved, mixed)
            out[x, w] = mixed.astype(jnp.bfloat16)
        return 0

    lax.fori_loop(0, WIN, one, 0)


def late_kernel(where, mid_cols, cols, cube_keep, near, far, low, high, given, right):
    def one(w, _):
        for i, offset in enumerate(LATE):
            s = step_of(where, offset)
            for t in range(KEPT):
                k = mid_cols[(w * ROWS + s) * KEPT + t]
                blocks = late_blocks(i, k, near, far, low, high)
                put_cube(right, w, s, t, blocks, cols, i * MARKS, k, cube_keep)
        return 0

    lax.fori_loop(0, WIN, one, 0)


def cube_kernel(where, own, same, other, right, out):
    core = where[3]

    def one(w, _):
        total = jnp.dot(own[w], right[w, INNER:, :], preferred_element_type=jnp.float32)
        for y in range(CHIPS):
            for lefts, c in ((same, 2 * y + core), (other, 2 * y + 1 - core)):
                rows = pl.ds(pl.multiple_of(c * BS, BS), BS)
                total += jnp.dot(lefts[y, w], right[w, rows, :], preferred_element_type=jnp.float32)
        total = -2.0 * total
        for g in range(GROUPS):
            out[w, g] = total[:, g * BS : (g + 1) * BS].astype(jnp.bfloat16)
        return 0

    lax.fori_loop(0, WIN, one, 0)


def call(kernel, out, scalars, arrays, aliases=None, flops=0):
    moved = sum(a.size * 2 for a in arrays)
    return pl.pallas_call(
        kernel,
        out_shape=out,
        in_specs=[SMEM] * len(scalars) + [VMEM] * len(arrays),
        out_specs=jax.tree.map(lambda _: VMEM, out),
        input_output_aliases=aliases or {},
        cost_estimate=pl.CostEstimate(flops=flops, bytes_accessed=moved, transcendentals=0),
        compiler_params=pltpu.CompilerParams(vmem_limit_bytes=8 * 2**20),
    )(*scalars, *arrays)


def shaped(*shape):
    return jax.ShapeDtypeStruct(shape, jnp.bfloat16)


def columns_of(marks):
    return jnp.concatenate([m[BR, 0, :MARKS] for m in marks]).astype(jnp.int32)


def on_device(p_vals, p_cols, square_cols, cube_cols):
    row = lax.axis_index("row")
    rep = lax.axis_index("rep")
    core = lax.axis_index("col") % 2
    where = jnp.stack([row, rep, 1 - 2 * (row % 2), core]).astype(jnp.int32)

    mine = lax.dynamic_slice_in_dim(p_vals, rep * Q, Q, 2)
    marks = p_cols.T.reshape(1, 1, MARKS).astype(jnp.bfloat16)
    marks = jnp.pad(marks, ((0, 0), (0, Q - 1), (0, BS - MARKS)))
    panel = jnp.concatenate([mine[:, 0], marks, mine[:, 1]], axis=0)

    left = lax.dynamic_slice_in_dim(p_vals[:WIN], rep * Q, Q, 3)
    left = left.transpose(0, 2, 1, 3).reshape(WIN * BS, GROUPS * Q)
    notes = jnp.concatenate([p_cols[:WIN].reshape(-1), square_cols.reshape(-1)])
    notes = jnp.pad(notes.astype(jnp.bfloat16)[None], ((0, 15), (0, GROUPS * Q - notes.shape[0])))
    left = jnp.concatenate([left, notes], axis=0)
    beside = lax.ppermute(left, "col", CORES)
    left = jnp.where(
        core == 0,
        jnp.concatenate([left, beside], axis=1),
        jnp.concatenate([beside, left], axis=1),
    )
    lefts = lax.all_gather(left, "col", axis_index_groups=SAME_CORE)
    notes = lefts[:, WIN * BS, :].astype(jnp.int32).reshape(COLS, GROUPS * Q)
    left_cols = notes[:, : WIN * GROUPS].reshape(COLS, WIN, GROUPS).transpose(1, 0, 2).reshape(-1)
    mid_cols = notes[:, WIN * GROUPS : WIN * GROUPS * (1 + KEPT)]
    mid_cols = mid_cols.reshape(COLS, WIN, GROUPS, KEPT).transpose(1, 0, 2, 3).reshape(-1)

    evens, odds = [panel], [panel]
    for _ in range(ROWS // 2 - 1):
        even, odd = over_even(odds[-1]), over_odd(evens[-1])
        evens.append(even)
        odds.append(odd)
    low = over_even(odds[-1][:HALF])
    high = over_odd(evens[-1][HALF - 1 :])
    early = evens[:-1] + odds[1:-1]
    late = [evens[-1], odds[-1], low, high]

    keep = square_cols.reshape(-1)
    cube_keep = cube_cols.reshape(-1)
    squares, cubes = call(
        early_kernel,
        (shaped(WIN, ROWS * Q, SLOTS * BS), shaped(WIN, INNER + BS, GROUPS * BS)),
        (where, left_cols, mid_cols, columns_of(early), keep, cube_keep),
        early,
    )
    cols = columns_of(late[:3])
    partial, _ = call(
        square_kernel,
        (shaped(REPS, WIN, BS, BS), shaped(*squares.shape)),
        (where, left_cols, cols, keep),
        (lefts, *late, squares),
        {9: 1},
        WIN * 2 * BS * ROWS * Q * SLOTS * BS,
    )
    cubes = call(late_kernel, shaped(*cubes.shape), (where, mid_cols, cols, cube_keep), (*late, cubes), {8: 0})
    parts = lax.all_to_all(partial, "rep", 0, 0, tiled=True)
    own = jnp.sum(parts.astype(jnp.float32), axis=0).astype(jnp.bfloat16)
    same = lax.all_to_all(
        jnp.broadcast_to(own[None], (CHIPS,) + own.shape), "col", 0, 0, axis_index_groups=SAME_CORE
    )
    other = lax.ppermute(same, "col", CORES)
    partial = call(
        cube_kernel,
        shaped(WIN, GROUPS, BS, BS),
        (where,),
        (own, same, other, cubes),
        None,
        WIN * 2 * BS * (INNER + BS) * GROUPS * BS,
    )
    parts = lax.all_to_all(partial, "rep", 0, 0, tiled=True)
    parts = parts.reshape((REPS, WIN // REPS) + parts.shape[1:]).astype(jnp.float32)
    return jnp.sum(parts, axis=0).astype(jnp.bfloat16)[:, :, None]


def solution(mesh):
    in_specs = (
        P("row", "col", None, None),
        P("row", "col"),
        P("row", "col", None),
        P("row", "col", None),
    )
    out_specs = P(("row", "rep"), "col", None, None, None)
    return jax.shard_map(
        on_device, mesh=mesh, in_specs=in_specs, out_specs=out_specs, check_vma=False
    )
```

time: 219 us -> 200 us (0.913)
  waiting for transfers between devices: 49.9 us -> 31.1 us
  blocking collectives: 24.6 us -> 39 us
  starting transfers between devices: 73.8 us -> 64.6 us
  local copies, waits for them, and re-layouts: 41.4 us -> 32.5 us
  Pallas kernels: 11.4 us -> 13.7 us
    all_to_all x1 -> x0, waiting for transfers between devices: 24.2 us -> none  [on_device(): lax.all_to_all(jnp.broadcast_to(own[None], (COLS,) + own.shape), 'col', 0...]
    all_to_all x1 -> x0, starting transfers between devices: 14.5 us -> none  [on_device(): lax.all_to_all(jnp.broadcast_to(own[None], (COLS,) + own.shape), 'col', 0...]
    all_to_all x0 -> x1, blocking collectives: none -> 13.7 us  [on_device(): lax.all_to_all(jnp.broadcast_to(own[None], (CHIPS,) + own.shape), 'col',...]
    ppermute x16 -> x18, waiting for transfers between devices: 25.6 us -> 31.1 us  [the longest x8 18.9 us: over_odd(): return lax.ppermute(value, 'row', ODD)]
    unnamed x74 -> x37, local copies, waits for them, and re-layouts: 23.3 us -> 17.9 us
    ppermute x16 -> x18, starting transfers between devices: 59.3 us -> 64.6 us  [the longest x8 30.1 us: over_odd(): return lax.ppermute(value, 'row', ODD)]
    slice x4 -> x2, local copies, waits for them, and re-layouts: 4.45 us -> 0.03 us  [the longest x1 0.02 us: on_device(): high = over_odd(evens[-1][HALF - 1:])]
    squeeze x15, local copies, waits for them, and re-layouts: 1.38 us -> 4.98 us  [columns_of(): return jnp.concatenate([m[BR, 0, :MARKS] for m in marks]).astype(jnp.int32)]
  transfers between devices with their start and end apart: 18 -> 19, of which waited for: 9 -> 7; matrix products, arithmetic and copies ran while one was open for 8% -> 8% of each run, Pallas kernels for 0% -> 3%
where the time goes in v2:
time: 200 us; the launch traced here: 198 us
  starting transfers between devices  64.6 us (32%)
  blocking collectives  39 us (20%)
  local copies, waits for them, and re-layouts  32.5 us (16%)
  waiting for transfers between devices  31.1 us (16%)
  between operations  13.9 us (7%)
  Pallas kernels  13.7 us (7%)
  other arithmetic  3.5 us (2%)
    ppermute x8, starting transfers between devices, over_odd(): return lax.ppermute(value, 'row', ODD)  30.1 us
    all_to_all x2, blocking collectives, on_device(): parts = lax.all_to_all(partial, 'rep', 0, 0, tiled=True)  25.3 us
    ppermute x8, starting transfers between devices, over_even(): return lax.ppermute(value, 'row', EVEN)  19.5 us
    ppermute x8, waiting for transfers between devices, over_odd(): return lax.ppermute(value, 'row', ODD)  18.9 us
    unnamed x37, local copies, waits for them, and re-layouts  17.9 us
    all_to_all x1, blocking collectives, on_device(): lax.all_to_all(jnp.broadcast_to(own[None], (CHIPS,) + own.shape), 'col',...  13.7 us
    pallas_call x4, Pallas kernels, call(): pl.pallas_call(kernel, out_shape=out, in_specs=[SMEM] * len(scalars) + [V...  13.7 us
    ppermute x1, starting transfers between devices, on_device(): other = lax.ppermute(same, 'col', CORES)  11.9 us
  transfers between devices with their start and end apart: 19, of which 7 were waited for; matrix products, arithmetic and copies ran while one was open for 8% of the time, Pallas kernels for 3%

profile of v2, /device:TPU:1, one launch (start us, length us, event | category | flops | bytes accessed | tf_op | source)
XLA Modules:
  0.0 198.3 jit_solution(13034816291618687968)
XLA Ops:
  7.3 1.1 dynamic-slice_bitcast_fusion.2
  8.4 4.4 %collective-permute-start.1 = (bf16[49,32,128]{2,1,0:T(8,128)(2,1)S(1)}, bf16[49,32,128]{2,1,0:T(8,128)(2,1)S(1)}, u32[]{:S(2)}, u32[]{:S(2)}) collective-permute-start(bf16[49,32,128]{2,1,0:T(8,128)(2,1)S(1)} %fusion.3.refs_0_), channel_id=1, source_target_pairs={{0,32},{32,0},{64,96},{96,64},{128,160},{160,128},{192,224},{224,1... | collective-permute-start | bytes 1204232 | tf_op jit(solution)/shard_map/ppermute | solution.py:33
  12.8 10.2 %collective-permute-start.8 = (bf16[49,32,128]{2,1,0:T(8,128)(2,1)S(1)}, bf16[49,32,128]{2,1,0:T(8,128)(2,1)S(1)}, u32[]{:S(2)}, u32[]{:S(2)}) collective-permute-start(bf16[49,32,128]{2,1,0:T(8,128)(2,1)S(1)} %fusion.3.refs_0_), channel_id=1, source_target_pairs={{0,480},{32,64},{64,32},{96,128},{128,96},{160,192},{192,160},{224... | collective-permute-start | bytes 1204232 | tf_op jit(solution)/shard_map/ppermute | solution.py:37
  23.0 1.1 slice.74
  25.9 3.1 %collective-permute-start = (bf16[1040,64]{0,1:T(8,128)(2,1)S(1)}, bf16[1040,64]{0,1:T(8,128)(2,1)S(1)}, u32[]{:S(2)}, u32[]{:S(2)}) collective-permute-start(bf16[1040,64]{0,1:T(8,128)(2,1)S(1)} %get-tuple-element.14), channel_id=1, source_target_pairs={{0,4},{4,0},{8,12},{12,8},{16,20},{20,16},{24,28},{28,24},{1,5},{5... | collective-permute-start | bytes 399368 | tf_op jit(solution)/shard_map/ppermute | solution.py:195
  30.1 0.9 copy.54
  31.0 1.9 collective-permute-start.2
  32.9 1.9 collective-permute-start.9
  34.9 9.7 %collective-permute-done.2.refs_8_ = bf16[49,32,128]{2,1,0:T(8,128)(2,1)S(1)} collective-permute-done((bf16[49,32,128]{2,1,0:T(8,128)(2,1)S(1)}, bf16[49,32,128]{2,1,0:T(8,128)(2,1)S(1)}, u32[]{:S(2)}, u32[]{:S(2)}) %collective-permute-start.2) | collective-permute-done | bytes 401440 | tf_op jit(solution)/shard_map/ppermute | solution.py:37
  44.6 1.9 collective-permute-start.3
  46.5 3.0 %collective-permute-start.10 = (bf16[49,32,128]{2,1,0:T(8,128)(2,1)S(1)}, bf16[49,32,128]{2,1,0:T(8,128)(2,1)S(1)}, u32[]{:S(2)}, u32[]{:S(2)}) collective-permute-start(bf16[49,32,128]{2,1,0:T(8,128)(2,1)S(1)} %collective-permute-done.9.refs_2_), channel_id=1, source_target_pairs={{0,480},{32,64},{64,32},{96,128},{128,96},{160,192},{192,160},{224... | collective-permute-start | bytes 1204232 | tf_op jit(solution)/shard_map/ppermute | solution.py:37
  50.4 5.8 %collective-permute-done.3.refs_3_ = bf16[49,32,128]{2,1,0:T(8,128)(2,1)S(1)} collective-permute-done((bf16[49,32,128]{2,1,0:T(8,128)(2,1)S(1)}, bf16[49,32,128]{2,1,0:T(8,128)(2,1)S(1)}, u32[]{:S(2)}, u32[]{:S(2)}) %collective-permute-start.3) | collective-permute-done | bytes 401440 | tf_op jit(solution)/shard_map/ppermute | solution.py:33
  56.2 1.9 collective-permute-start.4
  58.1 1.1 collective-permute-done.10.refs_9_
  59.2 2.0 collective-permute-start.11
  63.9 4.3 %collective-permute-done.4.refs_10_ = bf16[49,32,128]{2,1,0:T(8,128)(2,1)} collective-permute-done((bf16[49,32,128]{2,1,0:T(8,128)(2,1)S(1)}, bf16[49,32,128]{2,1,0:T(8,128)(2,1)}, u32[]{:S(2)}, u32[]{:S(2)}) %collective-permute-start.4) | collective-permute-done | bytes 401440 | tf_op jit(solution)/shard_map/ppermute | solution.py:37
  68.2 1.9 collective-permute-start.5
  70.1 3.0 %collective-permute-start.12 = (bf16[49,32,128]{2,1,0:T(8,128)(2,1)S(1)}, bf16[49,32,128]{2,1,0:T(8,128)(2,1)}, u32[]{:S(2)}, u32[]{:S(2)}) collective-permute-start(bf16[49,32,128]{2,1,0:T(8,128)(2,1)S(1)} %collective-permute-done.11.refs_4_), channel_id=1, source_target_pairs={{0,480},{32,64},{64,32},{96,128},{128,96},{160,192},{192,160},{224... | collective-permute-start | bytes 1204232 | tf_op jit(solution)/shard_map/ppermute | solution.py:37
  73.1 1.2 slice_bitcast_fusion.2
  75.6 0.8 fusion.6
  76.6 0.8 copy.60
  77.4 1.0 reshape.140.mid_cols
  78.8 3.5 %collective-permute-start.6 = (bf16[49,32,128]{2,1,0:T(8,128)(2,1)S(1)}, bf16[49,32,128]{2,1,0:T(8,128)(2,1)}, u32[]{:S(2)}, u32[]{:S(2)}) collective-permute-start(bf16[49,32,128]{2,1,0:T(8,128)(2,1)S(1)} %collective-permute-done.5.refs_5_), channel_id=1, source_target_pairs={{0,480},{32,64},{64,32},{96,128},{128,96},{160,192},{192,160},{224... | collective-permute-start | bytes 1204232 | tf_op jit(solution)/shard_map/ppermute | solution.py:37
  82.3 2.2 %collective-permute-start.13 = (bf16[49,32,128]{2,1,0:T(8,128)(2,1)}, bf16[49,32,128]{2,1,0:T(8,128)(2,1)}, u32[]{:S(2)}, u32[]{:S(2)}) collective-permute-start(bf16[49,32,128]{2,1,0:T(8,128)(2,1)} %collective-permute-done.12.refs_11_), channel_id=1, source_target_pairs={{0,32},{32,0},{64,96},{96,64},{128,160},{160,128},{192,224},{224,1... | collective-permute-start | bytes 1204232 | tf_op jit(solution)/shard_map/ppermute | solution.py:33
  85.9 5.9 %collective-permute-done.13.refs_6_ = bf16[49,32,128]{2,1,0:T(8,128)(2,1)} collective-permute-done((bf16[49,32,128]{2,1,0:T(8,128)(2,1)}, bf16[49,32,128]{2,1,0:T(8,128)(2,1)}, u32[]{:S(2)}, u32[]{:S(2)}) %collective-permute-start.13) | collective-permute-done | bytes 401440 | tf_op jit(solution)/shard_map/ppermute | solution.py:33
  91.8 2.7 %collective-permute-start.14 = (bf16[49,32,128]{2,1,0:T(8,128)(2,1)}, bf16[49,32,128]{2,1,0:T(8,128)(2,1)S(1)}, u32[]{:S(2)}, u32[]{:S(2)}) collective-permute-start(bf16[49,32,128]{2,1,0:T(8,128)(2,1)} %collective-permute-done.13.refs_6_), channel_id=1, source_target_pairs={{0,480},{32,64},{64,32},{96,128},{128,96},{160,192},{192,160},{224... | collective-permute-start | bytes 1204232 | tf_op jit(solution)/shard_map/ppermute | solution.py:37
  94.5 1.9 collective-permute-start.7
  97.8 2.8 %concatenate.61 = bf16[624]{0:T(1024)(128)(2,1)S(1)} concatenate(bf16[48]{0:T(256)(128)(2,1)S(1)} %convert_element_type.54, bf16[48]{0:T(256)(128)(2,1)S(1)} %slice_bitcast_fusion.11, bf16[48]{0:T(256)(128)(2,1)S(1)} %slice_bitcast_fusion.10, bf16[48]{0:T(256)(128)(2,1)} %slice_bitcast_fusion.9, bf16[48]{0:T(256)(128)(2,1)} %slice_bitcast_fusion.8, ...), dimensions={0} | concatenate | bytes 2496 | tf_op jit(solution)/shard_map/concatenate | solution.py:176
  100.6 1.0 copy-done.6
  101.6 1.0 copy-done.8
  102.6 1.0 copy-done.10
  103.6 1.0 copy-done.12
  104.6 1.0 copy-done.14
  105.5 5.6 %shard_map.46 = (bf16[8,512,512]{2,1,0:T(8,128)(2,1)S(1)}, bf16[8,1152,256]{2,1,0:T(8,128)(2,1)S(1)}) custom-call(s32[4]{0:T(128)S(1)} %pad_add_fusion.where, s32[128]{0:T(128)S(1)} %reshape.137.left_cols, s32[256]{0:T(256)S(1)} %reshape.140.mid_cols, s32[624]{0:T(1024)S(1)} %convert_element_type.55.cols, s32[32]{0:T(128)S(1)} %reshape.138.keep, ...), custom_call_target="tpu_custom_call" | custom-call | bytes 5218304 | tf_op jit(solution)/shard_map/pallas_call | solution.py:160
  111.2 2.1 %copy-done = bf16[8,1152,256]{2,1,0:T(8,128)(2,1)} copy-done((bf16[8,1152,256]{2,1,0:T(8,128)(2,1)}, bf16[8,1152,256]{2,1,0:T(8,128)(2,1)S(1)}, u32[]{:S(2)}) %copy-start) | copy-done | bytes 4718616
  113.3 3.4 %collective-permute-start.15 = (bf16[25,32,128]{2,1,0:T(8,128)(2,1)S(1)}, bf16[25,32,128]{2,1,0:T(8,128)(2,1)S(1)}, u32[]{:S(2)}, u32[]{:S(2)}) collective-permute-start(bf16[25,32,128]{2,1,0:T(8,128)(2,1)S(1)} %slice.101), channel_id=1, source_target_pairs={{0,32},{32,0},{64,96},{96,64},{128,160},{160,128},{192,224},{224,1... | collective-permute-start | bytes 614408 | tf_op jit(solution)/shard_map/ppermute | solution.py:33
  116.7 3.8 %collective-permute-start.16 = (bf16[25,32,128]{2,1,0:T(8,128)(2,1)S(1)}, bf16[25,32,128]{2,1,0:T(8,128)(2,1)S(1)}, u32[]{:S(2)}, u32[]{:S(2)}) collective-permute-start(bf16[25,32,128]{2,1,0:T(8,128)(2,1)S(1)} %slice.103), channel_id=1, source_target_pairs={{0,480},{32,64},{64,32},{96,128},{128,96},{160,192},{192,160},{224... | collective-permute-start | bytes 614408 | tf_op jit(solution)/shard_map/ppermute | solution.py:37
  120.7 3.8 %collective-permute-done.16.high = bf16[25,32,128]{2,1,0:T(8,128)(2,1)S(1)} collective-permute-done((bf16[25,32,128]{2,1,0:T(8,128)(2,1)S(1)}, bf16[25,32,128]{2,1,0:T(8,128)(2,1)S(1)}, u32[]{:S(2)}, u32[]{:S(2)}) %collective-permute-start.16) | collective-permute-done | bytes 204832 | tf_op jit(solution)/shard_map/ppermute | solution.py:37
  124.5 3.9 %shard_map.47 = (bf16[4,8,128,128]{3,2,1,0:T(8,128)(2,1)S(1)}, bf16[8,512,512]{2,1,0:T(8,128)(2,1)S(1)}) custom-call(s32[4]{0:T(128)S(1)} %pad_add_fusion.where, s32[128]{0:T(128)S(1)} %reshape.137.left_cols, s32[144]{0:T(256)S(1)} %maximum_convert_fusion.cols, s32[32]{0:T(128)S(1)} %reshape.138.keep, ...), custom_call_target="tpu_custom_call", output_to_operand_aliasing={{1}: (9, {})} | custom-call | flops 536870912 | bytes 6471680 | tf_op jit(solution)/shard_map/pallas_call | solution.py:160
  128.4 13.6 %all_to_all.15 = bf16[4,8,128,128]{3,2,1,0:T(8,128)(2,1)S(1)} all-to-all(bf16[4,8,128,128]{3,2,1,0:T(8,128)(2,1)S(1)} %get-tuple-element.9), channel_id=1, replica_groups=mesh['row'=16,'col'=8,'rep'=4] {'rep'}, dimensions={0} | all-to-all | bytes 2097152 | tf_op jit(solution)/shard_map/all_to_all | solution.py:235
  142.4 13.7 %all_to_all.16.same = bf16[4,8,128,128]{3,2,1,0:T(8,128)(2,1)S(1)} all-to-all(bf16[4,8,128,128]{3,2,1,0:T(8,128)(2,1)S(1)} %broadcast_in_dim.4), channel_id=1, replica_groups={{0,8,16,24},{4,12,20,28},{1,9,17,25},{5,13,21,29},{2,10,18,26},{6,14,22..., dimensions={0} | all-to-all | bytes 2097152 | tf_op jit(solution)/shard_map/all_to_all | solution.py:237
  156.1 11.9 %collective-permute-start.17 = (bf16[4,8,128,128]{3,2,1,0:T(8,128)(2,1)S(1)}, bf16[4,8,128,128]{3,2,1,0:T(8,128)(2,1)S(1)}, u32[]{:S(2)}, u32[]{:S(2)}) collective-permute-start(bf16[4,8,128,128]{3,2,1,0:T(8,128)(2,1)S(1)} %all_to_all.16.same), channel_id=1, source_target_pairs={{0,4},{4,0},{8,12},{12,8},{16,20},{20,16},{24,28},{28,24},{1,5},{5... | collective-permute-start | bytes 3145736 | tf_op jit(solution)/shard_map/ppermute | solution.py:240
  168.0 2.3 %copy-done.1 = bf16[8,1152,256]{2,1,0:T(8,128)(2,1)S(1)} copy-done((bf16[8,1152,256]{2,1,0:T(8,128)(2,1)S(1)}, bf16[8,1152,256]{2,1,0:T(8,128)(2,1)}, u32[]{:S(2)}) %copy-start.1) | copy-done | bytes 4718616
  170.3 1.1 shard_map.48.right
  171.4 2.1 %copy-done.2 = bf16[8,1152,256]{2,1,0:T(8,128)(2,1)} copy-done((bf16[8,1152,256]{2,1,0:T(8,128)(2,1)}, bf16[8,1152,256]{2,1,0:T(8,128)(2,1)S(1)}, u32[]{:S(2)}) %copy-start.2) | copy-done | bytes 4718616
  173.6 2.3 %copy-done.3 = bf16[8,1152,256]{2,1,0:T(8,128)(2,1)S(1)} copy-done((bf16[8,1152,256]{2,1,0:T(8,128)(2,1)S(1)}, bf16[8,1152,256]{2,1,0:T(8,128)(2,1)}, u32[]{:S(2)}) %copy-start.3) | copy-done | bytes 4718616
  175.9 3.1 %shard_map.49 = bf16[8,2,128,128]{3,2,1,0:T(8,128)(2,1)S(1)} custom-call(s32[4]{0:T(128)S(1)} %pad_add_fusion.where, bf16[8,128,128]{2,1,0:T(8,128)(2,1)S(1)} %reduce_sum.24.own, bf16[4,8,128,128]{3,2,1,0:T(8,128)(2,1)S(1)} %all_to_all.16.same, bf16[4,8,128,128]{3,2,1,0:T(8,128)(2,1)S(1)} %collective-permute-done.17.other, bf16[8,1152,256]{2,1,0:T(8,128)(2,1)S(1)} %copy-done.3), custom_call_target="tpu_custom_call" | custom-call | flops 603979776 | bytes 7077888 | tf_op jit(solution)/shard_map/pallas_call | solution.py:160
  179.0 11.7 %all_to_all.17 = bf16[8,2,128,128]{3,2,1,0:T(8,128)(2,1)S(1)} all-to-all(bf16[8,2,128,128]{3,2,1,0:T(8,128)(2,1)S(1)} %shard_map.49), channel_id=1, replica_groups=mesh['row'=16,'col'=8,'rep'=4] {'rep'}, dimensions={0} | all-to-all | bytes 1048576 | tf_op jit(solution)/shard_map/all_to_all | solution.py:249
  (89 shorter events, 13.1 us)
Async XLA Ops:
  6.5 18.7 %copy-start.15 = (s32[8,2,2]{0,2,1:T(2,128)S(1)}, s32[8,2,2]{0,2,1:T(2,128)}, u32[]{:S(2)}) copy-start(s32[8,2,2]{0,2,1:T(2,128)} %param.6) | copy-start | bytes 388
  6.5 22.8 %copy-start.16 = (s32[8,2,1]{0,2,1:T(1,128)S(1)}, s32[8,2,1]{0,2,1:T(1,128)}, u32[]{:S(2)}) copy-start(s32[8,2,1]{0,2,1:T(1,128)} %param.7) | copy-start | bytes 196
  6.5 69.0 %all-gather.2.cloned.1.call-start = ((), (), s32[]{:S(2)}) async-start(), calls=%async_computation.3 | async-start | bytes 1331200 | tf_op jit(solution)/shard_map/all_gather | solution.py:201
  8.4 22.6 %collective-permute-start.1 = (bf16[49,32,128]{2,1,0:T(8,128)(2,1)S(1)}, bf16[49,32,128]{2,1,0:T(8,128)(2,1)S(1)}, u32[]{:S(2)}, u32[]{:S(2)}) collective-permute-start(bf16[49,32,128]{2,1,0:T(8,128)(2,1)S(1)} %fusion.3.refs_0_), channel_id=1, source_target_pairs={{0,32},{32,0},{64,96},{96,64},{128,160},{160,128},{192,224},{224,1... | collective-permute-start | bytes 1204232 | tf_op jit(solution)/shard_map/ppermute | solution.py:33
  12.8 20.1 %collective-permute-start.8 = (bf16[49,32,128]{2,1,0:T(8,128)(2,1)S(1)}, bf16[49,32,128]{2,1,0:T(8,128)(2,1)S(1)}, u32[]{:S(2)}, u32[]{:S(2)}) collective-permute-start(bf16[49,32,128]{2,1,0:T(8,128)(2,1)S(1)} %fusion.3.refs_0_), channel_id=1, source_target_pairs={{0,480},{32,64},{64,32},{96,128},{128,96},{160,192},{192,160},{224... | collective-permute-start | bytes 1204232 | tf_op jit(solution)/shard_map/ppermute | solution.py:37
  25.9 4.1 %collective-permute-start = (bf16[1040,64]{0,1:T(8,128)(2,1)S(1)}, bf16[1040,64]{0,1:T(8,128)(2,1)S(1)}, u32[]{:S(2)}, u32[]{:S(2)}) collective-permute-start(bf16[1040,64]{0,1:T(8,128)(2,1)S(1)} %get-tuple-element.14), channel_id=1, source_target_pairs={{0,4},{4,0},{8,12},{12,8},{16,20},{20,16},{24,28},{28,24},{1,5},{5... | collective-permute-start | bytes 399368 | tf_op jit(solution)/shard_map/ppermute | solution.py:195
  31.0 13.6 %collective-permute-start.2 = (bf16[49,32,128]{2,1,0:T(8,128)(2,1)S(1)}, bf16[49,32,128]{2,1,0:T(8,128)(2,1)S(1)}, u32[]{:S(2)}, u32[]{:S(2)}) collective-permute-start(bf16[49,32,128]{2,1,0:T(8,128)(2,1)S(1)} %collective-permute-done.1.refs_1_), channel_id=1, source_target_pairs={{0,480},{32,64},{64,32},{96,128},{128,96},{160,192},{192,160},{224... | collective-permute-start | bytes 1204232 | tf_op jit(solution)/shard_map/ppermute | solution.py:37
  32.9 13.6 %collective-permute-start.9 = (bf16[49,32,128]{2,1,0:T(8,128)(2,1)S(1)}, bf16[49,32,128]{2,1,0:T(8,128)(2,1)S(1)}, u32[]{:S(2)}, u32[]{:S(2)}) collective-permute-start(bf16[49,32,128]{2,1,0:T(8,128)(2,1)S(1)} %collective-permute-done.8.refs_7_), channel_id=1, source_target_pairs={{0,32},{32,0},{64,96},{96,64},{128,160},{160,128},{192,224},{224,1... | collective-permute-start | bytes 1204232 | tf_op jit(solution)/shard_map/ppermute | solution.py:33
  44.6 11.6 %collective-permute-start.3 = (bf16[49,32,128]{2,1,0:T(8,128)(2,1)S(1)}, bf16[49,32,128]{2,1,0:T(8,128)(2,1)S(1)}, u32[]{:S(2)}, u32[]{:S(2)}) collective-permute-start(bf16[49,32,128]{2,1,0:T(8,128)(2,1)S(1)} %collective-permute-done.2.refs_8_), channel_id=1, source_target_pairs={{0,32},{32,0},{64,96},{96,64},{128,160},{160,128},{192,224},{224,1... | collective-permute-start | bytes 1204232 | tf_op jit(solution)/shard_map/ppermute | solution.py:33
  46.5 12.7 %collective-permute-start.10 = (bf16[49,32,128]{2,1,0:T(8,128)(2,1)S(1)}, bf16[49,32,128]{2,1,0:T(8,128)(2,1)S(1)}, u32[]{:S(2)}, u32[]{:S(2)}) collective-permute-start(bf16[49,32,128]{2,1,0:T(8,128)(2,1)S(1)} %collective-permute-done.9.refs_2_), channel_id=1, source_target_pairs={{0,480},{32,64},{64,32},{96,128},{128,96},{160,192},{192,160},{224... | collective-permute-start | bytes 1204232 | tf_op jit(solution)/shard_map/ppermute | solution.py:37
  49.6 0.8 copy-start.5
  56.2 12.0 %collective-permute-start.4 = (bf16[49,32,128]{2,1,0:T(8,128)(2,1)S(1)}, bf16[49,32,128]{2,1,0:T(8,128)(2,1)}, u32[]{:S(2)}, u32[]{:S(2)}) collective-permute-start(bf16[49,32,128]{2,1,0:T(8,128)(2,1)S(1)} %collective-permute-done.3.refs_3_), channel_id=1, source_target_pairs={{0,480},{32,64},{64,32},{96,128},{128,96},{160,192},{192,160},{224... | collective-permute-start | bytes 1204232 | tf_op jit(solution)/shard_map/ppermute | solution.py:37
  59.2 10.8 %collective-permute-start.11 = (bf16[49,32,128]{2,1,0:T(8,128)(2,1)S(1)}, bf16[49,32,128]{2,1,0:T(8,128)(2,1)S(1)}, u32[]{:S(2)}, u32[]{:S(2)}) collective-permute-start(bf16[49,32,128]{2,1,0:T(8,128)(2,1)S(1)} %collective-permute-done.10.refs_9_), channel_id=1, source_target_pairs={{0,32},{32,0},{64,96},{96,64},{128,160},{160,128},{192,224},{224,1... | collective-permute-start | bytes 1204232 | tf_op jit(solution)/shard_map/ppermute | solution.py:33
  61.8 0.7 copy-start.9
  63.1 0.8 copy-start.7
  68.2 10.6 %collective-permute-start.5 = (bf16[49,32,128]{2,1,0:T(8,128)(2,1)}, bf16[49,32,128]{2,1,0:T(8,128)(2,1)S(1)}, u32[]{:S(2)}, u32[]{:S(2)}) collective-permute-start(bf16[49,32,128]{2,1,0:T(8,128)(2,1)} %collective-permute-done.4.refs_10_), channel_id=1, source_target_pairs={{0,32},{32,0},{64,96},{96,64},{128,160},{160,128},{192,224},{224,1... | collective-permute-start | bytes 1204232 | tf_op jit(solution)/shard_map/ppermute | solution.py:33
  70.1 12.2 %collective-permute-start.12 = (bf16[49,32,128]{2,1,0:T(8,128)(2,1)S(1)}, bf16[49,32,128]{2,1,0:T(8,128)(2,1)}, u32[]{:S(2)}, u32[]{:S(2)}) collective-permute-start(bf16[49,32,128]{2,1,0:T(8,128)(2,1)S(1)} %collective-permute-done.11.refs_4_), channel_id=1, source_target_pairs={{0,480},{32,64},{64,32},{96,128},{128,96},{160,192},{192,160},{224... | collective-permute-start | bytes 1204232 | tf_op jit(solution)/shard_map/ppermute | solution.py:37
  74.8 0.7 copy-start.11
  75.6 48.9 %copy-start.4 = (bf16[4,1040,128]{2,1,0:T(8,128)(2,1)S(1)}, bf16[4,1040,128]{2,1,0:T(8,128)(2,1)}, u32[]{:S(2)}) copy-start(bf16[4,1040,128]{2,1,0:T(8,128)(2,1)} %all-gather.2.cloned.1.call-done.lefts) | copy-start | bytes 3194884
  78.8 15.7 %collective-permute-start.6 = (bf16[49,32,128]{2,1,0:T(8,128)(2,1)S(1)}, bf16[49,32,128]{2,1,0:T(8,128)(2,1)}, u32[]{:S(2)}, u32[]{:S(2)}) collective-permute-start(bf16[49,32,128]{2,1,0:T(8,128)(2,1)S(1)} %collective-permute-done.5.refs_5_), channel_id=1, source_target_pairs={{0,480},{32,64},{64,32},{96,128},{128,96},{160,192},{192,160},{224... | collective-permute-start | bytes 1204232 | tf_op jit(solution)/shard_map/ppermute | solution.py:37
  82.3 9.5 %collective-permute-start.13 = (bf16[49,32,128]{2,1,0:T(8,128)(2,1)}, bf16[49,32,128]{2,1,0:T(8,128)(2,1)}, u32[]{:S(2)}, u32[]{:S(2)}) collective-permute-start(bf16[49,32,128]{2,1,0:T(8,128)(2,1)} %collective-permute-done.12.refs_11_), channel_id=1, source_target_pairs={{0,32},{32,0},{64,96},{96,64},{128,160},{160,128},{192,224},{224,1... | collective-permute-start | bytes 1204232 | tf_op jit(solution)/shard_map/ppermute | solution.py:33
  85.1 0.8 copy-start.13
  91.8 21.5 %collective-permute-start.14 = (bf16[49,32,128]{2,1,0:T(8,128)(2,1)}, bf16[49,32,128]{2,1,0:T(8,128)(2,1)S(1)}, u32[]{:S(2)}, u32[]{:S(2)}) collective-permute-start(bf16[49,32,128]{2,1,0:T(8,128)(2,1)} %collective-permute-done.13.refs_6_), channel_id=1, source_target_pairs={{0,480},{32,64},{64,32},{96,128},{128,96},{160,192},{192,160},{224... | collective-permute-start | bytes 1204232 | tf_op jit(solution)/shard_map/ppermute | solution.py:37
  94.5 22.2 %collective-permute-start.7 = (bf16[49,32,128]{2,1,0:T(8,128)(2,1)}, bf16[49,32,128]{2,1,0:T(8,128)(2,1)S(1)}, u32[]{:S(2)}, u32[]{:S(2)}) collective-permute-start(bf16[49,32,128]{2,1,0:T(8,128)(2,1)} %collective-permute-done.6.refs_12_), channel_id=1, source_target_pairs={{0,32},{32,0},{64,96},{96,64},{128,160},{160,128},{192,224},{224,1... | collective-permute-start | bytes 1204232 | tf_op jit(solution)/shard_map/ppermute | solution.py:33
  100.6 1.0 copy-start.6
  101.6 1.0 copy-start.8
  102.6 1.0 copy-start.10
  103.5 1.0 copy-start.12
  104.5 1.0 copy-start.14
  111.2 2.1 %copy-start = (bf16[8,1152,256]{2,1,0:T(8,128)(2,1)}, bf16[8,1152,256]{2,1,0:T(8,128)(2,1)S(1)}, u32[]{:S(2)}) copy-start(bf16[8,1152,256]{2,1,0:T(8,128)(2,1)S(1)} %get-tuple-element.10.given) | copy-start | bytes 14155780
  113.3 7.2 %collective-permute-start.15 = (bf16[25,32,128]{2,1,0:T(8,128)(2,1)S(1)}, bf16[25,32,128]{2,1,0:T(8,128)(2,1)S(1)}, u32[]{:S(2)}, u32[]{:S(2)}) collective-permute-start(bf16[25,32,128]{2,1,0:T(8,128)(2,1)S(1)} %slice.101), channel_id=1, source_target_pairs={{0,32},{32,0},{64,96},{96,64},{128,160},{160,128},{192,224},{224,1... | collective-permute-start | bytes 614408 | tf_op jit(solution)/shard_map/ppermute | solution.py:33
  116.7 7.7 %collective-permute-start.16 = (bf16[25,32,128]{2,1,0:T(8,128)(2,1)S(1)}, bf16[25,32,128]{2,1,0:T(8,128)(2,1)S(1)}, u32[]{:S(2)}, u32[]{:S(2)}) collective-permute-start(bf16[25,32,128]{2,1,0:T(8,128)(2,1)S(1)} %slice.103), channel_id=1, source_target_pairs={{0,480},{32,64},{64,32},{96,128},{128,96},{160,192},{192,160},{224... | collective-permute-start | bytes 614408 | tf_op jit(solution)/shard_map/ppermute | solution.py:37
  156.1 17.4 %collective-permute-start.17 = (bf16[4,8,128,128]{3,2,1,0:T(8,128)(2,1)S(1)}, bf16[4,8,128,128]{3,2,1,0:T(8,128)(2,1)S(1)}, u32[]{:S(2)}, u32[]{:S(2)}) collective-permute-start(bf16[4,8,128,128]{3,2,1,0:T(8,128)(2,1)S(1)} %all_to_all.16.same), channel_id=1, source_target_pairs={{0,4},{4,0},{8,12},{12,8},{16,20},{20,16},{24,28},{28,24},{1,5},{5... | collective-permute-start | bytes 3145736 | tf_op jit(solution)/shard_map/ppermute | solution.py:240
  168.0 2.3 %copy-start.1 = (bf16[8,1152,256]{2,1,0:T(8,128)(2,1)S(1)}, bf16[8,1152,256]{2,1,0:T(8,128)(2,1)}, u32[]{:S(2)}) copy-start(bf16[8,1152,256]{2,1,0:T(8,128)(2,1)} %copy-done) | copy-start | bytes 14155780
  171.4 2.1 %copy-start.2 = (bf16[8,1152,256]{2,1,0:T(8,128)(2,1)}, bf16[8,1152,256]{2,1,0:T(8,128)(2,1)S(1)}, u32[]{:S(2)}) copy-start(bf16[8,1152,256]{2,1,0:T(8,128)(2,1)S(1)} %shard_map.48.right) | copy-start | bytes 14155780
  173.6 2.3 %copy-start.3 = (bf16[8,1152,256]{2,1,0:T(8,128)(2,1)S(1)}, bf16[8,1152,256]{2,1,0:T(8,128)(2,1)}, u32[]{:S(2)}) copy-start(bf16[8,1152,256]{2,1,0:T(8,128)(2,1)} %copy-done.2) | copy-start | bytes 14155780
Sparse Core Ops, SparseCore 0:
  31.1 26.0 all-gather.1

commit v3 on v1

v3 whole, which is shorter than its diff:
```python
import jax
import jax.numpy as jnp
from jax import lax
from jax.experimental import pallas as pl
from jax.experimental.pallas import tpu as pltpu
from jax.sharding import PartitionSpec as P

ROWS = 16
COLS = 8
CHIPS = 4
REPS = 4
GROUPS = 2
WIN = 8
BR = 24
BS = 128
Q = BS // REPS
HALF = BR + 1
KEPT = 2
SLOTS = GROUPS * KEPT
MARKS = GROUPS * BR
INNER = ROWS * KEPT * Q

CORES = [(i, i ^ 1) for i in range(COLS)]
SAME_CORE = [[c + i for i in range(0, COLS, 2)] for c in range(2)]

SMEM = pl.BlockSpec(memory_space=pltpu.SMEM)
VMEM = pl.BlockSpec(memory_space=pltpu.VMEM)


def put(right, w, at, n, block, hit):
    at = at if isinstance(at, int) else pl.multiple_of(at, Q)
    right[w, pl.ds(at, Q), n * BS : (n + 1) * BS] = jnp.where(hit, block, jnp.zeros_like(block))


def square_kernel(left_cols, cols, keep, lefts, panels, out, right):
    lane = lax.broadcasted_iota(jnp.int32, (BS, BS), 1) // Q
    right[...] = jnp.zeros_like(right)

    def pair(p, _):
        rows = pl.ds(pl.multiple_of(p * BS, BS), BS)
        left = jnp.concatenate([lefts[c, rows, :] for c in range(COLS)], axis=1)
        for half in range(2):
            w = 2 * p + half
            for s in range(ROWS):
                k = left_cols[w * ROWS + s]
                at = (s // GROUPS) * BS + (half * GROUPS + s % GROUPS) * Q
                for g in range(GROUPS):
                    block = panels[s, g * HALF + k]
                    col = cols[s * MARKS + g * BR + k]
                    for m in range(KEPT):
                        slot = g * KEPT + m
                        put(right, half, at, slot, block, col == keep[w * SLOTS + slot])
            full = jnp.dot(left, right[half], preferred_element_type=jnp.float32)
            parts = [full[:, i * BS : (i + 1) * BS] for i in range(SLOTS)]
            for x in range(REPS):
                mixed = parts[x]
                for i in range(SLOTS):
                    if i != x:
                        moved = pltpu.roll(parts[i], (Q * (i - x)) % BS, 1)
                        mixed = jnp.where(lane == i, moved, mixed)
                out[x, w] = mixed.astype(jnp.bfloat16)
        return 0

    lax.fori_loop(0, WIN // 2, pair, 0)


def cube_kernel(where, mid_cols, cols, keep, cube_keep, own, same, other, panels, out, right):
    rep, core = where[0], where[1]
    wide = lax.broadcasted_iota(jnp.int32, (BS, BS), 1)
    tall = lax.broadcasted_iota(jnp.int32, (BS, BS), 0)
    place = wide == (rep * Q + tall % Q)

    def pair(p, _):
        for half in range(2):
            w = 2 * p + half
            for s in range(ROWS):
                for t in range(KEPT):
                    k = mid_cols[(w * ROWS + s) * KEPT + t]
                    for g in range(GROUPS):
                        hit = cols[s * MARKS + g * BR + k] == cube_keep[w * GROUPS + g]
                        put(right, half, (s * KEPT + t) * Q, g, panels[s, g * HALF + k], hit)
            for g in range(GROUPS):
                found = jnp.zeros((BS, BS), jnp.float32)
                for m in range(KEPT):
                    hit = keep[w * SLOTS + g * KEPT + m] == cube_keep[w * GROUPS + g]
                    found = jnp.where(tall // Q == g * KEPT + m, jnp.where(hit, -1.5, 0.0), found)
                found = jnp.where(place, found, 0.0).astype(jnp.bfloat16)
                right[half, INNER : INNER + BS, g * BS : (g + 1) * BS] = found
            total = jnp.dot(own[w], right[half, INNER:, :], preferred_element_type=jnp.float32)
            for y in range(CHIPS):
                for lefts, c in ((same, 2 * y + core), (other, 2 * y + 1 - core)):
                    rows = pl.ds(pl.multiple_of(c * BS, BS), BS)
                    total += jnp.dot(
                        lefts[y, w], right[half, rows, :], preferred_element_type=jnp.float32
                    )
            total = -2.0 * total
            for g in range(GROUPS):
                out[w, g] = total[:, g * BS : (g + 1) * BS].astype(jnp.bfloat16)
        return 0

    lax.fori_loop(0, WIN // 2, pair, 0)


def call(kernel, out, scalars, arrays, scratch, flops):
    moved = sum(a.size * 2 for a in arrays)
    return pl.pallas_call(
        kernel,
        out_shape=jax.ShapeDtypeStruct(out, jnp.bfloat16),
        in_specs=[SMEM] * len(scalars) + [VMEM] * len(arrays),
        out_specs=VMEM,
        scratch_shapes=[pltpu.VMEM(scratch, jnp.bfloat16)],
        cost_estimate=pl.CostEstimate(flops=flops, bytes_accessed=moved, transcendentals=0),
        compiler_params=pltpu.CompilerParams(vmem_limit_bytes=8 * 2**20),
    )(*scalars, *arrays)


def on_device(p_vals, p_cols, square_cols, cube_cols):
    rep = lax.axis_index("rep")
    core = lax.axis_index("col") % 2
    where = jnp.stack([rep, core]).astype(jnp.int32)

    left = lax.dynamic_slice_in_dim(p_vals[:WIN], rep * Q, Q, 3)
    left = left.reshape(WIN // 2, 2, GROUPS, BS, Q).transpose(0, 3, 1, 2, 4)
    left = left.reshape(WIN // 2 * BS, BS)
    notes = jnp.concatenate([p_cols[:WIN].reshape(-1), square_cols.reshape(-1)])
    notes = jnp.pad(notes.astype(jnp.bfloat16)[None], ((0, 15), (0, BS - notes.shape[0])))
    lefts = lax.all_gather(jnp.concatenate([left, notes], axis=0), "col")
    notes = lefts[:, WIN // 2 * BS, :].astype(jnp.int32)
    left_cols = notes[:, : WIN * GROUPS].reshape(COLS, WIN, GROUPS).transpose(1, 0, 2).reshape(-1)
    mid_cols = notes[:, WIN * GROUPS : WIN * GROUPS * (1 + KEPT)]
    mid_cols = mid_cols.reshape(COLS, WIN, GROUPS, KEPT).transpose(1, 0, 2, 3).reshape(-1)

    mine = lax.dynamic_slice_in_dim(p_vals, rep * Q, Q, 2)
    peak = jnp.max(jnp.abs(mine)).astype(jnp.float32)
    power = jnp.clip(13.0 - jnp.floor(jnp.log2(jnp.maximum(peak, 1e-37))), 0.0, 110.0)
    mine = (mine.astype(jnp.float32) * jnp.exp2(power)).astype(jnp.float16)
    marks = jnp.concatenate([p_cols.T.reshape(-1).astype(jnp.float32), power[None]])
    marks = marks.astype(jnp.float16)[None, None]
    marks = jnp.pad(marks, ((0, 0), (0, Q - 1), (0, BS - MARKS - 1)))
    panels = lax.all_gather(jnp.concatenate([mine[:, 0], marks, mine[:, 1]], axis=0), "row")
    marks = panels[:, BR, 0, : MARKS + 1].astype(jnp.float32)
    cols = marks[:, :MARKS].astype(jnp.int32).reshape(-1)
    back = jnp.exp2(-marks[:, MARKS])[:, None, None, None]
    panels = (panels.astype(jnp.float32) * back).astype(jnp.bfloat16)

    keep = square_cols.reshape(-1)
    partial = call(
        square_kernel,
        (REPS, WIN, BS, BS),
        (left_cols, cols, keep),
        (lefts, panels),
        (2, COLS * BS, SLOTS * BS),
        WIN * 2 * BS * COLS * BS * SLOTS * BS,
    )
    parts = lax.all_to_all(partial, "rep", 0, 0, tiled=True)
    own = jnp.sum(parts.astype(jnp.float32), axis=0).astype(jnp.bfloat16)
    same = lax.all_to_all(
        jnp.broadcast_to(own[None], (CHIPS,) + own.shape), "col", 0, 0, axis_index_groups=SAME_CORE
    )
    other = lax.ppermute(same, "col", CORES)
    partial = call(
        cube_kernel,
        (WIN, GROUPS, BS, BS),
        (where, mid_cols, cols, keep, cube_cols.reshape(-1)),
        (own, same, other, panels),
        (2, INNER + BS, GROUPS * BS),
        WIN * 2 * BS * (INNER + BS) * GROUPS * BS,
    )
    parts = lax.all_to_all(partial, "rep", 0, 0, tiled=True)
    parts = parts.reshape((REPS, WIN // REPS) + parts.shape[1:]).astype(jnp.float32)
    return jnp.sum(parts, axis=0).astype(jnp.bfloat16)[:, :, None]


def solution(mesh):
    in_specs = (
        P("row", "col", None, None),
        P("row", "col"),
        P("row", "col", None),
        P("row", "col", None),
    )
    out_specs = P(("row", "rep"), "col", None, None, None)
    return jax.shard_map(
        on_device, mesh=mesh, in_specs=in_specs, out_specs=out_specs, check_vma=False
    )
```

time: 219 us -> 181 us (0.83)
  blocking collectives: 24.6 us -> 121 us
  starting transfers between devices: 73.8 us -> 10.4 us
  waiting for transfers between devices: 49.9 us -> 1.54 us
  local copies, waits for them, and re-layouts: 41.4 us -> 11.3 us
  other arithmetic: 2.64 us -> 14.1 us
  Pallas kernels: 11.4 us -> 7.76 us
    all_gather x0 -> x1, blocking collectives: none -> 81.8 us  [on_device(): lax.all_gather(jnp.concatenate([mine[:, 0], marks, mine[:, 1]], axis=0),...]
    ppermute x16 -> x1, starting transfers between devices: 59.3 us -> 10.4 us  [on_device(): other = lax.ppermute(same, 'col', CORES)]
    all_to_all x1 -> x0, waiting for transfers between devices: 24.2 us -> none  [on_device(): lax.all_to_all(jnp.broadcast_to(own[None], (COLS,) + own.shape), 'col', 0...]
    ppermute x16 -> x1, waiting for transfers between devices: 25.6 us -> 1.53 us  [on_device(): other = lax.ppermute(same, 'col', CORES)]
    unnamed x74 -> x13, local copies, waits for them, and re-layouts: 23.3 us -> 7.08 us
    all_to_all x1 -> x0, starting transfers between devices: 14.5 us -> none  [on_device(): lax.all_to_all(jnp.broadcast_to(own[None], (COLS,) + own.shape), 'col', 0...]
    all_to_all x0 -> x1, blocking collectives: none -> 13.7 us  [on_device(): lax.all_to_all(jnp.broadcast_to(own[None], (CHIPS,) + own.shape), 'col',...]
    convert_element_type x2 -> x5, other arithmetic: 0.76 us -> 9.48 us  [the longest x1 6.83 us: on_device(): panels = (panels.astype(jnp.float32) * back).astype(jnp.bfloat16)]
  transfers between devices with their start and end apart: 18 -> 2, of which waited for: 9 -> 1; matrix products, arithmetic and copies ran while one was open for 8% -> 7% of each run, Pallas kernels for 0% -> 0%
where the time goes in v3:
time: 181 us; the launch traced here: 180 us
  blocking collectives  121 us (67%)
  between operations  14.3 us (8%)
  other arithmetic  14.1 us (8%)
  local copies, waits for them, and re-layouts  11.3 us (6%)
  starting transfers between devices  10.4 us (6%)
  Pallas kernels  7.76 us (4%)
    all_gather x1, blocking collectives, on_device(): lax.all_gather(jnp.concatenate([mine[:, 0], marks, mine[:, 1]], axis=0),...  81.8 us
    all_to_all x2, blocking collectives, on_device(): parts = lax.all_to_all(partial, 'rep', 0, 0, tiled=True)  25.2 us
    all_to_all x1, blocking collectives, on_device(): lax.all_to_all(jnp.broadcast_to(own[None], (CHIPS,) + own.shape), 'col',...  13.7 us
    ppermute x1, starting transfers between devices, on_device(): other = lax.ppermute(same, 'col', CORES)  10.4 us
    pallas_call x2, Pallas kernels, call(): pl.pallas_call(kernel, out_shape=jax.ShapeDtypeStruct(out, jnp.bfloat16),...  7.76 us
    unnamed x13, local copies, waits for them, and re-layouts  7.08 us
    convert_element_type x1, other arithmetic, on_device(): panels = (panels.astype(jnp.float32) * back).astype(jnp.bfloat16)  6.83 us
  transfers between devices with their start and end apart: 2, of which 1 were waited for; matrix products, arithmetic and copies ran while one was open for 7% of the time, Pallas kernels for 0%

profile of v3, /device:TPU:1, one launch (start us, length us, event | category | flops | bytes accessed | tf_op | source)
XLA Modules:
  0.0 180.0 jit_solution(15578111164322710830)
XLA Ops:
  6.5 0.8 fusion.11
  7.3 1.1 slice.31
  8.4 0.2 constant_dynamic-slice_fusion.1
  8.6 0.2 copy.27
  8.9 0.1 copy.28
  8.9 0.1 concatenate.36
  9.0 0.7 convert.23
  9.7 0.1 copy.29
  9.8 0.1 concatenate.37
  9.9 0.1 pad_maximum_fusion.1
  10.0 0.1 copy.30
  10.1 0.8 copy.31
  10.9 1.7 abs_reduce_fusion
  13.3 1.1 multiply_convert_fusion.1
  14.5 0.1 slice_bitcast_fusion.1
  14.6 0.1 concatenate.40
  14.6 0.1 fusion.7
  14.7 0.1 pad_maximum_fusion
  14.8 81.8 %all-gather.6 = f16[784,32,128]{2,1,0:T(8,128)(2,1)} all-gather(f16[49,32,128]{2,1,0:T(8,128)(2,1)S(1)} %pad_maximum_fusion), channel_id=3, replica_groups=mesh['row'=16,'col'=8,'rep'=4] {'row'}, dimensions={0}, use_global_device_ids=true | all-gather | bytes 6823936 | tf_op jit(solution)/shard_map/all_gather | solution.py:140
  96.6 0.1 copy.35
  96.7 0.8 slice_convert_fusion.1
  97.5 0.1 reshape.120.cols
  97.6 0.1 reshape.121.keep
  97.6 0.2 fusion.10
  97.8 6.8 %multiply_convert_fusion.panels = bf16[16,49,32,128]{3,2,1,0:T(8,128)(2,1)} fusion(f16[16,49,32,128]{3,2,1,0:T(8,128)(2,1)} %bitcast.39, f32[16]{0:T(128)S(1)} %fusion.10), kind=kLoop, calls=%fused_computation | loop fusion | flops 9633792 | bytes 12845120 | tf_op jit(solution)/shard_map/convert_element_type | solution.py:144
  104.7 0.7 slice_convert_fusion.2
  105.4 0.1 copy.37
  105.5 0.1 copy.38
  105.6 0.1 reshape.124.left_cols
  105.7 2.8 %copy-done = bf16[16,49,32,128]{3,2,1,0:T(8,128)(2,1)S(1)} copy-done((bf16[16,49,32,128]{3,2,1,0:T(8,128)(2,1)S(1)}, bf16[16,49,32,128]{3,2,1,0:T(8,128)(2,1)}, u32[]{:S(2)}) %copy-start) | copy-done | bytes 6422552
  108.6 1.2 copy-done.2
  109.8 3.8 %shard_map.46 = bf16[4,8,128,128]{3,2,1,0:T(8,128)(2,1)S(1)} custom-call(s32[128]{0:T(128)S(1)} %reshape.124.left_cols, s32[768]{0:T(1024)S(1)} %reshape.120.cols, s32[32]{0:T(128)S(1)} %reshape.121.keep, bf16[8,528,128]{2,1,0:T(8,128)(2,1)S(1)} %bitcast.37, bf16[16,49,32,128]{3,2,1,0:T(8,128)(2,1)S(1)} %copy-done), custom_call_target="tpu_custom_call" | custom-call | flops 1073741824 | bytes 7503872 | tf_op jit(solution)/shard_map/pallas_call | solution.py:106
  113.6 13.6 %all_to_all.15 = bf16[4,8,128,128]{3,2,1,0:T(8,128)(2,1)S(1)} all-to-all(bf16[4,8,128,128]{3,2,1,0:T(8,128)(2,1)S(1)} %shard_map.46), channel_id=1, replica_groups=mesh['row'=16,'col'=8,'rep'=4] {'rep'}, dimensions={0} | all-to-all | bytes 2097152 | tf_op jit(solution)/shard_map/all_to_all | solution.py:155
  127.1 0.2 reduce_sum.24.own
  127.3 0.2 broadcast_in_dim.4
  127.6 13.7 %all_to_all.16.same = bf16[4,8,128,128]{3,2,1,0:T(8,128)(2,1)S(1)} all-to-all(bf16[4,8,128,128]{3,2,1,0:T(8,128)(2,1)S(1)} %broadcast_in_dim.4), channel_id=1, replica_groups={{0,8,16,24},{4,12,20,28},{1,9,17,25},{5,13,21,29},{2,10,18,26},{6,14,22..., dimensions={0} | all-to-all | bytes 2097152 | tf_op jit(solution)/shard_map/all_to_all | solution.py:157
  141.3 10.4 %collective-permute-start = (bf16[4,8,128,128]{3,2,1,0:T(8,128)(2,1)S(1)}, bf16[4,8,128,128]{3,2,1,0:T(8,128)(2,1)S(1)}, u32[]{:S(2)}, u32[]{:S(2)}) collective-permute-start(bf16[4,8,128,128]{3,2,1,0:T(8,128)(2,1)S(1)} %all_to_all.16.same), channel_id=1, source_target_pairs={{0,4},{4,0},{8,12},{12,8},{16,20},{20,16},{24,28},{28,24},{1,5},{5... | collective-permute-start | bytes 3145736 | tf_op jit(solution)/shard_map/ppermute | solution.py:160
  151.8 0.1 copy.36
  151.9 0.1 reshape.122.cube_keep
  151.9 0.1 pad_add_fusion.where
  152.1 0.1 copy.32
  152.2 0.2 copy.33
  152.3 0.2 reshape.119.mid_cols
  152.5 1.5 collective-permute-done.other
  154.0 2.8 %copy-done.1 = bf16[16,49,32,128]{3,2,1,0:T(8,128)(2,1)S(1)} copy-done((bf16[16,49,32,128]{3,2,1,0:T(8,128)(2,1)S(1)}, bf16[16,49,32,128]{3,2,1,0:T(8,128)(2,1)}, u32[]{:S(2)}) %copy-start.1) | copy-done | bytes 6422552
  156.8 4.0 %shard_map.47 = bf16[8,2,128,128]{3,2,1,0:T(8,128)(2,1)S(1)} custom-call(s32[2]{0:T(128)S(1)} %pad_add_fusion.where, s32[256]{0:T(256)S(1)} %reshape.119.mid_cols, s32[768]{0:T(1024)S(1)} %reshape.120.cols, s32[32]{0:T(128)S(1)} %reshape.121.keep, s32[16]{0:T(128)S(1)} %reshape.122.cube_keep, bf16[8,128,128]{2,1,0:T(8,128)(2,1)S(1)} %reduce_sum.24.own, ...), custom_call_target="tpu_custom_call" | custom-call | flops 603979776 | bytes 8781824 | tf_op jit(solution)/shard_map/pallas_call | solution.py:106
  160.8 11.6 %all_to_all.17 = bf16[8,2,128,128]{3,2,1,0:T(8,128)(2,1)S(1)} all-to-all(bf16[8,2,128,128]{3,2,1,0:T(8,128)(2,1)S(1)} %shard_map.47), channel_id=1, replica_groups=mesh['row'=16,'col'=8,'rep'=4] {'rep'}, dimensions={0} | all-to-all | bytes 1048576 | tf_op jit(solution)/shard_map/all_to_all | solution.py:169
  172.5 0.7 reduce_sum.25
  (14 shorter events, 0.2 us)
Async XLA Ops:
  6.5 98.1 %all-gather.5.cloned.1.call-start = ((), (), s32[]{:S(2)}) async-start(), calls=%async_computation.3 | async-start | bytes 1216512 | tf_op jit(solution)/shard_map/all_gather | solution.py:127
  8.4 88.2 %copy-start.3 = (s32[8,2,2]{0,2,1:T(2,128)S(1)}, s32[8,2,2]{0,2,1:T(2,128)}, u32[]{:S(2)}) copy-start(s32[8,2,2]{0,2,1:T(2,128)} %param.6) | copy-start | bytes 388
  105.7 2.8 %copy-start = (bf16[16,49,32,128]{3,2,1,0:T(8,128)(2,1)S(1)}, bf16[16,49,32,128]{3,2,1,0:T(8,128)(2,1)}, u32[]{:S(2)}) copy-start(bf16[16,49,32,128]{3,2,1,0:T(8,128)(2,1)} %multiply_convert_fusion.panels) | copy-start | bytes 19267588
  108.6 1.2 copy-start.2
  109.8 42.0 %copy-start.4 = (s32[8,2,1]{0,2,1:T(1,128)S(1)}, s32[8,2,1]{0,2,1:T(1,128)}, u32[]{:S(2)}) copy-start(s32[8,2,1]{0,2,1:T(1,128)} %param.7) | copy-start | bytes 196
  141.3 12.7 %collective-permute-start = (bf16[4,8,128,128]{3,2,1,0:T(8,128)(2,1)S(1)}, bf16[4,8,128,128]{3,2,1,0:T(8,128)(2,1)S(1)}, u32[]{:S(2)}, u32[]{:S(2)}) collective-permute-start(bf16[4,8,128,128]{3,2,1,0:T(8,128)(2,1)S(1)} %all_to_all.16.same), channel_id=1, source_target_pairs={{0,4},{4,0},{8,12},{12,8},{16,20},{20,16},{24,28},{28,24},{1,5},{5... | collective-permute-start | bytes 3145736 | tf_op jit(solution)/shard_map/ppermute | solution.py:160
  154.0 2.8 %copy-start.1 = (bf16[16,49,32,128]{3,2,1,0:T(8,128)(2,1)S(1)}, bf16[16,49,32,128]{3,2,1,0:T(8,128)(2,1)}, u32[]{:S(2)}) copy-start(bf16[16,49,32,128]{3,2,1,0:T(8,128)(2,1)} %multiply_convert_fusion.panels) | copy-start | bytes 19267588
Sparse Core Ops, SparseCore 0:
  11.0 36.8 all-gather.4

commit v4 on v3

v4 whole, which is shorter than its diff:
```python
import jax
import jax.numpy as jnp
from jax import lax
from jax.experimental import pallas as pl
from jax.experimental.pallas import tpu as pltpu
from jax.sharding import PartitionSpec as P

ROWS = 16
COLS = 8
CHIPS = 4
REPS = 4
GROUPS = 2
WIN = 8
BR = 24
BS = 128
Q = BS // REPS
HALF = BR + 1
KEPT = 2
SLOTS = GROUPS * KEPT
MARKS = GROUPS * BR
ROOM = 48
INNER = ROWS * KEPT * Q

CORES = [(i, i ^ 1) for i in range(COLS)]
SAME_CORE = [[c + i for i in range(0, COLS, 2)] for c in range(2)]

SMEM = pl.BlockSpec(memory_space=pltpu.SMEM)
HBM = pl.BlockSpec(memory_space=pltpu.HBM)
VMEM = pl.BlockSpec(memory_space=pltpu.VMEM)


def put(right, w, at, n, block, hit):
    at = at if isinstance(at, int) else pl.multiple_of(at, Q)
    right[w, pl.ds(at, Q), n * BS : (n + 1) * BS] = jnp.where(hit, block, jnp.zeros_like(block))


def fetch(panels, held, sems):
    copies = [pltpu.make_async_copy(panels.at[s], held.at[s], sems.at[s]) for s in range(ROWS)]
    for copy in copies:
        copy.start()
    return copies


def prepare_kernel(where, p_cols, square_cols, p_vals, spread, panel, heads, shares, sems):
    rep = where[0]
    rows = pl.ds(pl.multiple_of(rep * Q, Q), Q)
    first = pltpu.make_async_copy(p_vals.at[:WIN], heads, sems.at[0])
    second = pltpu.make_async_copy(p_vals.at[:, :, rows, :], shares, sems.at[1])
    first.start()
    second.start()
    lane = lax.broadcasted_iota(jnp.int32, (2 * 8, BS), 1)
    notes = jnp.zeros((2 * 8, BS), jnp.float32)
    for i in range(WIN * GROUPS):
        notes = jnp.where(lane == i, p_cols[i].astype(jnp.float32), notes)
    for i in range(WIN * SLOTS):
        notes = jnp.where(lane == WIN * GROUPS + i, square_cols[i].astype(jnp.float32), notes)
    notes = notes.astype(jnp.bfloat16)
    marks = jnp.zeros((2 * 8, BS), jnp.float32)
    for g in range(GROUPS):
        for k in range(BR):
            marks = jnp.where(lane == g * BR + k, p_cols[k * GROUPS + g].astype(jnp.float32), marks)

    group = lax.broadcasted_iota(jnp.int32, (BS, BS), 1) // Q
    first.wait()
    for p in range(WIN // 2):
        tile = jnp.zeros((BS, BS), jnp.float32)
        for i in range(2 * GROUPS):
            part = heads[2 * p + i // GROUPS, i % GROUPS].astype(jnp.float32)
            moved = pltpu.roll(part, lax.rem((i - rep) * Q + BS, BS), 1)
            tile = jnp.where(group == i, moved, tile)
        tile = tile.astype(jnp.bfloat16)
        for c in range(COLS):
            spread[c, p * BS : (p + 1) * BS, :] = tile
    for c in range(COLS):
        spread[c, WIN // 2 * BS :, :] = notes

    second.wait()
    peak = jnp.zeros((Q, BS), jnp.float32)
    for k in range(BR):
        for g in range(GROUPS):
            block = shares[k, g]
            panel[g * HALF + k] = block
            peak = jnp.maximum(peak, jnp.abs(block.astype(jnp.float32)))
    peak = jnp.maximum(jnp.max(peak, axis=(0, 1), keepdims=True), 1e-37)
    power = jnp.clip(13.0 - jnp.floor(jnp.log2(peak)), 0.0, 110.0)
    marks = jnp.where(lane == MARKS, power, marks)
    panel[BR] = jnp.concatenate([marks, marks], axis=0).astype(jnp.bfloat16)


def square_kernel(left_cols, cols, keep, lefts, panels, out, held, left, right, sems):
    copies = fetch(panels, held, sems)
    lane = lax.broadcasted_iota(jnp.int32, (BS, BS), 1)

    def gather_left(p, _):
        rows = pl.ds(pl.multiple_of(p * BS, BS), BS)
        for c in range(0, COLS, 2):
            one, two = lefts[c, rows, :].astype(jnp.float32), lefts[c + 1, rows, :].astype(jnp.float32)
            low = jnp.where(lane < BS // 2, one, pltpu.roll(two, BS // 2, 1))
            high = jnp.where(lane < BS // 2, pltpu.roll(one, BS // 2, 1), two)
            left[2 * p, :, c * BS // 2 : (c + 2) * BS // 2] = low.astype(jnp.bfloat16)
            left[2 * p + 1, :, c * BS // 2 : (c + 2) * BS // 2] = high.astype(jnp.bfloat16)
        return 0

    lax.fori_loop(0, WIN // 2, gather_left, 0)
    for s in range(ROWS):
        copies[s].wait()

        def one(w, _):
            k = left_cols[w * ROWS + s]
            for g in range(GROUPS):
                block = held[s, g * HALF + k]
                col = cols[s * MARKS + g * BR + k]
                for m in range(KEPT):
                    slot = g * KEPT + m
                    put(right, w, s * Q, slot, block, col == keep[w * SLOTS + slot])
            return 0

        lax.fori_loop(0, WIN, one, 0, unroll=True)

    def multiply(w, _):
        full = jnp.dot(left[w], right[w], preferred_element_type=jnp.float32)
        parts = [full[:, i * BS : (i + 1) * BS] for i in range(SLOTS)]
        for x in range(REPS):
            mixed = parts[x]
            for i in range(SLOTS):
                if i != x:
                    moved = pltpu.roll(parts[i], (Q * (i - x)) % BS, 1)
                    mixed = jnp.where(lane // Q == i, moved, mixed)
            out[x, w] = mixed.astype(jnp.bfloat16)
        return 0

    lax.fori_loop(0, WIN, multiply, 0)


def layout_kernel(where, mid_cols, cols, keep, cube_keep, panels, right, held, sems):
    copies = fetch(panels, held, sems)
    rep = where[0]
    wide = lax.broadcasted_iota(jnp.int32, (BS, BS), 1)
    tall = lax.broadcasted_iota(jnp.int32, (BS, BS), 0)
    place = wide == (rep * Q + tall % Q)

    def own(w, _):
        for g in range(GROUPS):
            found = jnp.zeros((BS, BS), jnp.float32)
            for m in range(KEPT):
                hit = keep[w * SLOTS + g * KEPT + m] == cube_keep[w * GROUPS + g]
                found = jnp.where(tall // Q == g * KEPT + m, jnp.where(hit, -1.5, 0.0), found)
            found = jnp.where(place, found, 0.0).astype(jnp.bfloat16)
            right[w, INNER : INNER + BS, g * BS : (g + 1) * BS] = found
        return 0

    lax.fori_loop(0, WIN, own, 0)
    for s in range(ROWS):
        copies[s].wait()

        def one(w, _):
            for t in range(KEPT):
                k = mid_cols[(w * ROWS + s) * KEPT + t]
                for g in range(GROUPS):
                    hit = cols[s * MARKS + g * BR + k] == cube_keep[w * GROUPS + g]
                    put(right, w, (s * KEPT + t) * Q, g, held[s, g * HALF + k], hit)
            return 0

        lax.fori_loop(0, WIN, one, 0, unroll=True)


def cube_kernel(where, own, same, other, right, out):
    core = where[1]

    def one(w, _):
        total = jnp.dot(own[w], right[w, INNER:, :], preferred_element_type=jnp.float32)
        for y in range(CHIPS):
            for lefts, c in ((same, 2 * y + core), (other, 2 * y + 1 - core)):
                rows = pl.ds(pl.multiple_of(c * BS, BS), BS)
                total += jnp.dot(lefts[y, w], right[w, rows, :], preferred_element_type=jnp.float32)
        total = -2.0 * total
        for g in range(GROUPS):
            out[w, g] = total[:, g * BS : (g + 1) * BS].astype(jnp.bfloat16)
        return 0

    lax.fori_loop(0, WIN, one, 0)


def shaped(*shape):
    return jax.ShapeDtypeStruct(shape, jnp.bfloat16)


def call(kernel, out, scalars, arrays, scratch=(), specs=None, room=8, work=(0, 0)):
    return pl.pallas_call(
        kernel,
        out_shape=out,
        in_specs=[SMEM] * len(scalars) + (specs or [VMEM] * len(arrays)),
        out_specs=jax.tree.map(lambda _: VMEM, out),
        scratch_shapes=scratch,
        cost_estimate=pl.CostEstimate(flops=work[0], bytes_accessed=work[1], transcendentals=0),
        compiler_params=pltpu.CompilerParams(vmem_limit_bytes=room * 2**20),
    )(*scalars, *arrays)


def on_device(p_vals, p_cols, square_cols, cube_cols):
    rep = lax.axis_index("rep")
    core = lax.axis_index("col") % 2
    where = jnp.stack([rep, core]).astype(jnp.int32)
    keep = square_cols.reshape(-1)
    cube_keep = cube_cols.reshape(-1)

    spread, panel = call(
        prepare_kernel,
        (shaped(COLS, WIN // 2 * BS + 16, BS), shaped(GROUPS * BR + 1, Q, BS)),
        (where, p_cols.reshape(-1), keep),
        [p_vals],
        [
            pltpu.VMEM((WIN, GROUPS, BS, BS), jnp.bfloat16),
            pltpu.VMEM((BR, GROUPS, Q, BS), jnp.bfloat16),
            pltpu.SemaphoreType.DMA((2,)),
        ],
        [HBM],
        63,
    )
    lefts = lax.all_to_all(spread, "col", 0, 0)
    scale = jnp.exp2(panel[BR, 0, MARKS].astype(jnp.float32))
    plain = lax.broadcasted_iota(jnp.int32, panel.shape, 0) == BR
    panel = (panel.astype(jnp.float32) * jnp.where(plain, 1.0, scale)).astype(jnp.float16)
    panels = lax.all_gather(panel, "row")
    panels, lefts = lax.optimization_barrier((panels, lefts))
    notes = lefts[:, WIN // 2 * BS, :].astype(jnp.int32)
    left_cols = notes[:, : WIN * GROUPS].reshape(COLS, WIN, GROUPS).transpose(1, 0, 2).reshape(-1)
    mid_cols = notes[:, WIN * GROUPS : WIN * GROUPS * (1 + KEPT)]
    mid_cols = mid_cols.reshape(COLS, WIN, GROUPS, KEPT).transpose(1, 0, 2, 3).reshape(-1)
    marks = panels[:, BR, 0, : MARKS + 1].astype(jnp.float32)
    cols = marks[:, :MARKS].astype(jnp.int32).reshape(-1)
    back = jnp.exp2(-marks[:, MARKS])[:, None, None, None]
    panels = (panels.astype(jnp.float32) * back).astype(jnp.bfloat16)
    held = [pltpu.VMEM(panels.shape, panels.dtype)]
    sems = [pltpu.SemaphoreType.DMA((ROWS,))]

    partial = call(
        square_kernel,
        shaped(REPS, WIN, BS, BS),
        (left_cols, cols, keep),
        (lefts, panels),
        held
        + [
            pltpu.VMEM((WIN, BS, ROWS * Q), jnp.bfloat16),
            pltpu.VMEM((WIN, ROWS * Q, SLOTS * BS), jnp.bfloat16),
        ]
        + sems,
        [VMEM, HBM],
        ROOM,
        (WIN * 2 * BS * ROWS * Q * SLOTS * BS, panels.size * 2),
    )
    right = call(
        layout_kernel,
        shaped(WIN, INNER + BS, GROUPS * BS),
        (where, mid_cols, cols, keep, cube_keep),
        [panels],
        held + sems,
        [HBM],
        ROOM,
        (0, 3 * panels.size * 2),
    )
    parts = lax.all_to_all(partial, "rep", 0, 0, tiled=True)
    own = jnp.sum(parts.astype(jnp.float32), axis=0).astype(jnp.bfloat16)
    same = lax.all_to_all(
        jnp.broadcast_to(own[None], (CHIPS,) + own.shape), "col", 0, 0, axis_index_groups=SAME_CORE
    )
    other = lax.ppermute(same, "col", CORES)
    partial = call(
        cube_kernel,
        shaped(WIN, GROUPS, BS, BS),
        (where,),
        (own, same, other, right),
        work=(WIN * 2 * BS * (INNER + BS) * GROUPS * BS, right.size * 2),
    )
    parts = lax.all_to_all(partial, "rep", 0, 0, tiled=True)
    parts = parts.reshape((REPS, WIN // REPS) + parts.shape[1:]).astype(jnp.float32)
    return jnp.sum(parts, axis=0).astype(jnp.bfloat16)[:, :, None]


def solution(mesh):
    in_specs = (
        P("row", "col", None, None),
        P("row", "col"),
        P("row", "col", None),
        P("row", "col", None),
    )
    out_specs = P(("row", "rep"), "col", None, None, None)
    return jax.shard_map(
        on_device, mesh=mesh, in_specs=in_specs, out_specs=out_specs, check_vma=False
    )
```

time: 181 us -> 171 us (0.945)
  between operations: 14.3 us -> 0.84 us
  Pallas kernels: 7.76 us -> 16.6 us
  starting transfers between devices: 10.4 us -> 18.7 us
  local copies, waits for them, and re-layouts: 11.3 us -> 5.44 us
  other arithmetic: 14.1 us -> 10.6 us
  blocking collectives: 121 us -> 118 us
    all_to_all x0 -> x1, starting transfers between devices: none -> 10.4 us  [on_device(): lefts = lax.all_to_all(spread, 'col', 0, 0)]
    pallas_call x2 -> x4, Pallas kernels: 7.76 us -> 16.6 us  [call(): pl.pallas_call(kernel, out_shape=out, in_specs=[SMEM] * len(scalars) + (s...]
    unnamed x13 -> x9, local copies, waits for them, and re-layouts: 7.08 us -> 1.62 us
    ppermute x1, starting transfers between devices: 10.4 us -> 8.37 us  [on_device(): other = lax.ppermute(same, 'col', CORES)]
    all_gather x1, blocking collectives: 81.8 us -> 79.9 us  [on_device(): panels = lax.all_gather(panel, 'row')]
  transfers between devices with their start and end apart: 2 -> 2, of which waited for: 1 -> 0; matrix products, arithmetic and copies ran while one was open for 7% -> 2% of each run, Pallas kernels for 0% -> 2%
where the time goes in v4:
time: 171 us
  blocking collectives  118 us (69%)
  starting transfers between devices  18.7 us (11%)
  Pallas kernels  16.6 us (10%)
  other arithmetic  10.6 us (6%)
  local copies, waits for them, and re-layouts  5.44 us (3%)
    all_gather x1, blocking collectives, on_device(): panels = lax.all_gather(panel, 'row')  79.9 us
    all_to_all x2, blocking collectives, on_device(): parts = lax.all_to_all(partial, 'rep', 0, 0, tiled=True)  26.3 us
    pallas_call x4, Pallas kernels, call(): pl.pallas_call(kernel, out_shape=out, in_specs=[SMEM] * len(scalars) + (s...  16.6 us
    all_to_all x1, blocking collectives, on_device(): lax.all_to_all(jnp.broadcast_to(own[None], (CHIPS,) + own.shape), 'col',...  12.2 us
    all_to_all x1, starting transfers between devices, on_device(): lefts = lax.all_to_all(spread, 'col', 0, 0)  10.4 us
    ppermute x1, starting transfers between devices, on_device(): other = lax.ppermute(same, 'col', CORES)  8.37 us
    convert_element_type x1, other arithmetic, on_device(): panels = (panels.astype(jnp.float32) * back).astype(jnp.bfloat16)  6.82 us
  transfers between devices with their start and end apart: 2, of which 0 were waited for; matrix products, arithmetic and copies ran while one was open for 2% of the time, Pallas kernels for 2%

profile of v4, /device:TPU:1, one launch (start us, length us, event | category | flops | bytes accessed | tf_op | source)
XLA Modules:
  0.0 170.5 jit_solution(4111096000104174201)
XLA Ops:
  0.0 0.8 copy.18
  0.8 0.7 reshape.48.square_cols.keep
  1.5 0.8 copy.17
  2.2 0.7 reshape.47.p_cols
  2.9 0.6 pad_add_fusion.where
  3.5 3.2 %shard_map.46 = (bf16[8,528,128]{2,1,0:T(8,128)(2,1)}, bf16[49,32,128]{2,1,0:T(8,128)(2,1)}) custom-call(s32[2]{0:T(128)} %pad_add_fusion.where, s32[48]{0:T(128)} %reshape.47.p_cols, s32[32]{0:T(128)} %reshape.48.square_cols.keep, bf16[24,2,128,128]{3,2,1,0:T(8,128)(2,1)} %p_vals.1), custom_call_target="tpu_custom_call" | custom-call | tf_op jit(solution)/shard_map/pallas_call | solution.py:189
  6.8 10.4 %all-to-all-start = ((bf16[8,528,128]{2,1,0:T(8,128)(2,1)}), bf16[8,528,128]{2,1,0:T(8,128)(2,1)S(1)}, u32[]{:S(2)}, u32[]{:S(2)}) async-start(bf16[8,528,128]{2,1,0:T(8,128)(2,1)} %get-tuple-element.10), calls=%async_computation | async-start | bytes 2162688 | tf_op jit(solution)/shard_map/all_to_all | solution.py:220
  17.1 1.3 slice.21
  19.1 1.2 multiply_convert_fusion.1
  20.2 79.9 %all-gather.2 = f16[784,32,128]{2,1,0:T(8,128)(2,1)} all-gather(f16[49,32,128]{2,1,0:T(8,128)(2,1)S(1)} %multiply_convert_fusion.1), channel_id=2, replica_groups=mesh['row'=16,'col'=8,'rep'=4] {'row'}, dimensions={0}, use_global_device_ids=true | all-gather | bytes 6823936 | tf_op jit(solution)/shard_map/all_gather | solution.py:224
  100.2 0.0 all-to-all-done.lefts
  100.2 0.8 slice_convert_fusion.1
  101.0 0.2 fusion.2
  101.1 0.0 copy-start
  101.2 6.8 %multiply_convert_fusion.panels = bf16[16,49,32,128]{3,2,1,0:T(8,128)(2,1)} fusion(f16[16,49,32,128]{3,2,1,0:T(8,128)(2,1)} %bitcast.18, f32[16]{0:T(128)S(1)} %fusion.2), kind=kLoop, calls=%fused_computation | loop fusion | flops 9633792 | bytes 12845120 | tf_op jit(solution)/shard_map/convert_element_type | solution.py:233
  108.0 0.1 reshape.51.cols
  108.1 0.1 copy.19
  108.1 0.1 copy.20
  108.3 0.1 reshape.50.left_cols
  108.4 0.0 copy-done
  108.4 0.0 copy-start.2
  108.4 0.0 copy-start.1
  108.4 6.6 %shard_map.47 = bf16[4,8,128,128]{3,2,1,0:T(8,128)(2,1)S(1)} custom-call(s32[128]{0:T(128)S(1)} %reshape.50.left_cols, s32[768]{0:T(1024)S(1)} %reshape.51.cols, s32[32]{0:T(128)S(1)} %copy-done, bf16[8,528,128]{2,1,0:T(8,128)(2,1)S(1)} %all-to-all-done.lefts, bf16[16,49,32,128]{3,2,1,0:T(8,128)(2,1)} %multiply_convert_fusion.panels), custom_call_target="tpu_custom_call" | custom-call | flops 536870912 | bytes 6422528 | tf_op jit(solution)/shard_map/pallas_call | solution.py:189
  115.1 14.5 %all_to_all.20 = bf16[4,8,128,128]{3,2,1,0:T(8,128)(2,1)S(1)} all-to-all(bf16[4,8,128,128]{3,2,1,0:T(8,128)(2,1)S(1)} %shard_map.47), channel_id=1, replica_groups=mesh['row'=16,'col'=8,'rep'=4] {'rep'}, dimensions={0} | all-to-all | bytes 2097152 | tf_op jit(solution)/shard_map/all_to_all | solution.py:262
  129.6 0.2 reduce_sum.24.own
  129.8 0.2 broadcast_in_dim.20
  130.1 12.2 %all_to_all.21.same = bf16[4,8,128,128]{3,2,1,0:T(8,128)(2,1)S(1)} all-to-all(bf16[4,8,128,128]{3,2,1,0:T(8,128)(2,1)S(1)} %broadcast_in_dim.20), channel_id=1, replica_groups={{0,8,16,24},{4,12,20,28},{1,9,17,25},{5,13,21,29},{2,10,18,26},{6,14,22..., dimensions={0} | all-to-all | bytes 2097152 | tf_op jit(solution)/shard_map/all_to_all | solution.py:264
  142.2 8.4 %collective-permute-start = (bf16[4,8,128,128]{3,2,1,0:T(8,128)(2,1)S(1)}, bf16[4,8,128,128]{3,2,1,0:T(8,128)(2,1)S(1)}, u32[]{:S(2)}, u32[]{:S(2)}) collective-permute-start(bf16[4,8,128,128]{3,2,1,0:T(8,128)(2,1)S(1)} %all_to_all.21.same), channel_id=1, source_target_pairs={{0,4},{4,0},{8,12},{12,8},{16,20},{20,16},{24,28},{28,24},{1,5},{5... | collective-permute-start | bytes 3145736 | tf_op jit(solution)/shard_map/ppermute | solution.py:267
  150.6 0.0 copy-done.2
  150.6 0.1 copy.23
  150.7 0.1 reshape.54.cube_keep
  150.8 0.1 slice.27
  150.9 0.1 copy.21
  150.9 0.2 copy.22
  151.1 0.2 reshape.53.mid_cols
  151.3 0.0 copy-done.1
  151.3 3.6 %shard_map.48.right = bf16[8,1152,256]{2,1,0:T(8,128)(2,1)S(1)} custom-call(s32[2]{0:T(128)S(1)} %copy-done.1, s32[256]{0:T(256)S(1)} %reshape.53.mid_cols, s32[768]{0:T(1024)S(1)} %reshape.51.cols, s32[32]{0:T(128)S(1)} %copy-done, s32[16]{0:T(128)S(1)} %reshape.54.cube_keep, bf16[16,49,32,128]{3,2,1,0:T(8,128)(2,1)} %multiply_convert_fusion.panels), custom_call_target="tpu_custom_call" | custom-call | bytes 19267584 | tf_op jit(solution)/shard_map/pallas_call | solution.py:189
  154.9 0.0 collective-permute-done.other
  154.9 3.1 %shard_map.49 = bf16[8,2,128,128]{3,2,1,0:T(8,128)(2,1)S(1)} custom-call(s32[2]{0:T(128)S(1)} %copy-done.1, bf16[8,128,128]{2,1,0:T(8,128)(2,1)S(1)} %reduce_sum.24.own, bf16[4,8,128,128]{3,2,1,0:T(8,128)(2,1)S(1)} %all_to_all.21.same, bf16[4,8,128,128]{3,2,1,0:T(8,128)(2,1)S(1)} %collective-permute-done.other, bf16[8,1152,256]{2,1,0:T(8,128)(2,1)S(1)} %shard_map.48.right), custom_call_target="tpu_custom_call" | custom-call | flops 603979776 | bytes 4718592 | tf_op jit(solution)/shard_map/pallas_call | solution.py:189
  158.0 11.7 %all_to_all.22 = bf16[8,2,128,128]{3,2,1,0:T(8,128)(2,1)S(1)} all-to-all(bf16[8,2,128,128]{3,2,1,0:T(8,128)(2,1)S(1)} %shard_map.49), channel_id=1, replica_groups=mesh['row'=16,'col'=8,'rep'=4] {'rep'}, dimensions={0} | all-to-all | bytes 1048576 | tf_op jit(solution)/shard_map/all_to_all | solution.py:275
  169.8 0.7 reduce_sum.25
  (3 shorter events, 0.0 us)
Async XLA Ops:
  6.8 93.4 %all-to-all-start = ((bf16[8,528,128]{2,1,0:T(8,128)(2,1)}), bf16[8,528,128]{2,1,0:T(8,128)(2,1)S(1)}, u32[]{:S(2)}, u32[]{:S(2)}) async-start(bf16[8,528,128]{2,1,0:T(8,128)(2,1)} %get-tuple-element.10), calls=%async_computation | async-start | bytes 2162688 | tf_op jit(solution)/shard_map/all_to_all | solution.py:220
  101.1 7.3 %copy-start = (s32[32]{0:T(128)S(1)}, s32[32]{0:T(128)}, u32[]{:S(2)}) copy-start(s32[32]{0:T(128)} %reshape.48.square_cols.keep) | copy-start | bytes 388
  108.4 42.2 %copy-start.2 = (s32[8,2,1]{0,2,1:T(1,128)S(1)}, s32[8,2,1]{0,2,1:T(1,128)}, u32[]{:S(2)}) copy-start(s32[8,2,1]{0,2,1:T(1,128)} %param.7) | copy-start | bytes 196
  108.4 42.8 %copy-start.1 = (s32[2]{0:T(128)S(1)}, s32[2]{0:T(128)}, u32[]{:S(2)}) copy-start(s32[2]{0:T(128)} %pad_add_fusion.where) | copy-start | bytes 28
  142.2 12.7 %collective-permute-start = (bf16[4,8,128,128]{3,2,1,0:T(8,128)(2,1)S(1)}, bf16[4,8,128,128]{3,2,1,0:T(8,128)(2,1)S(1)}, u32[]{:S(2)}, u32[]{:S(2)}) collective-permute-start(bf16[4,8,128,128]{3,2,1,0:T(8,128)(2,1)S(1)} %all_to_all.21.same), channel_id=1, source_target_pairs={{0,4},{4,0},{8,12},{12,8},{16,20},{20,16},{24,28},{28,24},{1,5},{5... | collective-permute-start | bytes 3145736 | tf_op jit(solution)/shard_map/ppermute | solution.py:267

commit v5 on v4

v5 whole, which is shorter than its diff:
```python
import jax
import jax.numpy as jnp
from jax import lax
from jax.experimental import pallas as pl
from jax.experimental.pallas import tpu as pltpu
from jax.sharding import PartitionSpec as P

ROWS = 16
COLS = 8
CHIPS = 4
REPS = 4
GROUPS = 2
WIN = 8
BR = 24
BS = 128
Q = BS // REPS
HALF = BR + 1
KEPT = 2
SLOTS = GROUPS * KEPT
MARKS = GROUPS * BR
ROOM = 48
INNER = ROWS * KEPT * Q

CORES = [(i, i ^ 1) for i in range(COLS)]
SAME_CORE = [[c + i for i in range(0, COLS, 2)] for c in range(2)]

SMEM = pl.BlockSpec(memory_space=pltpu.SMEM)
HBM = pl.BlockSpec(memory_space=pltpu.HBM)
VMEM = pl.BlockSpec(memory_space=pltpu.VMEM)


def put(right, w, row, lane_tile, block, hit, spare):
    row = pl.multiple_of(jnp.where(hit, row, spare), Q)
    right[w, pl.ds(row, Q), pl.ds(pl.multiple_of(lane_tile * BS, BS), BS)] = block


def clear(right, rows):
    def one(w, _):
        right[w, :rows, :] = jnp.zeros((rows, right.shape[2]), right.dtype)
        return 0

    lax.fori_loop(0, WIN, one, 0)


def fetch(panels, held, sems):
    copies = [pltpu.make_async_copy(panels.at[s], held.at[s], sems.at[s]) for s in range(ROWS)]
    for copy in copies:
        copy.start()
    return copies


def prepare_kernel(p_cols, square_cols, p_vals, spread, panel, heads, shares, sems):
    rep = lax.axis_index("rep")
    rows = pl.ds(pl.multiple_of(rep * Q, Q), Q)
    first = pltpu.make_async_copy(p_vals.at[:WIN], heads, sems.at[0])
    second = pltpu.make_async_copy(p_vals.at[:, :, rows, :], shares, sems.at[1])
    first.start()
    second.start()
    lane = lax.broadcasted_iota(jnp.int32, (2 * 8, BS), 1)
    notes = jnp.zeros((2 * 8, BS), jnp.float32)
    for w in range(WIN):
        for g in range(GROUPS):
            at = w * GROUPS + g
            notes = jnp.where(lane == at, p_cols[g, w].astype(jnp.float32), notes)
            for m in range(KEPT):
                value = square_cols[g, m, w].astype(jnp.float32)
                notes = jnp.where(lane == WIN * GROUPS + at * KEPT + m, value, notes)
    notes = notes.astype(jnp.bfloat16)
    marks = jnp.zeros((2 * 8, BS), jnp.float32)
    for g in range(GROUPS):
        for k in range(BR):
            marks = jnp.where(lane == g * BR + k, p_cols[g, k].astype(jnp.float32), marks)

    group = lax.broadcasted_iota(jnp.int32, (BS, BS), 1) // Q
    first.wait()
    for p in range(WIN // 2):
        tile = jnp.zeros((BS, BS), jnp.float32)
        for i in range(2 * GROUPS):
            part = heads[2 * p + i // GROUPS, i % GROUPS].astype(jnp.float32)
            moved = pltpu.roll(part, lax.rem((i - rep) * Q + BS, BS), 1)
            tile = jnp.where(group == i, moved, tile)
        tile = tile.astype(jnp.bfloat16)
        for c in range(COLS):
            spread[c, p * BS : (p + 1) * BS, :] = tile
    for c in range(COLS):
        spread[c, WIN // 2 * BS :, :] = notes

    second.wait()
    peak = jnp.zeros((Q, BS), jnp.float32)
    for k in range(BR):
        for g in range(GROUPS):
            peak = jnp.maximum(peak, jnp.abs(shares[k, g].astype(jnp.float32)))
    peak = jnp.maximum(jnp.max(peak, axis=(0, 1), keepdims=True), 1e-37)
    power = jnp.clip(13.0 - jnp.floor(jnp.log2(peak)), 0.0, 110.0)
    scale = jnp.exp2(power)
    for k in range(BR):
        for g in range(GROUPS):
            block = shares[k, g].astype(jnp.float32) * scale
            panel[g * HALF + k] = block.astype(jnp.bfloat16)
    marks = jnp.where(lane == MARKS, power, marks)
    panel[BR] = jnp.concatenate([marks, marks], axis=0).astype(jnp.bfloat16)


def square_kernel(notes, marks, keep, lefts, panels, out, right, held, sems):
    def pick(p):
        for half in range(2):
            for s in range(ROWS):
                k = notes[s // GROUPS, 0, (2 * p + half) * GROUPS + s % GROUPS]
                for g in range(GROUPS):
                    pltpu.make_async_copy(
                        panels.at[s, g * HALF + k], held.at[p, half, s, g], sems.at[p]
                    ).start()

    pick(0)
    group = lax.broadcasted_iota(jnp.int32, (BS, BS), 1) // Q
    right[...] = jnp.zeros_like(right)

    def pair(p, _):
        @pl.when(p < WIN // 2 - 1)
        def _():
            pick(p + 1)

        pltpu.make_async_copy(held.at[p], held.at[p], sems.at[p]).wait()
        rows = pl.ds(pl.multiple_of(p * BS, BS), BS)
        left = jnp.concatenate([lefts[c, rows, :] for c in range(COLS)], axis=1)
        for half in range(2):
            w = 2 * p + half
            for s in range(ROWS):
                k = notes[s // GROUPS, 0, w * GROUPS + s % GROUPS]
                at = (s // GROUPS) * BS + (half * GROUPS + s % GROUPS) * Q
                for g in range(GROUPS):
                    block = held[p, half, s, g]
                    col = marks[s, g * BR + k]
                    for m in range(KEPT):
                        n = (g * KEPT + m) * BS
                        right[half, at : at + Q, n : n + BS] = jnp.where(
                            col == keep[g, m, w], block, jnp.zeros_like(block)
                        )
            full = jnp.dot(left, right[half], preferred_element_type=jnp.float32)
            p4 = [full[:, i * BS : (i + 1) * BS] for i in range(SLOTS)]
            u = [jnp.where(group < 2, p4[i], pltpu.roll(p4[i + 2], BS // 2, 1)) for i in range(2)]
            u += [jnp.where(group < 2, pltpu.roll(p4[i], BS // 2, 1), p4[i + 2]) for i in range(2)]
            for i in (0, 2):
                one = jnp.where(group % 2 == 0, u[i], pltpu.roll(u[i + 1], Q, 1))
                two = jnp.where(group % 2 == 0, pltpu.roll(u[i], BS - Q, 1), u[i + 1])
                out[i, w] = one.astype(jnp.bfloat16)
                out[i + 1, w] = two.astype(jnp.bfloat16)
        return 0

    lax.fori_loop(0, WIN // 2, pair, 0)


def layout_kernel(notes, marks, keep, cube_keep, panels, right, held, sems):
    copies = fetch(panels, held, sems)
    clear(right, INNER)
    rep = lax.axis_index("rep")
    wide = lax.broadcasted_iota(jnp.int32, (BS, BS), 1)
    tall = lax.broadcasted_iota(jnp.int32, (BS, BS), 0)
    place = wide == (rep * Q + tall % Q)

    def own(w, _):
        for g in range(GROUPS):
            found = jnp.zeros((BS, BS), jnp.float32)
            for m in range(KEPT):
                scale = jnp.where(keep[g, m, w] == cube_keep[g, 0, w], -1.5, 0.0)
                found = jnp.where(tall // Q == g * KEPT + m, scale, found)
            found = jnp.where(place, found, 0.0).astype(jnp.bfloat16)
            right[w, INNER : INNER + BS, g * BS : (g + 1) * BS] = found
        return 0

    lax.fori_loop(0, WIN, own, 0)
    for s in range(ROWS):
        copies[s].wait()
        for w in range(WIN):
            for t in range(KEPT):
                at = WIN * GROUPS + (w * GROUPS + s % GROUPS) * KEPT + t
                k = notes[s // GROUPS, 0, at]
                for g in range(GROUPS):
                    hit = marks[s, g * BR + k] == cube_keep[g, 0, w]
                    row = (s * KEPT + t) * Q
                    put(right, w, row, g, held[s, g * HALF + k], hit, INNER + BS)


def cube_kernel(own, same, other, right, out):
    core = lax.rem(lax.axis_index("col"), 2)

    def one(w, _):
        total = jnp.dot(own[w], right[w, INNER : INNER + BS, :], preferred_element_type=jnp.float32)
        for y in range(CHIPS):
            for lefts, c in ((same, 2 * y + core), (other, 2 * y + 1 - core)):
                rows = pl.ds(pl.multiple_of(c * BS, BS), BS)
                total += jnp.dot(lefts[y, w], right[w, rows, :], preferred_element_type=jnp.float32)
        total = -2.0 * total
        for g in range(GROUPS):
            out[w, g] = total[:, g * BS : (g + 1) * BS].astype(jnp.bfloat16)
        return 0

    lax.fori_loop(0, WIN, one, 0)


def shaped(*shape):
    return jax.ShapeDtypeStruct(shape, jnp.bfloat16)


def call(kernel, out, scalars, arrays, scratch=(), specs=None, room=8, work=(0, 0)):
    return pl.pallas_call(
        kernel,
        out_shape=out,
        in_specs=[SMEM] * len(scalars) + (specs or [VMEM] * len(arrays)),
        out_specs=jax.tree.map(lambda _: VMEM, out),
        scratch_shapes=scratch,
        cost_estimate=pl.CostEstimate(flops=work[0], bytes_accessed=work[1], transcendentals=0),
        compiler_params=pltpu.CompilerParams(vmem_limit_bytes=room * 2**20),
    )(*scalars, *arrays)


def on_device(p_vals, p_cols, square_cols, cube_cols):
    own_cols = p_cols.T
    keep = square_cols.transpose(1, 2, 0)
    cube_keep = cube_cols.transpose(1, 2, 0)

    spread, panel = call(
        prepare_kernel,
        (shaped(COLS, WIN // 2 * BS + 16, BS), shaped(GROUPS * BR + 1, Q, BS)),
        (own_cols, keep),
        [p_vals],
        [
            pltpu.VMEM((WIN, GROUPS, BS, BS), jnp.bfloat16),
            pltpu.VMEM((BR, GROUPS, Q, BS), jnp.bfloat16),
            pltpu.SemaphoreType.DMA((2,)),
        ],
        [HBM],
        63,
    )
    lefts = lax.all_to_all(spread, "col", 0, 0)
    panels = lax.all_gather(panel.astype(jnp.float16), "row")
    panels = lax.optimization_barrier(panels)
    notes = lefts[:, WIN // 2 * BS : WIN // 2 * BS + 1, :].astype(jnp.int32)
    marks = panels[:, BR, 0, :].astype(jnp.float32)
    back = jnp.exp2(-marks[:, MARKS])[:, None, None, None]
    marks = marks.astype(jnp.int32)
    panels = (panels.astype(jnp.float32) * back).astype(jnp.bfloat16)

    partial = call(
        square_kernel,
        shaped(REPS, WIN, BS, BS),
        (notes, marks, keep),
        (lefts, panels),
        [
            pltpu.VMEM((2, COLS * BS, SLOTS * BS), jnp.bfloat16),
            pltpu.VMEM((WIN // 2, 2, ROWS, GROUPS, Q, BS), jnp.bfloat16),
            pltpu.SemaphoreType.DMA((WIN // 2,)),
        ],
        [VMEM, HBM],
        ROOM,
        (WIN * 2 * BS * ROWS * Q * SLOTS * BS, panels.size * 2),
    )
    right = call(
        layout_kernel,
        shaped(WIN, INNER + BS + Q, GROUPS * BS),
        (notes, marks, keep, cube_keep),
        [panels],
        [pltpu.VMEM(panels.shape, panels.dtype), pltpu.SemaphoreType.DMA((ROWS,))],
        [HBM],
        ROOM,
        (0, 3 * panels.size * 2),
    )
    parts = lax.all_to_all(partial, "rep", 0, 0, tiled=True)
    own = jnp.sum(parts.astype(jnp.float32), axis=0).astype(jnp.bfloat16)
    same = lax.all_to_all(
        jnp.broadcast_to(own[None], (CHIPS,) + own.shape), "col", 0, 0, axis_index_groups=SAME_CORE
    )
    other = lax.ppermute(same, "col", CORES)
    partial = call(
        cube_kernel,
        shaped(WIN, GROUPS, BS, BS),
        (),
        (own, same, other, right),
        work=(WIN * 2 * BS * (INNER + BS) * GROUPS * BS, right.size * 2),
    )
    parts = lax.all_to_all(partial, "rep", 0, 0, tiled=True)
    parts = parts.reshape((REPS, WIN // REPS) + parts.shape[1:]).astype(jnp.float32)
    return jnp.sum(parts, axis=0).astype(jnp.bfloat16)[:, :, None]


def solution(mesh):
    in_specs = (
        P("row", "col", None, None),
        P("row", "col"),
        P("row", "col", None),
        P("row", "col", None),
    )
    out_specs = P(("row", "rep"), "col", None, None, None)
    return jax.shard_map(
        on_device, mesh=mesh, in_specs=in_specs, out_specs=out_specs, check_vma=False
    )
```

time: 171 us -> 158 us (0.924)
  local copies, waits for them, and re-layouts: 5.44 us -> 0.25 us
  other arithmetic: 10.6 us -> 6.22 us
    convert_element_type x1, other arithmetic: 6.82 us -> 4 us  [on_device(): panels = (panels.astype(jnp.float32) * back).astype(jnp.bfloat16)]
    reshape x6 -> x0, local copies, waits for them, and re-layouts: 1.81 us -> none  [the longest x1 0.69 us: on_device(): keep = square_cols.reshape(-1)]
  transfers between devices with their start and end apart: 2 -> 2, of which waited for: 0 -> 0; matrix products, arithmetic and copies ran while one was open for 2% -> 3% of each run, Pallas kernels for 2% -> 3%
where the time goes in v5:
time: 158 us
  blocking collectives  117 us (74%)
  starting transfers between devices  18.9 us (12%)
  Pallas kernels  15.2 us (10%)
  other arithmetic  6.22 us (4%)
    all_gather x1, blocking collectives, on_device(): panels = lax.all_gather(panel.astype(jnp.float16), 'row')  78.5 us
    all_to_all x2, blocking collectives, on_device(): parts = lax.all_to_all(partial, 'rep', 0, 0, tiled=True)  26.1 us
    pallas_call x4, Pallas kernels, call(): pl.pallas_call(kernel, out_shape=out, in_specs=[SMEM] * len(scalars) + (s...  15.2 us
    all_to_all x1, blocking collectives, on_device(): lax.all_to_all(jnp.broadcast_to(own[None], (CHIPS,) + own.shape), 'col',...  12.2 us
    all_to_all x1, starting transfers between devices, on_device(): lefts = lax.all_to_all(spread, 'col', 0, 0)  10.4 us
    ppermute x1, starting transfers between devices, on_device(): other = lax.ppermute(same, 'col', CORES)  8.59 us
    convert_element_type x1, other arithmetic, on_device(): panels = (panels.astype(jnp.float32) * back).astype(jnp.bfloat16)  4 us
  transfers between devices with their start and end apart: 2, of which 0 were waited for; matrix products, arithmetic and copies ran while one was open for 3% of the time, Pallas kernels for 3%

profile of v5, /device:TPU:1, one launch (start us, length us, event | category | flops | bytes accessed | tf_op | source)
XLA Modules:
  0.0 157.6 jit_solution(17663067718938277167)
XLA Ops:
  0.0 3.1 %shard_map.46 = (bf16[8,528,128]{2,1,0:T(8,128)(2,1)}, bf16[49,32,128]{2,1,0:T(8,128)(2,1)}) custom-call(s32[2,24]{1,0:T(2,128)} %bitcast.16, s32[2,2,8]{2,1,0:T(2,128)} %bitcast.7, bf16[24,2,128,128]{3,2,1,0:T(8,128)(2,1)} %p_vals.1), custom_call_target="tpu_custom_call" | custom-call | tf_op jit(solution)/shard_map/pallas_call | solution.py:206
  3.1 10.4 %all-to-all-start = ((bf16[8,528,128]{2,1,0:T(8,128)(2,1)}), bf16[8,528,128]{2,1,0:T(8,128)(2,1)S(1)}, u32[]{:S(2)}, u32[]{:S(2)}) async-start(bf16[8,528,128]{2,1,0:T(8,128)(2,1)} %get-tuple-element.7), calls=%async_computation | async-start | bytes 2162688 | tf_op jit(solution)/shard_map/all_to_all | solution.py:235
  13.5 1.1 convert_element_type.26
  14.6 78.5 %all-gather.2 = f16[784,32,128]{2,1,0:T(8,128)(2,1)S(1)} all-gather(f16[49,32,128]{2,1,0:T(8,128)(2,1)S(1)} %convert_element_type.26), channel_id=2, replica_groups=mesh['row'=16,'col'=8,'rep'=4] {'row'}, dimensions={0}, use_global_device_ids=true | all-gather | bytes 6823936 | tf_op jit(solution)/shard_map/all_gather | solution.py:236
  93.1 0.2 fusion.2
  93.3 0.0 copy-start
  93.3 4.0 %multiply_convert_fusion.panels = bf16[16,49,32,128]{3,2,1,0:T(8,128)(2,1)} fusion(f16[16,49,32,128]{3,2,1,0:T(8,128)(2,1)S(1)} %bitcast.12, f32[16]{0:T(128)S(1)} %fusion.2), kind=kLoop, calls=%fused_computation | loop fusion | flops 9633792 | bytes 12845120 | tf_op jit(solution)/shard_map/convert_element_type | solution.py:242
  97.3 0.0 all-to-all-done.lefts
  97.3 0.0 copy-done
  97.3 0.0 copy-start.1
  97.3 5.6 %shard_map.47 = bf16[4,8,128,128]{3,2,1,0:T(8,128)(2,1)S(1)} custom-call(s32[8,1,128]{2,1,0:T(1,128)S(1)} %slice_convert_fusion.1.notes, s32[16,128]{1,0:T(8,128)S(1)} %convert_element_type.29.marks, s32[2,2,8]{2,1,0:T(2,128)S(1)} %bitcast.8, bf16[8,528,128]{2,1,0:T(8,128)(2,1)S(1)} %all-to-all-done.lefts, bf16[16,49,32,128]{3,2,1,0:T(8,128)(2,1)} %multiply_convert_fusion.panels), custom_call_target="tpu_custom_call" | custom-call | flops 536870912 | bytes 6422528 | tf_op jit(solution)/shard_map/pallas_call | solution.py:206
  102.9 14.4 %all_to_all.20 = bf16[4,8,128,128]{3,2,1,0:T(8,128)(2,1)S(1)} all-to-all(bf16[4,8,128,128]{3,2,1,0:T(8,128)(2,1)S(1)} %shard_map.47), channel_id=1, replica_groups=mesh['row'=16,'col'=8,'rep'=4] {'rep'}, dimensions={0} | all-to-all | bytes 2097152 | tf_op jit(solution)/shard_map/all_to_all | solution.py:268
  117.3 0.2 reduce_sum.24.own
  117.5 0.2 broadcast_in_dim.4
  117.8 12.2 %all_to_all.21.same = bf16[4,8,128,128]{3,2,1,0:T(8,128)(2,1)S(1)} all-to-all(bf16[4,8,128,128]{3,2,1,0:T(8,128)(2,1)S(1)} %broadcast_in_dim.4), channel_id=1, replica_groups={{0,8,16,24},{4,12,20,28},{1,9,17,25},{5,13,21,29},{2,10,18,26},{6,14,22..., dimensions={0} | all-to-all | bytes 2097152 | tf_op jit(solution)/shard_map/all_to_all | solution.py:270
  129.9 8.6 %collective-permute-start = (bf16[4,8,128,128]{3,2,1,0:T(8,128)(2,1)S(1)}, bf16[4,8,128,128]{3,2,1,0:T(8,128)(2,1)S(1)}, u32[]{:S(2)}, u32[]{:S(2)}) collective-permute-start(bf16[4,8,128,128]{3,2,1,0:T(8,128)(2,1)S(1)} %all_to_all.21.same), channel_id=1, source_target_pairs={{0,4},{4,0},{8,12},{12,8},{16,20},{20,16},{24,28},{28,24},{1,5},{5... | collective-permute-start | bytes 3145736 | tf_op jit(solution)/shard_map/ppermute | solution.py:273
  138.5 0.0 copy-done.1
  138.5 4.0 %shard_map.48.right = bf16[8,1184,256]{2,1,0:T(8,128)(2,1)S(1)} custom-call(s32[8,1,128]{2,1,0:T(1,128)S(1)} %slice_convert_fusion.1.notes, s32[16,128]{1,0:T(8,128)S(1)} %convert_element_type.29.marks, s32[2,2,8]{2,1,0:T(2,128)S(1)} %bitcast.9, s32[2,1,8]{2,1,0:T(1,128)S(1)} %bitcast.10, bf16[16,49,32,128]{3,2,1,0:T(8,128)(2,1)} %multiply_convert_fusion.panels), custom_call_target="tpu_custom_call" | custom-call | bytes 19267584 | tf_op jit(solution)/shard_map/pallas_call | solution.py:206
  142.5 0.0 collective-permute-done.other
  142.6 2.5 %shard_map.49 = bf16[8,2,128,128]{3,2,1,0:T(8,128)(2,1)S(1)} custom-call(bf16[8,128,128]{2,1,0:T(8,128)(2,1)S(1)} %reduce_sum.24.own, bf16[4,8,128,128]{3,2,1,0:T(8,128)(2,1)S(1)} %all_to_all.21.same, bf16[4,8,128,128]{3,2,1,0:T(8,128)(2,1)S(1)} %collective-permute-done.other, bf16[8,1184,256]{2,1,0:T(8,128)(2,1)S(1)} %shard_map.48.right), custom_call_target="tpu_custom_call" | custom-call | flops 603979776 | bytes 4849664 | tf_op jit(solution)/shard_map/pallas_call | solution.py:206
  145.1 11.7 %all_to_all.22 = bf16[8,2,128,128]{3,2,1,0:T(8,128)(2,1)S(1)} all-to-all(bf16[8,2,128,128]{3,2,1,0:T(8,128)(2,1)S(1)} %shard_map.49), channel_id=1, replica_groups=mesh['row'=16,'col'=8,'rep'=4] {'rep'}, dimensions={0} | all-to-all | bytes 1048576 | tf_op jit(solution)/shard_map/all_to_all | solution.py:281
  156.8 0.7 reduce_sum.25
  (3 shorter events, 0.0 us)
Async XLA Ops:
  3.1 94.2 %all-to-all-start = ((bf16[8,528,128]{2,1,0:T(8,128)(2,1)}), bf16[8,528,128]{2,1,0:T(8,128)(2,1)S(1)}, u32[]{:S(2)}, u32[]{:S(2)}) async-start(bf16[8,528,128]{2,1,0:T(8,128)(2,1)} %get-tuple-element.7), calls=%async_computation | async-start | bytes 2162688 | tf_op jit(solution)/shard_map/all_to_all | solution.py:235
  93.3 4.0 %copy-start = (s32[8,2,2]{0,2,1:T(2,128)S(1)}, s32[8,2,2]{0,2,1:T(2,128)}, u32[]{:S(2)}) copy-start(s32[8,2,2]{0,2,1:T(2,128)} %param.6) | copy-start | bytes 388
  97.3 41.2 %copy-start.1 = (s32[8,2,1]{0,2,1:T(1,128)S(1)}, s32[8,2,1]{0,2,1:T(1,128)}, u32[]{:S(2)}) copy-start(s32[8,2,1]{0,2,1:T(1,128)} %param.7) | copy-start | bytes 196
  129.9 12.6 %collective-permute-start = (bf16[4,8,128,128]{3,2,1,0:T(8,128)(2,1)S(1)}, bf16[4,8,128,128]{3,2,1,0:T(8,128)(2,1)S(1)}, u32[]{:S(2)}, u32[]{:S(2)}) collective-permute-start(bf16[4,8,128,128]{3,2,1,0:T(8,128)(2,1)S(1)} %all_to_all.21.same), channel_id=1, source_target_pairs={{0,4},{4,0},{8,12},{12,8},{16,20},{20,16},{24,28},{28,24},{1,5},{5... | collective-permute-start | bytes 3145736 | tf_op jit(solution)/shard_map/ppermute | solution.py:273

commit v6 on v5

--- a/solution.py
+++ b/solution.py
@@ -14,12 +14,13 @@
 BR = 24
 BS = 128
 Q = BS // REPS
-HALF = BR + 1
 KEPT = 2
 SLOTS = GROUPS * KEPT
 MARKS = GROUPS * BR
 ROOM = 48
 INNER = ROWS * KEPT * Q
+PAIR = GROUPS * Q
+TALL = BR * PAIR + 16
 
 CORES = [(i, i ^ 1) for i in range(COLS)]
 SAME_CORE = [[c + i for i in range(0, COLS, 2)] for c in range(2)]
@@ -40,6 +41,13 @@
         return 0
 
     lax.fori_loop(0, WIN, one, 0)
+
+
+def scalars(sources, held, sems):
+    copies = [pltpu.make_async_copy(*pair, sems.at[i]) for i, pair in enumerate(zip(sources, held))]
+    for copy in copies:
+        copy.start()
+    return copies
 
 
 def fetch(panels, held, sems):
@@ -49,13 +57,16 @@
     return copies
 
 
-def prepare_kernel(p_cols, square_cols, p_vals, spread, panel, heads, shares, sems):
+def prepare_kernel(p_cols_in, square_in, p_vals, spread, panel, heads, shares, sems, *small):
+    p_cols, square_cols, small_sems = small
     rep = lax.axis_index("rep")
     rows = pl.ds(pl.multiple_of(rep * Q, Q), Q)
     first = pltpu.make_async_copy(p_vals.at[:WIN], heads, sems.at[0])
     second = pltpu.make_async_copy(p_vals.at[:, :, rows, :], shares, sems.at[1])
     first.start()
     second.start()
+    for copy in scalars((p_cols_in, square_in), (p_cols, square_cols), small_sems):
+        copy.wait()
     lane = lax.broadcasted_iota(jnp.int32, (2 * 8, BS), 1)
     notes = jnp.zeros((2 * 8, BS), jnp.float32)
     for w in range(WIN):
@@ -96,28 +107,33 @@
     for k in range(BR):
         for g in range(GROUPS):
             block = shares[k, g].astype(jnp.float32) * scale
-            panel[g * HALF + k] = block.astype(jnp.bfloat16)
+            panel[k * PAIR + g * Q : k * PAIR + (g + 1) * Q, :] = block.astype(jnp.bfloat16)
     marks = jnp.where(lane == MARKS, power, marks)
-    panel[BR] = jnp.concatenate([marks, marks], axis=0).astype(jnp.bfloat16)
-
-
-def square_kernel(notes, marks, keep, lefts, panels, out, right, held, sems):
+    panel[BR * PAIR :, :] = marks.astype(jnp.bfloat16)
+
+
+def square_kernel(notes_in, marks_in, keep_in, lefts, panels, out, right, held, sems, *small):
+    notes, marks, keep, small_sems = small
+    waits = scalars((notes_in, marks_in, keep_in), small[:-1], small_sems)
+
     def pick(p):
         for half in range(2):
             for s in range(ROWS):
                 k = notes[s // GROUPS, 0, (2 * p + half) * GROUPS + s % GROUPS]
-                for g in range(GROUPS):
-                    pltpu.make_async_copy(
-                        panels.at[s, g * HALF + k], held.at[p, half, s, g], sems.at[p]
-                    ).start()
-
+                rows = pl.ds(pl.multiple_of(k * PAIR, PAIR), PAIR)
+                pltpu.make_async_copy(
+                    panels.at[s, rows, :], held.at[p, half, s], sems.at[p]
+                ).start()
+
+    waits[0].wait()
     pick(0)
     group = lax.broadcasted_iota(jnp.int32, (BS, BS), 1) // Q
     right[...] = jnp.zeros_like(right)
+    for copy in waits[1:]:
+        copy.wait()
 
     def pair(p, _):
-        @pl.when(p < WIN // 2 - 1)
-        def _():
+        if p < WIN // 2 - 1:
             pick(p + 1)
 
         pltpu.make_async_copy(held.at[p], held.at[p], sems.at[p]).wait()
@@ -129,7 +145,7 @@
                 k = notes[s // GROUPS, 0, w * GROUPS + s % GROUPS]
                 at = (s // GROUPS) * BS + (half * GROUPS + s % GROUPS) * Q
                 for g in range(GROUPS):
-                    block = held[p, half, s, g]
+                    block = held[p, half, s, g * Q : (g + 1) * Q, :]
                     col = marks[s, g * BR + k]
                     for m in range(KEPT):
                         n = (g * KEPT + m) * BS
@@ -147,12 +163,18 @@
                 out[i + 1, w] = two.astype(jnp.bfloat16)
         return 0
 
-    lax.fori_loop(0, WIN // 2, pair, 0)
-
-
-def layout_kernel(notes, marks, keep, cube_keep, panels, right, held, sems):
+    for p in range(WIN // 2):
+        pair(p, 0)
+
+
+def layout_kernel(notes_in, marks_in, keep_in, cube_keep_in, panels, right, held, sems, *small):
+    notes, marks, keep, cube_keep, small_sems = small
+    sources = (notes_in, marks_in, keep_in, cube_keep_in)
+    waits = scalars(sources, small[:-1], small_sems)
     copies = fetch(panels, held, sems)
     clear(right, INNER)
+    for copy in waits:
+        copy.wait()
     rep = lax.axis_index("rep")
     wide = lax.broadcasted_iota(jnp.int32, (BS, BS), 1)
     tall = lax.broadcasted_iota(jnp.int32, (BS, BS), 0)
@@ -178,7 +200,8 @@
                 for g in range(GROUPS):
                     hit = marks[s, g * BR + k] == cube_keep[g, 0, w]
                     row = (s * KEPT + t) * Q
-                    put(right, w, row, g, held[s, g * HALF + k], hit, INNER + BS)
+                    block = held[s, pl.ds(pl.multiple_of(k * PAIR + g * Q, Q), Q), :]
+                    put(right, w, row, g, block, hit, INNER + BS)
 
 
 def cube_kernel(own, same, other, right, out):
@@ -196,6 +219,11 @@
         return 0
 
     lax.fori_loop(0, WIN, one, 0)
+
+
+def small_room(*arrays):
+    held = [pltpu.SMEM(a.shape, a.dtype) for a in arrays]
+    return (*held, pltpu.SemaphoreType.DMA((len(arrays),)))
 
 
 def shaped(*shape):
@@ -221,47 +249,53 @@
 
     spread, panel = call(
         prepare_kernel,
-        (shaped(COLS, WIN // 2 * BS + 16, BS), shaped(GROUPS * BR + 1, Q, BS)),
-        (own_cols, keep),
-        [p_vals],
+        (shaped(COLS, WIN // 2 * BS + 16, BS), shaped(TALL, BS)),
+        (),
+        [own_cols, keep, p_vals],
         [
             pltpu.VMEM((WIN, GROUPS, BS, BS), jnp.bfloat16),
             pltpu.VMEM((BR, GROUPS, Q, BS), jnp.bfloat16),
             pltpu.SemaphoreType.DMA((2,)),
+            *small_room(own_cols, keep),
         ],
-        [HBM],
+        [HBM] * 3,
         63,
     )
     lefts = lax.all_to_all(spread, "col", 0, 0)
     panels = lax.all_gather(panel.astype(jnp.float16), "row")
     panels = lax.optimization_barrier(panels)
     notes = lefts[:, WIN // 2 * BS : WIN // 2 * BS + 1, :].astype(jnp.int32)
-    marks = panels[:, BR, 0, :].astype(jnp.float32)
-    back = jnp.exp2(-marks[:, MARKS])[:, None, None, None]
+    marks = panels[:, BR * PAIR, :].astype(jnp.float32)
+    back = jnp.exp2(-marks[:, MARKS])[:, None, None]
     marks = marks.astype(jnp.int32)
     panels = (panels.astype(jnp.float32) * back).astype(jnp.bfloat16)
 
     partial = call(
         square_kernel,
         shaped(REPS, WIN, BS, BS),
-        (notes, marks, keep),
-        (lefts, panels),
+        (),
+        (notes, marks, keep, lefts, panels),
         [
             pltpu.VMEM((2, COLS * BS, SLOTS * BS), jnp.bfloat16),
-            pltpu.VMEM((WIN // 2, 2, ROWS, GROUPS, Q, BS), jnp.bfloat16),
+            pltpu.VMEM((WIN // 2, 2, ROWS, PAIR, BS), jnp.bfloat16),
             pltpu.SemaphoreType.DMA((WIN // 2,)),
+            *small_room(notes, marks, keep),
         ],
-        [VMEM, HBM],
+        [HBM] * 3 + [VMEM, HBM],
         ROOM,
         (WIN * 2 * BS * ROWS * Q * SLOTS * BS, panels.size * 2),
     )
     right = call(
         layout_kernel,
         shaped(WIN, INNER + BS + Q, GROUPS * BS),
-        (notes, marks, keep, cube_keep),
-        [panels],
-        [pltpu.VMEM(panels.shape, panels.dtype), pltpu.SemaphoreType.DMA((ROWS,))],
-        [HBM],
+        (),
+        [notes, marks, keep, cube_keep, panels],
+        [
+            pltpu.VMEM(panels.shape, panels.dtype),
+            pltpu.SemaphoreType.DMA((ROWS,)),
+            *small_room(notes, marks, keep, cube_keep),
+        ],
+        [HBM] * 5,
         ROOM,
         (0, 3 * panels.size * 2),
     )

time: 158 us -> 156 us (0.987)
  Pallas kernels: 15.2 us -> 13.5 us
    pallas_call x4, Pallas kernels: 15.2 us -> 13.5 us  [call(): pl.pallas_call(kernel, out_shape=out, in_specs=[SMEM] * len(scalars) + (s...]
  transfers between devices with their start and end apart: 2 -> 2, of which waited for: 0 -> 0; matrix products, arithmetic and copies ran while one was open for 3% -> 3% of each run, Pallas kernels for 3% -> 2%
where the time goes in v6:
time: 156 us; the launch traced here: 155 us
  blocking collectives  116 us (74%)
  starting transfers between devices  18.8 us (12%)
  Pallas kernels  13.5 us (9%)
  other arithmetic  6.18 us (4%)
    all_gather x1, blocking collectives, on_device(): panels = lax.all_gather(panel.astype(jnp.float16), 'row')  78 us
    all_to_all x2, blocking collectives, on_device(): parts = lax.all_to_all(partial, 'rep', 0, 0, tiled=True)  26.2 us
    pallas_call x4, Pallas kernels, call(): pl.pallas_call(kernel, out_shape=out, in_specs=[SMEM] * len(scalars) + (s...  13.5 us
    all_to_all x1, blocking collectives, on_device(): lax.all_to_all(jnp.broadcast_to(own[None], (CHIPS,) + own.shape), 'col',...  12.2 us
    all_to_all x1, starting transfers between devices, on_device(): lefts = lax.all_to_all(spread, 'col', 0, 0)  10.4 us
    ppermute x1, starting transfers between devices, on_device(): other = lax.ppermute(same, 'col', CORES)  8.48 us
    convert_element_type x1, other arithmetic, on_device(): panels = (panels.astype(jnp.float32) * back).astype(jnp.bfloat16)  3.95 us
  transfers between devices with their start and end apart: 2, of which 0 were waited for; matrix products, arithmetic and copies ran while one was open for 3% of the time, Pallas kernels for 2%

profile of v6, /device:TPU:1, one launch (start us, length us, event | category | flops | bytes accessed | tf_op | source)
XLA Modules:
  0.0 155.2 jit_solution(5745843051955392681)
XLA Ops:
  0.0 2.4 %shard_map.46 = (bf16[8,528,128]{2,1,0:T(8,128)(2,1)}, bf16[1552,128]{1,0:T(8,128)(2,1)}) custom-call(s32[2,24]{1,0:T(2,128)} %bitcast.16, s32[2,2,8]{2,1,0:T(2,128)} %bitcast.7, bf16[24,2,128,128]{3,2,1,0:T(8,128)(2,1)} %p_vals.1), custom_call_target="tpu_custom_call" | custom-call | tf_op jit(solution)/shard_map/pallas_call | solution.py:234
  2.4 10.4 %all-to-all-start = ((bf16[8,528,128]{2,1,0:T(8,128)(2,1)}), bf16[8,528,128]{2,1,0:T(8,128)(2,1)S(1)}, u32[]{:S(2)}, u32[]{:S(2)}) async-start(bf16[8,528,128]{2,1,0:T(8,128)(2,1)} %get-tuple-element.7), calls=%async_computation | async-start | bytes 2162688 | tf_op jit(solution)/shard_map/all_to_all | solution.py:264
  12.8 1.1 convert_element_type.26
  13.9 78.0 %all-gather.2 = f16[24832,128]{1,0:T(8,128)(2,1)S(1)} all-gather(f16[1552,128]{1,0:T(8,128)(2,1)S(1)} %convert_element_type.26), channel_id=2, replica_groups=mesh['row'=16,'col'=8,'rep'=4] {'row'}, dimensions={0}, use_global_device_ids=true | all-gather | bytes 6754304 | tf_op jit(solution)/shard_map/all_gather | solution.py:265
  91.9 0.2 fusion.2
  92.1 0.0 copy-start
  92.1 4.0 %multiply_convert_fusion.panels = bf16[16,1552,128]{2,1,0:T(8,128)(2,1)} fusion(f16[16,1552,128]{2,1,0:T(8,128)(2,1)S(1)} %bitcast.12, f32[16]{0:T(128)S(1)} %fusion.2), kind=kLoop, calls=%fused_computation | loop fusion | flops 9535488 | bytes 12714048 | tf_op jit(solution)/shard_map/convert_element_type | solution.py:271
  96.0 0.0 all-to-all-done.lefts
  96.0 0.0 copy-done
  96.0 0.0 copy-start.1
  96.0 4.9 %shard_map.47 = bf16[4,8,128,128]{3,2,1,0:T(8,128)(2,1)S(1)} custom-call(s32[8,1,128]{2,1,0:T(1,128)S(1)} %slice_convert_fusion.1.notes_in, s32[16,128]{1,0:T(8,128)S(1)} %convert_element_type.29.marks_in, s32[2,2,8]{2,1,0:T(2,128)S(1)} %bitcast.8, bf16[8,528,128]{2,1,0:T(8,128)(2,1)S(1)} %all-to-all-done.lefts, ...), custom_call_target="tpu_custom_call" | custom-call | flops 536870912 | bytes 6356992 | tf_op jit(solution)/shard_map/pallas_call | solution.py:234
  100.9 14.5 %all_to_all.20 = bf16[4,8,128,128]{3,2,1,0:T(8,128)(2,1)S(1)} all-to-all(bf16[4,8,128,128]{3,2,1,0:T(8,128)(2,1)S(1)} %shard_map.47), channel_id=1, replica_groups=mesh['row'=16,'col'=8,'rep'=4] {'rep'}, dimensions={0} | all-to-all | bytes 2097152 | tf_op jit(solution)/shard_map/all_to_all | solution.py:302
  115.4 0.2 reduce_sum.24.own
  115.6 0.2 broadcast_in_dim.4
  115.8 12.2 %all_to_all.21.same = bf16[4,8,128,128]{3,2,1,0:T(8,128)(2,1)S(1)} all-to-all(bf16[4,8,128,128]{3,2,1,0:T(8,128)(2,1)S(1)} %broadcast_in_dim.4), channel_id=1, replica_groups={{0,8,16,24},{4,12,20,28},{1,9,17,25},{5,13,21,29},{2,10,18,26},{6,14,22..., dimensions={0} | all-to-all | bytes 2097152 | tf_op jit(solution)/shard_map/all_to_all | solution.py:304
  128.0 8.5 %collective-permute-start = (bf16[4,8,128,128]{3,2,1,0:T(8,128)(2,1)S(1)}, bf16[4,8,128,128]{3,2,1,0:T(8,128)(2,1)S(1)}, u32[]{:S(2)}, u32[]{:S(2)}) collective-permute-start(bf16[4,8,128,128]{3,2,1,0:T(8,128)(2,1)S(1)} %all_to_all.21.same), channel_id=1, source_target_pairs={{0,4},{4,0},{8,12},{12,8},{16,20},{20,16},{24,28},{28,24},{1,5},{5... | collective-permute-start | bytes 3145736 | tf_op jit(solution)/shard_map/ppermute | solution.py:307
  136.5 0.0 copy-done.1
  136.5 3.7 %shard_map.48.right = bf16[8,1184,256]{2,1,0:T(8,128)(2,1)S(1)} custom-call(s32[8,1,128]{2,1,0:T(1,128)S(1)} %slice_convert_fusion.1.notes_in, s32[16,128]{1,0:T(8,128)S(1)} %convert_element_type.29.marks_in, s32[2,2,8]{2,1,0:T(2,128)S(1)} %bitcast.9, s32[2,1,8]{2,1,0:T(1,128)S(1)} %bitcast.10, bf16[16,1552,128]{2,1,0:T(8,128)(2,1)} %multiply_convert_fusion.panels), custom_call_target="tpu_custom_call" | custom-call | bytes 19070976 | tf_op jit(solution)/shard_map/pallas_call | solution.py:234
  140.2 0.0 collective-permute-done.other
  140.2 2.5 %shard_map.49 = bf16[8,2,128,128]{3,2,1,0:T(8,128)(2,1)S(1)} custom-call(bf16[8,128,128]{2,1,0:T(8,128)(2,1)S(1)} %reduce_sum.24.own, bf16[4,8,128,128]{3,2,1,0:T(8,128)(2,1)S(1)} %all_to_all.21.same, bf16[4,8,128,128]{3,2,1,0:T(8,128)(2,1)S(1)} %collective-permute-done.other, bf16[8,1184,256]{2,1,0:T(8,128)(2,1)S(1)} %shard_map.48.right), custom_call_target="tpu_custom_call" | custom-call | flops 603979776 | bytes 4849664 | tf_op jit(solution)/shard_map/pallas_call | solution.py:234
  142.7 11.7 %all_to_all.22 = bf16[8,2,128,128]{3,2,1,0:T(8,128)(2,1)S(1)} all-to-all(bf16[8,2,128,128]{3,2,1,0:T(8,128)(2,1)S(1)} %shard_map.49), channel_id=1, replica_groups=mesh['row'=16,'col'=8,'rep'=4] {'rep'}, dimensions={0} | all-to-all | bytes 1048576 | tf_op jit(solution)/shard_map/all_to_all | solution.py:315
  154.4 0.7 reduce_sum.25
  (3 shorter events, 0.0 us)
Async XLA Ops:
  2.4 93.6 %all-to-all-start = ((bf16[8,528,128]{2,1,0:T(8,128)(2,1)}), bf16[8,528,128]{2,1,0:T(8,128)(2,1)S(1)}, u32[]{:S(2)}, u32[]{:S(2)}) async-start(bf16[8,528,128]{2,1,0:T(8,128)(2,1)} %get-tuple-element.7), calls=%async_computation | async-start | bytes 2162688 | tf_op jit(solution)/shard_map/all_to_all | solution.py:264
  92.1 4.0 %copy-start = (s32[8,2,2]{0,2,1:T(2,128)S(1)}, s32[8,2,2]{0,2,1:T(2,128)}, u32[]{:S(2)}) copy-start(s32[8,2,2]{0,2,1:T(2,128)} %param.6) | copy-start | bytes 388
  96.0 40.4 %copy-start.1 = (s32[8,2,1]{0,2,1:T(1,128)S(1)}, s32[8,2,1]{0,2,1:T(1,128)}, u32[]{:S(2)}) copy-start(s32[8,2,1]{0,2,1:T(1,128)} %param.7) | copy-start | bytes 196
  128.0 12.2 %collective-permute-start = (bf16[4,8,128,128]{3,2,1,0:T(8,128)(2,1)S(1)}, bf16[4,8,128,128]{3,2,1,0:T(8,128)(2,1)S(1)}, u32[]{:S(2)}, u32[]{:S(2)}) collective-permute-start(bf16[4,8,128,128]{3,2,1,0:T(8,128)(2,1)S(1)} %all_to_all.21.same), channel_id=1, source_target_pairs={{0,4},{4,0},{8,12},{12,8},{16,20},{20,16},{24,28},{28,24},{1,5},{5... | collective-permute-start | bytes 3145736 | tf_op jit(solution)/shard_map/ppermute | solution.py:307

commit v7 on v6

--- a/solution.py
+++ b/solution.py
@@ -205,20 +205,17 @@
 
 
 def cube_kernel(own, same, other, right, out):
-    core = lax.rem(lax.axis_index("col"), 2)
-
-    def one(w, _):
-        total = jnp.dot(own[w], right[w, INNER : INNER + BS, :], preferred_element_type=jnp.float32)
+    first = lax.rem(lax.axis_index("col"), 2) == 0
+    for w in range(WIN):
+        tiles = []
         for y in range(CHIPS):
-            for lefts, c in ((same, 2 * y + core), (other, 2 * y + 1 - core)):
-                rows = pl.ds(pl.multiple_of(c * BS, BS), BS)
-                total += jnp.dot(lefts[y, w], right[w, rows, :], preferred_element_type=jnp.float32)
+            one, two = same[y, w], other[y, w]
+            tiles += [jnp.where(first, one, two), jnp.where(first, two, one)]
+        left = jnp.concatenate(tiles + [own[w]], axis=1)
+        total = jnp.dot(left, right[w, : INNER + BS, :], preferred_element_type=jnp.float32)
         total = -2.0 * total
         for g in range(GROUPS):
             out[w, g] = total[:, g * BS : (g + 1) * BS].astype(jnp.bfloat16)
-        return 0
-
-    lax.fori_loop(0, WIN, one, 0)
 
 
 def small_room(*arrays):

time: 156 us -> 154 us (0.987)
  Pallas kernels: 13.5 us -> 11.8 us
    pallas_call x4, Pallas kernels: 13.5 us -> 11.8 us  [call(): pl.pallas_call(kernel, out_shape=out, in_specs=[SMEM] * len(scalars) + (s...]
where the time goes in v7:
time: 154 us
  blocking collectives  116 us (75%)
  starting transfers between devices  18.8 us (12%)
  Pallas kernels  11.8 us (8%)
  other arithmetic  6.18 us (4%)
    all_gather x1, blocking collectives, on_device(): panels = lax.all_gather(panel.astype(jnp.float16), 'row')  78 us
    all_to_all x2, blocking collectives, on_device(): parts = lax.all_to_all(partial, 'rep', 0, 0, tiled=True)  26.2 us
    all_to_all x1, blocking collectives, on_device(): lax.all_to_all(jnp.broadcast_to(own[None], (CHIPS,) + own.shape), 'col',...  12.2 us
    pallas_call x4, Pallas kernels, call(): pl.pallas_call(kernel, out_shape=out, in_specs=[SMEM] * len(scalars) + (s...  11.8 us
    all_to_all x1, starting transfers between devices, on_device(): lefts = lax.all_to_all(spread, 'col', 0, 0)  10.4 us
    ppermute x1, starting transfers between devices, on_device(): other = lax.ppermute(same, 'col', CORES)  8.49 us
    convert_element_type x1, other arithmetic, on_device(): panels = (panels.astype(jnp.float32) * back).astype(jnp.bfloat16)  3.95 us
  transfers between devices with their start and end apart: 2, of which 0 were waited for; matrix products, arithmetic and copies ran while one was open for 3% of the time, Pallas kernels for 2%

profile of v7, /device:TPU:1, one launch (start us, length us, event | category | flops | bytes accessed | tf_op | source)
XLA Modules:
  0.0 153.6 jit_solution(7194129671531045465)
XLA Ops:
  0.0 2.4 %shard_map.46 = (bf16[8,528,128]{2,1,0:T(8,128)(2,1)}, bf16[1552,128]{1,0:T(8,128)(2,1)}) custom-call(s32[2,24]{1,0:T(2,128)} %bitcast.16, s32[2,2,8]{2,1,0:T(2,128)} %bitcast.7, bf16[24,2,128,128]{3,2,1,0:T(8,128)(2,1)} %p_vals.1), custom_call_target="tpu_custom_call" | custom-call | tf_op jit(solution)/shard_map/pallas_call | solution.py:231
  2.4 10.4 %all-to-all-start = ((bf16[8,528,128]{2,1,0:T(8,128)(2,1)}), bf16[8,528,128]{2,1,0:T(8,128)(2,1)S(1)}, u32[]{:S(2)}, u32[]{:S(2)}) async-start(bf16[8,528,128]{2,1,0:T(8,128)(2,1)} %get-tuple-element.7), calls=%async_computation | async-start | bytes 2162688 | tf_op jit(solution)/shard_map/all_to_all | solution.py:261
  12.8 1.1 convert_element_type.26
  13.9 78.0 %all-gather.2 = f16[24832,128]{1,0:T(8,128)(2,1)S(1)} all-gather(f16[1552,128]{1,0:T(8,128)(2,1)S(1)} %convert_element_type.26), channel_id=2, replica_groups=mesh['row'=16,'col'=8,'rep'=4] {'row'}, dimensions={0}, use_global_device_ids=true | all-gather | bytes 6754304 | tf_op jit(solution)/shard_map/all_gather | solution.py:262
  91.9 0.2 fusion.2
  92.1 0.0 copy-start
  92.1 4.0 %multiply_convert_fusion.panels = bf16[16,1552,128]{2,1,0:T(8,128)(2,1)} fusion(f16[16,1552,128]{2,1,0:T(8,128)(2,1)S(1)} %bitcast.12, f32[16]{0:T(128)S(1)} %fusion.2), kind=kLoop, calls=%fused_computation | loop fusion | flops 9535488 | bytes 12714048 | tf_op jit(solution)/shard_map/convert_element_type | solution.py:268
  96.0 0.0 all-to-all-done.lefts
  96.0 0.0 copy-done
  96.0 0.0 copy-start.1
  96.0 4.9 %shard_map.47 = bf16[4,8,128,128]{3,2,1,0:T(8,128)(2,1)S(1)} custom-call(s32[8,1,128]{2,1,0:T(1,128)S(1)} %slice_convert_fusion.1.notes_in, s32[16,128]{1,0:T(8,128)S(1)} %convert_element_type.29.marks_in, s32[2,2,8]{2,1,0:T(2,128)S(1)} %bitcast.8, bf16[8,528,128]{2,1,0:T(8,128)(2,1)S(1)} %all-to-all-done.lefts, ...), custom_call_target="tpu_custom_call" | custom-call | flops 536870912 | bytes 6356992 | tf_op jit(solution)/shard_map/pallas_call | solution.py:231
  100.9 14.5 %all_to_all.20 = bf16[4,8,128,128]{3,2,1,0:T(8,128)(2,1)S(1)} all-to-all(bf16[4,8,128,128]{3,2,1,0:T(8,128)(2,1)S(1)} %shard_map.47), channel_id=1, replica_groups=mesh['row'=16,'col'=8,'rep'=4] {'rep'}, dimensions={0} | all-to-all | bytes 2097152 | tf_op jit(solution)/shard_map/all_to_all | solution.py:299
  115.4 0.2 reduce_sum.24.own
  115.6 0.2 broadcast_in_dim.4
  115.8 12.2 %all_to_all.21.same = bf16[4,8,128,128]{3,2,1,0:T(8,128)(2,1)S(1)} all-to-all(bf16[4,8,128,128]{3,2,1,0:T(8,128)(2,1)S(1)} %broadcast_in_dim.4), channel_id=1, replica_groups={{0,8,16,24},{4,12,20,28},{1,9,17,25},{5,13,21,29},{2,10,18,26},{6,14,22..., dimensions={0} | all-to-all | bytes 2097152 | tf_op jit(solution)/shard_map/all_to_all | solution.py:301
  128.0 8.5 %collective-permute-start = (bf16[4,8,128,128]{3,2,1,0:T(8,128)(2,1)S(1)}, bf16[4,8,128,128]{3,2,1,0:T(8,128)(2,1)S(1)}, u32[]{:S(2)}, u32[]{:S(2)}) collective-permute-start(bf16[4,8,128,128]{3,2,1,0:T(8,128)(2,1)S(1)} %all_to_all.21.same), channel_id=1, source_target_pairs={{0,4},{4,0},{8,12},{12,8},{16,20},{20,16},{24,28},{28,24},{1,5},{5... | collective-permute-start | bytes 3145736 | tf_op jit(solution)/shard_map/ppermute | solution.py:304
  136.5 0.0 copy-done.1
  136.5 3.7 %shard_map.48.right = bf16[8,1184,256]{2,1,0:T(8,128)(2,1)S(1)} custom-call(s32[8,1,128]{2,1,0:T(1,128)S(1)} %slice_convert_fusion.1.notes_in, s32[16,128]{1,0:T(8,128)S(1)} %convert_element_type.29.marks_in, s32[2,2,8]{2,1,0:T(2,128)S(1)} %bitcast.9, s32[2,1,8]{2,1,0:T(1,128)S(1)} %bitcast.10, bf16[16,1552,128]{2,1,0:T(8,128)(2,1)} %multiply_convert_fusion.panels), custom_call_target="tpu_custom_call" | custom-call | bytes 19070976 | tf_op jit(solution)/shard_map/pallas_call | solution.py:231
  140.2 0.0 collective-permute-done.other
  140.2 0.9 shard_map.49
  141.1 11.7 %all_to_all.22 = bf16[8,2,128,128]{3,2,1,0:T(8,128)(2,1)S(1)} all-to-all(bf16[8,2,128,128]{3,2,1,0:T(8,128)(2,1)S(1)} %shard_map.49), channel_id=1, replica_groups=mesh['row'=16,'col'=8,'rep'=4] {'rep'}, dimensions={0} | all-to-all | bytes 1048576 | tf_op jit(solution)/shard_map/all_to_all | solution.py:312
  152.8 0.7 reduce_sum.25
  (3 shorter events, 0.0 us)
Async XLA Ops:
  2.4 93.6 %all-to-all-start = ((bf16[8,528,128]{2,1,0:T(8,128)(2,1)}), bf16[8,528,128]{2,1,0:T(8,128)(2,1)S(1)}, u32[]{:S(2)}, u32[]{:S(2)}) async-start(bf16[8,528,128]{2,1,0:T(8,128)(2,1)} %get-tuple-element.7), calls=%async_computation | async-start | bytes 2162688 | tf_op jit(solution)/shard_map/all_to_all | solution.py:261
  92.1 4.0 %copy-start = (s32[8,2,2]{0,2,1:T(2,128)S(1)}, s32[8,2,2]{0,2,1:T(2,128)}, u32[]{:S(2)}) copy-start(s32[8,2,2]{0,2,1:T(2,128)} %param.6) | copy-start | bytes 388
  96.0 40.5 %copy-start.1 = (s32[8,2,1]{0,2,1:T(1,128)S(1)}, s32[8,2,1]{0,2,1:T(1,128)}, u32[]{:S(2)}) copy-start(s32[8,2,1]{0,2,1:T(1,128)} %param.7) | copy-start | bytes 196
  128.0 12.2 %collective-permute-start = (bf16[4,8,128,128]{3,2,1,0:T(8,128)(2,1)S(1)}, bf16[4,8,128,128]{3,2,1,0:T(8,128)(2,1)S(1)}, u32[]{:S(2)}, u32[]{:S(2)}) collective-permute-start(bf16[4,8,128,128]{3,2,1,0:T(8,128)(2,1)S(1)} %all_to_all.21.same), channel_id=1, source_target_pairs={{0,4},{4,0},{8,12},{12,8},{16,20},{20,16},{24,28},{28,24},{1,5},{5... | collective-permute-start | bytes 3145736 | tf_op jit(solution)/shard_map/ppermute | solution.py:304

commit v8 on v7

--- a/solution.py
+++ b/solution.py
@@ -153,14 +153,14 @@
                             col == keep[g, m, w], block, jnp.zeros_like(block)
                         )
             full = jnp.dot(left, right[half], preferred_element_type=jnp.float32)
-            p4 = [full[:, i * BS : (i + 1) * BS] for i in range(SLOTS)]
+            p4 = [full[:, i * BS : (i + 1) * BS].astype(jnp.bfloat16) for i in range(SLOTS)]
             u = [jnp.where(group < 2, p4[i], pltpu.roll(p4[i + 2], BS // 2, 1)) for i in range(2)]
             u += [jnp.where(group < 2, pltpu.roll(p4[i], BS // 2, 1), p4[i + 2]) for i in range(2)]
             for i in (0, 2):
                 one = jnp.where(group % 2 == 0, u[i], pltpu.roll(u[i + 1], Q, 1))
                 two = jnp.where(group % 2 == 0, pltpu.roll(u[i], BS - Q, 1), u[i + 1])
-                out[i, w] = one.astype(jnp.bfloat16)
-                out[i + 1, w] = two.astype(jnp.bfloat16)
+                out[i, w] = one
+                out[i + 1, w] = two
         return 0
 
     for p in range(WIN // 2):

time: 154 us -> 154 us (level)
  no operation moved by 1% of the time
where the time goes in v8:
time: 154 us; the launch traced here: 153 us
  blocking collectives  116 us (75%)
  starting transfers between devices  18.8 us (12%)
  Pallas kernels  11.8 us (8%)
  other arithmetic  6.18 us (4%)
    all_gather x1, blocking collectives, on_device(): panels = lax.all_gather(panel.astype(jnp.float16), 'row')  78 us
    all_to_all x2, blocking collectives, on_device(): parts = lax.all_to_all(partial, 'rep', 0, 0, tiled=True)  26.2 us
    all_to_all x1, blocking collectives, on_device(): lax.all_to_all(jnp.broadcast_to(own[None], (CHIPS,) + own.shape), 'col',...  12.2 us
    pallas_call x4, Pallas kernels, call(): pl.pallas_call(kernel, out_shape=out, in_specs=[SMEM] * len(scalars) + (s...  11.8 us
    all_to_all x1, starting transfers between devices, on_device(): lefts = lax.all_to_all(spread, 'col', 0, 0)  10.4 us
    ppermute x1, starting transfers between devices, on_device(): other = lax.ppermute(same, 'col', CORES)  8.49 us
    convert_element_type x1, other arithmetic, on_device(): panels = (panels.astype(jnp.float32) * back).astype(jnp.bfloat16)  3.95 us
  transfers between devices with their start and end apart: 2, of which 0 were waited for; matrix products, arithmetic and copies ran while one was open for 3% of the time, Pallas kernels for 2%

profile of v8, /device:TPU:1, one launch (start us, length us, event | category | flops | bytes accessed | tf_op | source)
XLA Modules:
  0.0 153.5 jit_solution(10102464753944813121)
XLA Ops:
  0.0 2.4 %shard_map.46 = (bf16[8,528,128]{2,1,0:T(8,128)(2,1)}, bf16[1552,128]{1,0:T(8,128)(2,1)}) custom-call(s32[2,24]{1,0:T(2,128)} %bitcast.16, s32[2,2,8]{2,1,0:T(2,128)} %bitcast.7, bf16[24,2,128,128]{3,2,1,0:T(8,128)(2,1)} %p_vals.1), custom_call_target="tpu_custom_call" | custom-call | tf_op jit(solution)/shard_map/pallas_call | solution.py:231
  2.4 10.4 %all-to-all-start = ((bf16[8,528,128]{2,1,0:T(8,128)(2,1)}), bf16[8,528,128]{2,1,0:T(8,128)(2,1)S(1)}, u32[]{:S(2)}, u32[]{:S(2)}) async-start(bf16[8,528,128]{2,1,0:T(8,128)(2,1)} %get-tuple-element.7), calls=%async_computation | async-start | bytes 2162688 | tf_op jit(solution)/shard_map/all_to_all | solution.py:261
  12.8 1.1 convert_element_type.26
  13.9 78.0 %all-gather.2 = f16[24832,128]{1,0:T(8,128)(2,1)S(1)} all-gather(f16[1552,128]{1,0:T(8,128)(2,1)S(1)} %convert_element_type.26), channel_id=2, replica_groups=mesh['row'=16,'col'=8,'rep'=4] {'row'}, dimensions={0}, use_global_device_ids=true | all-gather | bytes 6754304 | tf_op jit(solution)/shard_map/all_gather | solution.py:262
  91.9 0.2 fusion.2
  92.1 0.0 copy-start
  92.1 4.0 %multiply_convert_fusion.panels = bf16[16,1552,128]{2,1,0:T(8,128)(2,1)} fusion(f16[16,1552,128]{2,1,0:T(8,128)(2,1)S(1)} %bitcast.12, f32[16]{0:T(128)S(1)} %fusion.2), kind=kLoop, calls=%fused_computation | loop fusion | flops 9535488 | bytes 12714048 | tf_op jit(solution)/shard_map/convert_element_type | solution.py:268
  96.0 0.0 all-to-all-done.lefts
  96.0 0.0 copy-done
  96.0 0.0 copy-start.1
  96.0 4.8 %shard_map.47 = bf16[4,8,128,128]{3,2,1,0:T(8,128)(2,1)S(1)} custom-call(s32[8,1,128]{2,1,0:T(1,128)S(1)} %slice_convert_fusion.1.notes_in, s32[16,128]{1,0:T(8,128)S(1)} %convert_element_type.29.marks_in, s32[2,2,8]{2,1,0:T(2,128)S(1)} %bitcast.8, bf16[8,528,128]{2,1,0:T(8,128)(2,1)S(1)} %all-to-all-done.lefts, ...), custom_call_target="tpu_custom_call" | custom-call | flops 536870912 | bytes 6356992 | tf_op jit(solution)/shard_map/pallas_call | solution.py:231
  100.9 14.4 %all_to_all.20 = bf16[4,8,128,128]{3,2,1,0:T(8,128)(2,1)S(1)} all-to-all(bf16[4,8,128,128]{3,2,1,0:T(8,128)(2,1)S(1)} %shard_map.47), channel_id=1, replica_groups=mesh['row'=16,'col'=8,'rep'=4] {'rep'}, dimensions={0} | all-to-all | bytes 2097152 | tf_op jit(solution)/shard_map/all_to_all | solution.py:299
  115.3 0.2 reduce_sum.24.own
  115.5 0.2 broadcast_in_dim.4
  115.7 12.2 %all_to_all.21.same = bf16[4,8,128,128]{3,2,1,0:T(8,128)(2,1)S(1)} all-to-all(bf16[4,8,128,128]{3,2,1,0:T(8,128)(2,1)S(1)} %broadcast_in_dim.4), channel_id=1, replica_groups={{0,8,16,24},{4,12,20,28},{1,9,17,25},{5,13,21,29},{2,10,18,26},{6,14,22..., dimensions={0} | all-to-all | bytes 2097152 | tf_op jit(solution)/shard_map/all_to_all | solution.py:301
  127.9 8.5 %collective-permute-start = (bf16[4,8,128,128]{3,2,1,0:T(8,128)(2,1)S(1)}, bf16[4,8,128,128]{3,2,1,0:T(8,128)(2,1)S(1)}, u32[]{:S(2)}, u32[]{:S(2)}) collective-permute-start(bf16[4,8,128,128]{3,2,1,0:T(8,128)(2,1)S(1)} %all_to_all.21.same), channel_id=1, source_target_pairs={{0,4},{4,0},{8,12},{12,8},{16,20},{20,16},{24,28},{28,24},{1,5},{5... | collective-permute-start | bytes 3145736 | tf_op jit(solution)/shard_map/ppermute | solution.py:304
  136.4 0.0 copy-done.1
  136.4 3.7 %shard_map.48.right = bf16[8,1184,256]{2,1,0:T(8,128)(2,1)S(1)} custom-call(s32[8,1,128]{2,1,0:T(1,128)S(1)} %slice_convert_fusion.1.notes_in, s32[16,128]{1,0:T(8,128)S(1)} %convert_element_type.29.marks_in, s32[2,2,8]{2,1,0:T(2,128)S(1)} %bitcast.9, s32[2,1,8]{2,1,0:T(1,128)S(1)} %bitcast.10, bf16[16,1552,128]{2,1,0:T(8,128)(2,1)} %multiply_convert_fusion.panels), custom_call_target="tpu_custom_call" | custom-call | bytes 19070976 | tf_op jit(solution)/shard_map/pallas_call | solution.py:231
  140.1 0.0 collective-permute-done.other
  140.1 0.9 shard_map.49
  141.0 11.7 %all_to_all.22 = bf16[8,2,128,128]{3,2,1,0:T(8,128)(2,1)S(1)} all-to-all(bf16[8,2,128,128]{3,2,1,0:T(8,128)(2,1)S(1)} %shard_map.49), channel_id=1, replica_groups=mesh['row'=16,'col'=8,'rep'=4] {'rep'}, dimensions={0} | all-to-all | bytes 1048576 | tf_op jit(solution)/shard_map/all_to_all | solution.py:312
  152.7 0.7 reduce_sum.25
  (3 shorter events, 0.0 us)
Async XLA Ops:
  2.4 93.6 %all-to-all-start = ((bf16[8,528,128]{2,1,0:T(8,128)(2,1)}), bf16[8,528,128]{2,1,0:T(8,128)(2,1)S(1)}, u32[]{:S(2)}, u32[]{:S(2)}) async-start(bf16[8,528,128]{2,1,0:T(8,128)(2,1)} %get-tuple-element.7), calls=%async_computation | async-start | bytes 2162688 | tf_op jit(solution)/shard_map/all_to_all | solution.py:261
  92.1 4.0 %copy-start = (s32[8,2,2]{0,2,1:T(2,128)S(1)}, s32[8,2,2]{0,2,1:T(2,128)}, u32[]{:S(2)}) copy-start(s32[8,2,2]{0,2,1:T(2,128)} %param.6) | copy-start | bytes 388
  96.0 40.4 %copy-start.1 = (s32[8,2,1]{0,2,1:T(1,128)S(1)}, s32[8,2,1]{0,2,1:T(1,128)}, u32[]{:S(2)}) copy-start(s32[8,2,1]{0,2,1:T(1,128)} %param.7) | copy-start | bytes 196
  127.9 12.2 %collective-permute-start = (bf16[4,8,128,128]{3,2,1,0:T(8,128)(2,1)S(1)}, bf16[4,8,128,128]{3,2,1,0:T(8,128)(2,1)S(1)}, u32[]{:S(2)}, u32[]{:S(2)}) collective-permute-start(bf16[4,8,128,128]{3,2,1,0:T(8,128)(2,1)S(1)} %all_to_all.21.same), channel_id=1, source_target_pairs={{0,4},{4,0},{8,12},{12,8},{16,20},{20,16},{24,28},{28,24},{1,5},{5... | collective-permute-start | bytes 3145736 | tf_op jit(solution)/shard_map/ppermute | solution.py:304
